TPU v7x, 512 devices: a whole 4x8x8 slice. The times are simulated.
512 devices in a mesh: dp: 128 (over z, y_lo, x, core), tensor: 4 (over y_hi).
Axes of the slice: x: 4, y: 8 (y_hi: 4, y_lo: 2; y = y_hi * 2 + y_lo), z: 8, core: 2. Of those that a mesh axis runs over, the one named last changes fastest.
Arguments:
- activations: bfloat16 [65536, 4096], P('dp', 'tensor'), may hold values from -512 to 512
- token_mask: int32 [65536], P('dp'), may hold values 0 or 1
- gradient: bfloat16 [16384, 4096], P(('dp', 'tensor')), may hold values from -6 to 6
Outputs:
- preconditioned: bfloat16 [16384, 4096], P(('dp', 'tensor'))
All inputs are finite; a program needn't handle non-finite values. Where the computation divides by a largest or mean magnitude, that divisor is 1e-20 or more. No bound on the sum of `token_mask` on one device may be relied on, other than what follows from the above.
Results may differ from a plain program's by a relative error of at most 0.0049.
Values may be sent and summed in bfloat16 or wider, within the bound.
No kernel may reach another device: no remote copies, remote signals or barrier semaphores. Data moves between devices by JAX's collectives and lax.ppermute only.
A program may use at most 64 MiB of HBM per device.

v0:
```python
import jax
import jax.numpy as jnp
from jax import lax
from jax.sharding import PartitionSpec as P

B = 512
BPT = 2
NS_ITERS = 3


DAMPING = 0.05


def inverse_root(gram_block, token_total):
    identity = jnp.eye(gram_block.shape[0], dtype=jnp.float32)
    damped = gram_block / token_total + DAMPING * identity
    scale_norm = jnp.max(jnp.sum(jnp.abs(damped), axis=1))
    iterate = damped / scale_norm
    inverse = identity
    for sweep_index in range(NS_ITERS):
        middle = 1.5 * identity - 0.5 * jnp.dot(inverse, iterate, precision=lax.Precision.HIGHEST)
        if sweep_index + 1 < NS_ITERS:
            iterate = jnp.dot(iterate, middle, precision=lax.Precision.HIGHEST)
        inverse = jnp.dot(middle, inverse, precision=lax.Precision.HIGHEST)
    return (inverse / jnp.sqrt(scale_norm)).astype(jnp.bfloat16)


def apply_blocks(columns, own_roots):
    row_count = columns.shape[0]
    piece_count = own_roots.shape[0]
    split_cols = columns.reshape(row_count, piece_count, B)
    product = jnp.einsum("qkb,kbc->qkc", split_cols, own_roots, preferred_element_type=jnp.float32)
    return product.reshape(row_count, piece_count * B).astype(jnp.bfloat16)


def local(activations, token_mask, gradient):
    token_total = activations.shape[0] * lax.axis_size("dp")
    masked = activations * token_mask.astype(activations.dtype)[:, None]
    partials = []
    for block_index in range(BPT):
        block_cols = masked[:, block_index * B : (block_index + 1) * B]
        partials.append(
            lax.dot_general(
                block_cols, block_cols, (((0,), (0,)), ((), ())), preferred_element_type=jnp.float32
            )
        )
    stacked = jnp.stack(partials)
    gram_sums = lax.psum(stacked, "dp")
    own_roots = jnp.stack(
        [inverse_root(gram_sums[block_index], token_total) for block_index in range(BPT)]
    )
    return apply_blocks(gradient, lax.all_gather(own_roots, "tensor", axis=0, tiled=True))


def solution(mesh):
    placed = (P("dp", "tensor"), P("dp"), P(("dp", "tensor"), None))
    return jax.shard_map(
        local, mesh=mesh, in_specs=placed, out_specs=P(("dp", "tensor"), None), check_vma=False
    )
```

profile of v0, /device:TPU:1, one launch (start us, length us, event | category | flops | bytes accessed | tf_op | source)
XLA Modules:
  0.0 1244.9 jit_solution(822042567953686945)
XLA Ops:
  7.2 1.4 broadcast_multiply_fusion
  9.5 1.5 pad_maximum_fusion
  11.1 1098.8 %all-reduce.2.cloned.1.call-done = f32[2,512,512]{2,1,0:T(8,128)} async-done(((f32[2,512,512]{2,1,0:T(8,128)}), f32[2,512,512]{2,1,0:T(8,128)}) %all-reduce.2.cloned.1.call-update) | async-done | bytes 2097168 | tf_op jit(solution)/shard_map/psum | solution.py:48
  1109.8 2.0 abs_reduce_fusion.1
  1113.1 1.8 select_subtract_fusion.5
  1115.0 1.0 fusion.8
  1115.9 2.6 fusion.18
  1118.5 1.8 select_subtract_fusion.4
  1120.4 1.8 fusion.33
  1122.2 1.8 fusion.34
  1125.4 3.0 select_subtract_fusion.2
  1128.4 1.0 fusion.7
  1130.0 2.8 fusion.15
  1132.8 1.9 select_subtract_fusion.1
  1134.6 1.8 fusion.35
  1136.5 1.8 fusion.36
  1138.3 1.9 select_subtract_fusion.3
  1140.2 1.9 fusion.3
  1142.0 1.8 select_subtract_fusion
  1143.9 1.9 fusion.2
  1145.8 1.1 pad_maximum_fusion.1
  1146.9 87.6 %all-gather.2.cloned.1.call-done = bf16[8,512,512]{2,1,0:T(8,128)(2,1)} async-done(((bf16[2,512,512]{2,1,0:T(8,128)(2,1)}), bf16[8,512,512]{2,1,0:T(8,128)(2,1)}) %all-gather.2.cloned.1.call-update) | async-done | bytes 4194320 | tf_op jit(solution)/shard_map/all_gather | solution.py:52
  1234.4 2.9 fusion.4
  1237.4 0.7 copy.10
  (15 shorter events, 3.5 us)
Async XLA Ops:
  6.5 1103.3 %all-reduce.2.cloned.1.call-start = ((), (), s32[]{:S(2)}) async-start(), calls=%async_computation | async-start | bytes 4194304 | tf_op jit(solution)/shard_map/psum | solution.py:48
  11.0 1223.4 %all-gather.2.cloned.1.call-start = ((), (), s32[]{:S(2)}) async-start(), calls=%async_computation.1 | async-start | bytes 5242880 | tf_op jit(solution)/shard_map/all_gather | solution.py:52
  1109.8 3.3 copy-start
  1128.4 1.6 copy-start.1
  1145.8 88.7 %copy-start.2 = (bf16[32,4096]{1,0:T(8,128)(2,1)S(1)}, bf16[32,4096]{1,0:T(8,128)(2,1)}, u32[]{:S(2)}) copy-start(bf16[32,4096]{1,0:T(8,128)(2,1)} %param.5) | copy-start | bytes 786436
Sparse Core Ops, SparseCore 0:
  11.1 1098.6 all-reduce.1
  1147.0 87.4 all-gather.1
where the time goes:
time: 1250 us; the launch traced here: 1240 us
  waiting for transfers between devices  1190 us (95%)
  matrix products  34.4 us (3%)
  between operations  15 us (1%)
    psum x1, waiting for transfers between devices, local(): gram_sums = lax.psum(stacked, 'dp')  1100 us
    all_gather x1, waiting for transfers between devices, local(): lax.all_gather(own_roots, 'tensor', axis=0, tiled=True)  87.6 us
  transfers between devices with their start and end apart: 2, of which 2 were waited for; matrix products, arithmetic and copies ran while one was open for 0% of the time, Pallas kernels for 0%

commit v1 on v0

v1 whole, which is shorter than its diff:
```python
import jax
import jax.numpy as jnp
from jax import lax
from jax.experimental import pallas as pl
from jax.experimental.pallas import tpu as pltpu
from jax.sharding import Mesh, PartitionSpec as P

B = 512
H = 256
LANES = 128
DAMPING = 0.05
BF = jnp.bfloat16
F32 = jnp.float32
AXES = (("z", 4), ("yl", 2), ("x", 8), ("core", 2), ("yh", 4))
SHARDS = 8
PACKED = 3 * 2 * H // SHARDS
VMEM = pl.BlockSpec(memory_space=pltpu.VMEM)


def call(kernel, out, *operands):
    return pl.pallas_call(
        kernel,
        out_shape=jax.ShapeDtypeStruct(*out),
        in_specs=[VMEM] * len(operands),
        out_specs=VMEM,
        compiler_params=pltpu.CompilerParams(vmem_limit_bytes=40 * 1024 * 1024),
    )(*operands)


def tdot(left, right):
    return lax.dot_general(left, right, (((0,), (0,)), ((), ())), preferred_element_type=F32)


def gram_kernel(own_ref, other_ref, out_ref):
    lows, highs = [], []
    for ref in (own_ref, other_ref):
        lows.append(ref[:, :H])
        highs.append(ref[:, H:])
    for slot, (left, right) in enumerate(((lows, lows), (highs, lows), (highs, highs))):
        block = tdot(left[0], right[0]) + tdot(left[1], right[1])
        for half in range(2):
            out_ref[2 * slot + half] = block[:, half * LANES : (half + 1) * LANES].astype(BF)


def sum_kernel(parts_ref, out_ref):
    total = parts_ref[0].astype(F32)
    for part in range(1, SHARDS):
        total += parts_ref[part].astype(F32)
    rounded = total.astype(BF)
    for copy in range(SHARDS):
        out_ref[copy] = rounded


def split(array):
    high = array.astype(BF)
    return high, (array - high.astype(F32)).astype(BF)


def dot3(left, right):
    one = lambda a, b: jnp.dot(a, b, preferred_element_type=F32)
    return one(left[0], right[0]) + (one(left[0], right[1]) + one(left[1], right[0]))


def root_kernel(gram_ref, rows_ref, out_ref):
    packed = [gram_ref[piece].astype(F32) for piece in range(6)]
    first, cross, last = [jnp.concatenate(packed[2 * k : 2 * k + 2], axis=1) for k in range(3)]
    gram = jnp.concatenate(
        [jnp.concatenate([first, cross.T], axis=1), jnp.concatenate([cross, last], axis=1)], axis=0
    )
    row = lax.broadcasted_iota(jnp.int32, (B, B), 0)
    column = lax.broadcasted_iota(jnp.int32, (B, B), 1)
    identity = jnp.where(row == column, 1.0, 0.0).astype(F32)
    damped = gram * (1.0 / 65536) + DAMPING * identity
    norm = jnp.max(jnp.sum(jnp.abs(damped), axis=1, keepdims=True), axis=0, keepdims=True)
    y = damped / norm
    ys = split(y)
    square = dot3(ys, ys)
    squares = split(square)
    z = 2.25 * identity - 2.4375 * y + 1.6875 * square + dot3(squares, split(0.0625 * square - 0.5625 * y))
    zs = split(z)
    root = 1.5 * z - 0.5 * dot3(split(dot3(zs, zs)), split(dot3(ys, zs)))
    root = (root / jnp.sqrt(norm)).astype(BF)
    out_ref[...] = jnp.dot(rows_ref[...], root, preferred_element_type=F32).astype(BF)


def local(activations, token_mask, gradient):
    core = lax.axis_index("core")
    mask = token_mask.astype(BF)[:, None]

    def columns(index):
        return lax.dynamic_slice(activations, (0, index * B), (activations.shape[0], B)) * mask

    other = lax.ppermute(columns(1 - core), "core", [(0, 1), (1, 0)])
    rows = gradient.shape[0]
    blocks = gradient.reshape(rows, SHARDS, B).transpose(1, 0, 2)
    blocks = lax.all_to_all(blocks, ("yh", "core"), 0, 0).reshape(SHARDS * rows, B)
    packed = call(gram_kernel, ((6, H, LANES), BF), columns(core), other).reshape(SHARDS, PACKED, LANES)
    for axes in (("x",), ("z", "yl")):
        packed = call(sum_kernel, (packed.shape, BF), lax.all_to_all(packed, axes, 0, 0))
    packed = lax.all_to_all(packed, "x", 0, 0).reshape(6, H, LANES)
    product = call(root_kernel, ((SHARDS * rows, B), BF), packed, blocks)
    product = lax.all_to_all(product.reshape(SHARDS, rows, B), ("yh", "core"), 0, 0)
    return product.transpose(1, 0, 2).reshape(rows, SHARDS * B)


def solution(mesh):
    names, sizes = zip(*AXES)
    cut = Mesh(mesh.devices.reshape(sizes), names)
    dp = names[:4]
    placed = (P(dp, "yh"), P(dp), P(names, None))
    return jax.shard_map(local, mesh=cut, in_specs=placed, out_specs=P(names, None), check_vma=False)
```

time: 1250 us -> 96.1 us (0.08)
  waiting for transfers between devices: 1190 us -> 23.6 us
  blocking collectives: 0 us -> 36.3 us
  matrix products: 34.4 us -> 0 us
  starting transfers between devices: 0.04 us -> 25.5 us
  between operations: 15 us -> 0.05 us
    psum x1 -> x0, waiting for transfers between devices: 1100 us -> none  [local(): gram_sums = lax.psum(stacked, 'dp')]
    all_gather x1 -> x0, waiting for transfers between devices: 87.6 us -> none  [local(): lax.all_gather(own_roots, 'tensor', axis=0, tiled=True)]
    all_to_all x0 -> x3, blocking collectives: none -> 36.3 us  [the longest x1 15.1 us: local(): lax.all_to_all(product.reshape(SHARDS, rows, B), ('yh', 'core'), 0, 0)]
    dot_general x19 -> x0, matrix products: 34.4 us -> none  [the longest x6 12.2 us: inverse_root(): jnp.dot(inverse, iterate, precision=lax.Precision.HIGHEST)]
    all_to_all x0 -> x2, waiting for transfers between devices: none -> 22.1 us  [the longest x1 11.4 us: local(): lax.all_to_all(packed, axes, 0, 0)]
    all_to_all x0 -> x2, starting transfers between devices: none -> 16.7 us  [the longest x1 9.67 us: local(): lax.all_to_all(blocks, ('yh', 'core'), 0, 0).reshape(SHARDS * rows, B)]
  transfers between devices with their start and end apart: 2 -> 3, of which waited for: 2 -> 3; matrix products, arithmetic and copies ran while one was open for 0% -> 1% of each run, Pallas kernels for 0% -> 0%
where the time goes in v1:
time: 96.1 us; the launch traced here: 95.6 us
  blocking collectives  36.3 us (38%)
  starting transfers between devices  25.5 us (27%)
  waiting for transfers between devices  23.6 us (25%)
  Pallas kernels  6.59 us (7%)
  local copies, waits for them, and re-layouts  2.13 us (2%)
  other arithmetic  1.44 us (1%)
    all_to_all x1, blocking collectives, local(): lax.all_to_all(product.reshape(SHARDS, rows, B), ('yh', 'core'), 0, 0)  15.1 us
    all_to_all x1, waiting for transfers between devices, local(): lax.all_to_all(packed, axes, 0, 0)  11.4 us
    all_to_all x1, blocking collectives, local(): packed = lax.all_to_all(packed, 'x', 0, 0).reshape(6, H, LANES)  10.8 us
    all_to_all x1, waiting for transfers between devices, local(): lax.all_to_all(blocks, ('yh', 'core'), 0, 0).reshape(SHARDS * rows, B)  10.6 us
    all_to_all x1, blocking collectives, local(): lax.all_to_all(packed, axes, 0, 0)  10.3 us
    all_to_all x1, starting transfers between devices, local(): lax.all_to_all(blocks, ('yh', 'core'), 0, 0).reshape(SHARDS * rows, B)  9.67 us
    ppermute x1, starting transfers between devices, local(): other = lax.ppermute(columns(1 - core), 'core', [(0, 1), (1, 0)])  8.79 us
    all_to_all x1, starting transfers between devices, local(): lax.all_to_all(packed, axes, 0, 0)  7.05 us
  transfers between devices with their start and end apart: 3, of which 3 were waited for; matrix products, arithmetic and copies ran while one was open for 1% of the time, Pallas kernels for 0%

profile of v1, /device:TPU:1, one launch (start us, length us, event | category | flops | bytes accessed | tf_op | source)
XLA Modules:
  0.0 95.6 jit_solution(2013053227543928534)
XLA Ops:
  0.0 0.0 copy-start.1
  0.0 0.7 copy-done.1
  0.7 1.4 %dynamic-slice_multiply_fusion = (bf16[512,512]{1,0:T(8,128)(2,1)S(1)}, bf16[512,512]{1,0:T(8,128)(2,1)S(1)}) fusion(bf16[512,1024]{1,0:T(8,128)(2,1)} %param.3, s32[]{:T(128)S(6)} %select_n.7, bf16[512]{0:T(512)(128)(2,1)S(1)} %convert_element_type.3, s32[]{:T(128)S(6)} %select_n.6), kind=kLoop, calls=%fused_computation | loop fusion | flops 1835008 | bytes 2098184 | tf_op jit(solution)/shard_map/mul | solution.py:91
  2.1 8.8 %collective-permute-start = (bf16[512,512]{1,0:T(8,128)(2,1)S(1)}, bf16[512,512]{1,0:T(8,128)(2,1)S(1)}, u32[]{:S(2)}, u32[]{:S(2)}) collective-permute-start(bf16[512,512]{1,0:T(8,128)(2,1)S(1)} %get-tuple-element.5), channel_id=1, source_target_pairs={{0,4},{4,0},{1,5},{5,1},{2,6},{6,2},{3,7},{7,3},{8,12},{12,8},{9,1... | collective-permute-start | bytes 1572872 | tf_op jit(solution)/shard_map/ppermute | solution.py:93
  10.9 1.5 %collective-permute-done.other_ref = bf16[512,512]{1,0:T(8,128)(2,1)S(1)} collective-permute-done((bf16[512,512]{1,0:T(8,128)(2,1)S(1)}, bf16[512,512]{1,0:T(8,128)(2,1)S(1)}, u32[]{:S(2)}, u32[]{:S(2)}) %collective-permute-start) | collective-permute-done | bytes 524320 | tf_op jit(solution)/shard_map/ppermute | solution.py:93
  12.4 0.6 shard_map.37
  13.1 10.3 %all_to_all.25.parts_ref = bf16[8,192,128]{2,1,0:T(8,128)(2,1)S(1)} all-to-all(bf16[8,192,128]{2,1,0:T(8,128)(2,1)S(1)} %bitcast.15), channel_id=1, replica_groups=mesh['z'=4,'yl'=2,'x'=8,'core'=2,'yh'=4] {'x'}, dimensions={0} | all-to-all | bytes 786432 | tf_op jit(solution)/shard_map/all_to_all | solution.py:99
  23.4 0.8 shard_map.38
  24.2 0.0 copy-start
  24.2 7.0 %all-to-all-start.1 = ((bf16[8,192,128]{2,1,0:T(8,128)(2,1)}), bf16[8,192,128]{2,1,0:T(8,128)(2,1)S(1)}, u32[]{:S(2)}, u32[]{:S(2)}) async-start(bf16[8,192,128]{2,1,0:T(8,128)(2,1)} %shard_map.38), calls=%async_computation.1 | async-start | bytes 786432 | tf_op jit(solution)/shard_map/all_to_all | solution.py:99
  31.2 0.0 copy-done
  31.3 0.7 copy.9
  32.0 11.4 %all-to-all-done.1.parts_ref = bf16[8,192,128]{2,1,0:T(8,128)(2,1)S(1)} async-done(((bf16[8,192,128]{2,1,0:T(8,128)(2,1)}), bf16[8,192,128]{2,1,0:T(8,128)(2,1)S(1)}, u32[]{:S(2)}, u32[]{:S(2)}) %all-to-all-start.1) | async-done | bytes 393248 | tf_op jit(solution)/shard_map/all_to_all | solution.py:99
  43.4 9.7 %all-to-all-start.3 = ((bf16[8,32,512]{2,1,0:T(8,128)(2,1)}), bf16[8,32,512]{2,1,0:T(8,128)(2,1)S(1)}, u32[]{:S(2)}, u32[]{:S(2)}) async-start(bf16[8,32,512]{2,1,0:T(8,128)(2,1)} %bitcast.13), calls=%async_computation.3 | async-start | bytes 524288 | tf_op jit(solution)/shard_map/all_to_all | solution.py:96
  53.1 0.1 shard_map.39
  53.1 10.6 %all-to-all-done.3 = bf16[8,32,512]{2,1,0:T(8,128)(2,1)S(1)} async-done(((bf16[8,32,512]{2,1,0:T(8,128)(2,1)}), bf16[8,32,512]{2,1,0:T(8,128)(2,1)S(1)}, u32[]{:S(2)}, u32[]{:S(2)}) %all-to-all-start.3) | async-done | bytes 262176 | tf_op jit(solution)/shard_map/all_to_all | solution.py:96
  63.8 10.8 %all_to_all.26 = bf16[8,192,128]{2,1,0:T(8,128)(2,1)S(1)} all-to-all(bf16[8,192,128]{2,1,0:T(8,128)(2,1)S(1)} %shard_map.39), channel_id=1, replica_groups=mesh['z'=4,'yl'=2,'x'=8,'core'=2,'yh'=4] {'x'}, dimensions={0} | all-to-all | bytes 786432 | tf_op jit(solution)/shard_map/all_to_all | solution.py:100
  74.6 5.1 %shard_map.40 = bf16[256,512]{1,0:T(8,128)(2,1)S(1)} custom-call(bf16[6,256,128]{2,1,0:T(8,128)(2,1)S(1)} %bitcast.14, bf16[256,512]{1,0:T(8,128)(2,1)S(1)} %bitcast.16), custom_call_target="tpu_custom_call" | custom-call | tf_op jit(solution)/shard_map/pallas_call | solution.py:21
  79.7 15.1 %all_to_all.27 = bf16[8,32,512]{2,1,0:T(8,128)(2,1)S(1)} all-to-all(bf16[8,32,512]{2,1,0:T(8,128)(2,1)S(1)} %bitcast.17), channel_id=1, replica_groups=mesh['z'=4,'yl'=2,'x'=8,'core'=2,'yh'=4] {'yh','core'}, dimensions={0} | all-to-all | bytes 524288 | tf_op jit(solution)/shard_map/all_to_all | solution.py:102
  94.9 0.7 copy.7
  (1 shorter events, 0.0 us)
Async XLA Ops:
  0.0 0.7 copy-start.1
  2.1 10.3 %collective-permute-start = (bf16[512,512]{1,0:T(8,128)(2,1)S(1)}, bf16[512,512]{1,0:T(8,128)(2,1)S(1)}, u32[]{:S(2)}, u32[]{:S(2)}) collective-permute-start(bf16[512,512]{1,0:T(8,128)(2,1)S(1)} %get-tuple-element.5), channel_id=1, source_target_pairs={{0,4},{4,0},{1,5},{5,1},{2,6},{6,2},{3,7},{7,3},{8,12},{12,8},{9,1... | collective-permute-start | bytes 1572872 | tf_op jit(solution)/shard_map/ppermute | solution.py:93
  24.2 7.1 %copy-start = (bf16[32,4096]{1,0:T(8,128)(2,1)S(1)}, bf16[32,4096]{1,0:T(8,128)(2,1)}, u32[]{:S(2)}) copy-start(bf16[32,4096]{1,0:T(8,128)(2,1)} %param.5) | copy-start | bytes 786436
  24.2 19.2 %all-to-all-start.1 = ((bf16[8,192,128]{2,1,0:T(8,128)(2,1)}), bf16[8,192,128]{2,1,0:T(8,128)(2,1)S(1)}, u32[]{:S(2)}, u32[]{:S(2)}) async-start(bf16[8,192,128]{2,1,0:T(8,128)(2,1)} %shard_map.38), calls=%async_computation.1 | async-start | bytes 786432 | tf_op jit(solution)/shard_map/all_to_all | solution.py:99
  43.4 20.4 %all-to-all-start.3 = ((bf16[8,32,512]{2,1,0:T(8,128)(2,1)}), bf16[8,32,512]{2,1,0:T(8,128)(2,1)S(1)}, u32[]{:S(2)}, u32[]{:S(2)}) async-start(bf16[8,32,512]{2,1,0:T(8,128)(2,1)} %bitcast.13), calls=%async_computation.3 | async-start | bytes 524288 | tf_op jit(solution)/shard_map/all_to_all | solution.py:96

commit v2 on v1

v2 whole, which is shorter than its diff:
```python
import jax
import jax.numpy as jnp
from jax import lax
from jax.experimental import pallas as pl
from jax.experimental.pallas import tpu as pltpu
from jax.sharding import Mesh, PartitionSpec as P

B = 512
H = 256
LANES = 128
DAMPING = 0.05
BF = jnp.bfloat16
F32 = jnp.float32
AXES = (("z", 8), ("yl", 2), ("x", 4), ("core", 2), ("yh", 4))
REDUCE = ("z", "yl", "x")
SHARDS = 64
PACKED = 3 * 2 * H // SHARDS
ROWS = 32
TOKENS = 512
MASK_ROWS = 16
SLAB = TOKENS + 4 * ROWS + MASK_ROWS
VMEM = pl.BlockSpec(memory_space=pltpu.VMEM)
HBM = pl.BlockSpec(memory_space=pl.ANY)


def call(kernel, outs, operands, specs=None, scratch=(), flops=0):
    shapes = [jax.ShapeDtypeStruct(*out) for out in outs]
    moved = sum(o.size * o.dtype.itemsize for o in (*operands, *shapes))
    return pl.pallas_call(
        kernel,
        out_shape=shapes,
        in_specs=specs or [VMEM] * len(operands),
        out_specs=[VMEM] * len(outs),
        scratch_shapes=scratch,
        cost_estimate=pl.CostEstimate(flops=flops, bytes_accessed=moved, transcendentals=0),
        compiler_params=pltpu.CompilerParams(vmem_limit_bytes=40 * 1024 * 1024),
    )(*operands)


def at(index, size=B):
    return pl.ds(pl.multiple_of(index * size, size), size)


def slab_kernel(act_ref, mask_ref, grad_ref, out_ref, sems):
    other = 1 - lax.axis_index("core")
    copies = [pltpu.make_async_copy(act_ref.at[:, at(other)], out_ref.at[pl.ds(0, TOKENS)], sems.at[0])]
    for k in range(4):
        rows = pl.ds(TOKENS + ROWS * k, ROWS)
        copies.append(pltpu.make_async_copy(grad_ref.at[:, at(2 * k + other)], out_ref.at[rows], sems.at[k + 1]))
    for copy in copies:
        copy.start()
    mask = mask_ref[...].astype(F32).astype(BF)
    out_ref[pl.ds(TOKENS + 4 * ROWS, MASK_ROWS), :] = jnp.broadcast_to(mask, (MASK_ROWS, TOKENS))
    for copy in copies:
        copy.wait()


def masked(columns, mask):
    column = jnp.broadcast_to(mask.astype(F32), (LANES, TOKENS)).T.astype(BF)
    return columns * jnp.concatenate([column] * (B // LANES), axis=1)


def triangle(columns):
    dot = lambda a, b: lax.dot_general(a, b, (((0,), (0,)), ((), ())), preferred_element_type=F32)
    low, high = columns[:, :H], columns[:, H:]
    return dot(low, low), dot(high, low), dot(high, high)


def own_kernel(act_ref, mask_ref, out_ref, held, sem):
    copy = pltpu.make_async_copy(act_ref.at[:, at(lax.axis_index("core"))], held, sem)
    copy.start()
    mask = mask_ref[...].astype(F32)
    copy.wait()
    for slot, block in enumerate(triangle(masked(held[...], mask))):
        out_ref[slot] = block


def gram_kernel(slab_ref, own_ref, grad_ref, out_ref, send_ref, keep_ref):
    mask = slab_ref[pl.ds(TOKENS + 4 * ROWS, MASK_ROWS), :][:1]
    for slot, block in enumerate(triangle(masked(slab_ref[pl.ds(0, TOKENS), :], mask))):
        block += own_ref[slot]
        for half in range(2):
            out_ref[2 * slot + half] = block[:, half * LANES : (half + 1) * LANES].astype(BF)
    core = lax.axis_index("core")
    upper = lax.axis_index("yh") // 2
    for ref, part in ((send_ref, 1 - upper), (keep_ref, upper)):
        for k in range(2):
            ref[k, core] = grad_ref[:, at(2 * (2 * part + k) + core)]
            ref[k, 1 - core] = slab_ref[pl.ds(pl.multiple_of(TOKENS + ROWS * (2 * part + k), ROWS), ROWS), :]


def sum_kernel(parts_ref, kept_ref, come_ref, out_ref, send_ref, keep_ref):
    total = parts_ref[0].astype(F32)
    for part in range(1, SHARDS):
        total += parts_ref[part].astype(F32)
    rounded = total.astype(BF)
    for copy in range(SHARDS):
        out_ref[copy] = rounded
    upper, lower = lax.axis_index("yh") // 2, lax.axis_index("yh") % 2
    for ref, part in ((send_ref, 1 - lower), (keep_ref, lower)):
        ref[upper] = kept_ref[part]
        ref[1 - upper] = come_ref[part]


def split(array):
    high = array.astype(BF)
    return high, (array - high.astype(F32)).astype(BF)


def dot3(left, right):
    one = lambda a, b: jnp.dot(a, b, preferred_element_type=F32)
    return one(left[0], right[0]) + (one(left[0], right[1]) + one(left[1], right[0]))


def root_kernel(gram_ref, kept_ref, come_ref, out_ref):
    packed = [gram_ref[piece].astype(F32) for piece in range(6)]
    first, cross, last = [jnp.concatenate(packed[2 * k : 2 * k + 2], axis=1) for k in range(3)]
    gram = jnp.concatenate(
        [jnp.concatenate([first, cross.T], axis=1), jnp.concatenate([cross, last], axis=1)], axis=0
    )
    row = lax.broadcasted_iota(jnp.int32, (B, B), 0)
    column = lax.broadcasted_iota(jnp.int32, (B, B), 1)
    identity = jnp.where(row == column, 1.0, 0.0).astype(F32)
    damped = gram * (1.0 / 65536) + DAMPING * identity
    norm = jnp.max(jnp.sum(jnp.abs(damped), axis=1, keepdims=True), axis=0, keepdims=True)
    y = damped / norm
    ys = split(y)
    square = dot3(ys, ys)
    squares = split(square)
    z = 2.25 * identity - 2.4375 * y + 1.6875 * square + dot3(squares, split(0.0625 * square - 0.5625 * y))
    zs = split(z)
    root = 1.5 * z - 0.5 * dot3(split(dot3(zs, zs)), split(dot3(ys, zs)))
    root = (root / jnp.sqrt(norm)).astype(BF)
    lower = lax.axis_index("yh") % 2
    for ref, place in ((kept_ref, lower), (come_ref, 1 - lower)):
        product = jnp.dot(ref[...].reshape(4 * ROWS, B), root, preferred_element_type=F32).astype(BF)
        for upper in range(2):
            out_ref[upper, place] = product[2 * ROWS * upper : 2 * ROWS * (upper + 1)]


def local(activations, token_mask, gradient):
    mask = token_mask.reshape(1, TOKENS)
    dma = pltpu.SemaphoreType.DMA
    (slab,) = call(
        slab_kernel, [((SLAB, B), BF)], (activations, mask, gradient), [HBM, VMEM, HBM], [dma((5,))]
    )
    other = lax.ppermute(slab, "core", [(0, 1), (1, 0)])
    (own,) = call(
        own_kernel,
        [((3, H, H), F32)],
        (activations, mask),
        [HBM, VMEM],
        [pltpu.VMEM((TOKENS, B), BF), dma],
        flops=6 * TOKENS * H * H,
    )
    half = ((2, 2, ROWS, B), BF)
    packed, send, kept = call(
        gram_kernel, [((6, H, LANES), BF), half, half], (other, own, gradient), flops=6 * TOKENS * H * H
    )
    come = lax.ppermute(send, "yh", [(k, k ^ 2) for k in range(4)])
    parts = lax.all_to_all(packed.reshape(SHARDS, PACKED, LANES), REDUCE, 0, 0)
    copies, send, kept = call(sum_kernel, [(parts.shape, BF), half, half], (parts, kept, come))
    come = lax.ppermute(send, "yh", [(k, k ^ 1) for k in range(4)])
    packed = lax.all_to_all(copies, REDUCE, 0, 0).reshape(6, H, LANES)
    (product,) = call(
        root_kernel, [((2, 2, 2 * ROWS, B), BF)], (packed, kept, come), flops=2 * 16 * B * B * B
    )
    product = lax.all_to_all(product.reshape(8, ROWS, B), ("yh", "core"), 0, 0)
    return product.transpose(1, 0, 2).reshape(ROWS, 8 * B)


def solution(mesh):
    names, sizes = zip(*AXES)
    cut = Mesh(mesh.devices.reshape(sizes), names)
    dp = names[:4]
    placed = (P(dp, "yh"), P(dp), P(names, None))
    return jax.shard_map(local, mesh=cut, in_specs=placed, out_specs=P(names, None), check_vma=False)
```

time: 96.1 us -> 88.4 us (0.920)
  blocking collectives: 36.3 us -> 18.9 us
  starting transfers between devices: 25.5 us -> 37.1 us
  waiting for transfers between devices: 23.6 us -> 20.2 us
  Pallas kernels: 6.59 us -> 8.06 us
  local copies, waits for them, and re-layouts: 2.13 us -> 3.58 us
  other arithmetic: 1.44 us -> 0 us
    all_to_all x3 -> x1, blocking collectives: 36.3 us -> 18.9 us  [local(): product = lax.all_to_all(product.reshape(8, ROWS, B), ('yh', 'core'), 0, 0)]
    all_to_all x2, waiting for transfers between devices: 22.1 us -> 5.29 us  [the longest x1 4.28 us: local(): packed = lax.all_to_all(copies, REDUCE, 0, 0).reshape(6, H, LANES)]
    ppermute x1 -> x3, waiting for transfers between devices: 1.51 us -> 14.9 us  [the longest x1 6.93 us: local(): come = lax.ppermute(send, 'yh', [(k, k ^ 2) for k in range(4)])]
    ppermute x1 -> x3, starting transfers between devices: 8.79 us -> 17.4 us  [the longest x1 8.92 us: local(): other = lax.ppermute(slab, 'core', [(0, 1), (1, 0)])]
    all_to_all x2, starting transfers between devices: 16.7 us -> 19.7 us  [the longest x1 10.6 us: local(): packed = lax.all_to_all(copies, REDUCE, 0, 0).reshape(6, H, LANES)]
    unnamed x4 -> x8, local copies, waits for them, and re-layouts: 0.68 us -> 2.86 us
    pallas_call x4 -> x5, Pallas kernels: 6.59 us -> 8.06 us  [call(): pl.pallas_call(kernel, out_shape=shapes, in_specs=specs or [VMEM] * len(o...]
    mul x1 -> x0, other arithmetic: 1.43 us -> none  [columns(): lax.dynamic_slice(activations, (0, index * B), (activations.shape[0], B))]
  transfers between devices with their start and end apart: 3 -> 5, of which waited for: 3 -> 5; matrix products, arithmetic and copies ran while one was open for 1% -> 0% of each run, Pallas kernels for 0% -> 1%
where the time goes in v2:
time: 88.4 us; the launch traced here: 88 us
  starting transfers between devices  37.1 us (42%)
  waiting for transfers between devices  20.2 us (23%)
  blocking collectives  18.9 us (21%)
  Pallas kernels  8.06 us (9%)
  local copies, waits for them, and re-layouts  3.58 us (4%)
    all_to_all x1, blocking collectives, local(): product = lax.all_to_all(product.reshape(8, ROWS, B), ('yh', 'core'), 0, 0)  18.9 us
    all_to_all x1, starting transfers between devices, local(): packed = lax.all_to_all(copies, REDUCE, 0, 0).reshape(6, H, LANES)  10.6 us
    all_to_all x1, starting transfers between devices, local(): parts = lax.all_to_all(packed.reshape(SHARDS, PACKED, LANES), REDUCE, 0, 0)  9.14 us
    ppermute x1, starting transfers between devices, local(): other = lax.ppermute(slab, 'core', [(0, 1), (1, 0)])  8.92 us
    pallas_call x5, Pallas kernels, call(): pl.pallas_call(kernel, out_shape=shapes, in_specs=specs or [VMEM] * len(o...  8.06 us
    ppermute x1, waiting for transfers between devices, local(): come = lax.ppermute(send, 'yh', [(k, k ^ 2) for k in range(4)])  6.93 us
    ppermute x1, waiting for transfers between devices, local(): come = lax.ppermute(send, 'yh', [(k, k ^ 1) for k in range(4)])  6.88 us
    ppermute x1, starting transfers between devices, local(): come = lax.ppermute(send, 'yh', [(k, k ^ 2) for k in range(4)])  6.56 us
  transfers between devices with their start and end apart: 5, of which 5 were waited for; matrix products, arithmetic and copies ran while one was open for 0% of the time, Pallas kernels for 1%

profile of v2, /device:TPU:1, one launch (start us, length us, event | category | flops | bytes accessed | tf_op | source)
XLA Modules:
  0.0 88.0 jit_solution(9015902042519055126)
XLA Ops:
  0.0 0.0 copy-start
  0.0 1.2 %copy-done = bf16[512,1024]{1,0:T(8,128)(2,1)S(1)} copy-done((bf16[512,1024]{1,0:T(8,128)(2,1)S(1)}, bf16[512,1024]{1,0:T(8,128)(2,1)}, u32[]{:S(2)}) %copy-start) | copy-done | bytes 1048600
  1.2 0.0 copy-start.1
  1.2 0.9 %copy-done.1 = bf16[32,4096]{1,0:T(8,128)(2,1)S(1)} copy-done((bf16[32,4096]{1,0:T(8,128)(2,1)S(1)}, bf16[32,4096]{1,0:T(8,128)(2,1)}, u32[]{:S(2)}) %copy-start.1) | copy-done | bytes 262168
  2.2 0.7 copy-done.3
  2.9 0.2 shard_map.37
  3.0 0.0 copy-start.2
  3.0 8.9 %collective-permute-start = (bf16[656,512]{1,0:T(8,128)(2,1)S(1)}, bf16[656,512]{1,0:T(8,128)(2,1)S(1)}, u32[]{:S(2)}, u32[]{:S(2)}) collective-permute-start(bf16[656,512]{1,0:T(8,128)(2,1)S(1)} %shard_map.37), channel_id=1, source_target_pairs={{0,4},{4,0},{1,5},{5,1},{2,6},{6,2},{3,7},{7,3},{8,12},{12,8},{9,1... | collective-permute-start | bytes 2015240 | tf_op jit(solution)/shard_map/ppermute | solution.py:147
  12.0 0.6 shard_map.38.own_ref
  12.6 1.1 %collective-permute-done.slab_ref = bf16[656,512]{1,0:T(8,128)(2,1)S(1)} collective-permute-done((bf16[656,512]{1,0:T(8,128)(2,1)S(1)}, bf16[656,512]{1,0:T(8,128)(2,1)S(1)}, u32[]{:S(2)}, u32[]{:S(2)}) %collective-permute-start) | collective-permute-done | bytes 671776 | tf_op jit(solution)/shard_map/ppermute | solution.py:147
  13.7 0.0 copy-done.2
  13.7 1.3 %shard_map.39 = (bf16[6,256,128]{2,1,0:T(8,128)(2,1)}, bf16[2,2,32,512]{3,2,1,0:T(8,128)(2,1)S(1)}, bf16[2,2,32,512]{3,2,1,0:T(8,128)(2,1)S(1)}) custom-call(bf16[656,512]{1,0:T(8,128)(2,1)S(1)} %collective-permute-done.slab_ref, f32[3,256,256]{2,1,0:T(8,128)S(1)} %shard_map.38.own_ref, bf16[32,4096]{1,0:T(8,128)(2,1)S(1)} %copy-done.2), custom_call_target="tpu_custom_call" | custom-call | flops 201326592 | bytes 2375680 | tf_op jit(solution)/shard_map/pallas_call | solution.py:29
  15.0 9.1 %all-to-all-start = ((bf16[64,24,128]{2,1,0:T(8,128)(2,1)}), bf16[64,24,128]{2,1,0:T(8,128)(2,1)S(1)}, u32[]{:S(2)}, u32[]{:S(2)}) async-start(bf16[64,24,128]{2,1,0:T(8,128)(2,1)} %bitcast.1), calls=%async_computation | async-start | bytes 786432 | tf_op jit(solution)/shard_map/all_to_all | solution.py:161
  24.1 6.6 %collective-permute-start.1 = (bf16[2,2,32,512]{3,2,1,0:T(8,128)(2,1)S(1)}, bf16[2,2,32,512]{3,2,1,0:T(8,128)(2,1)S(1)}, u32[]{:S(2)}, u32[]{:S(2)}) collective-permute-start(bf16[2,2,32,512]{3,2,1,0:T(8,128)(2,1)S(1)} %get-tuple-element.13), channel_id=1, source_target_pairs={{0,2},{1,3},{2,0},{3,1},{4,6},{5,7},{6,4},{7,5},{8,10},{9,11},{10,... | collective-permute-start | bytes 393224 | tf_op jit(solution)/shard_map/ppermute | solution.py:160
  30.7 6.9 %collective-permute-done.1.come_ref = bf16[2,2,32,512]{3,2,1,0:T(8,128)(2,1)S(1)} collective-permute-done((bf16[2,2,32,512]{3,2,1,0:T(8,128)(2,1)S(1)}, bf16[2,2,32,512]{3,2,1,0:T(8,128)(2,1)S(1)}, u32[]{:S(2)}, u32[]{:S(2)}) %collective-permute-start.1) | collective-permute-done | bytes 131104 | tf_op jit(solution)/shard_map/ppermute | solution.py:160
  37.6 1.0 %all-to-all-done.parts_ref = bf16[64,24,128]{2,1,0:T(8,128)(2,1)S(1)} async-done(((bf16[64,24,128]{2,1,0:T(8,128)(2,1)}), bf16[64,24,128]{2,1,0:T(8,128)(2,1)S(1)}, u32[]{:S(2)}, u32[]{:S(2)}) %all-to-all-start) | async-done | bytes 393248 | tf_op jit(solution)/shard_map/all_to_all | solution.py:161
  38.6 0.9 shard_map.40
  39.5 10.6 %all-to-all-start.1 = ((bf16[64,24,128]{2,1,0:T(8,128)(2,1)}), bf16[64,24,128]{2,1,0:T(8,128)(2,1)S(1)}, u32[]{:S(2)}, u32[]{:S(2)}) async-start(bf16[64,24,128]{2,1,0:T(8,128)(2,1)} %get-tuple-element.14), calls=%async_computation.1 | async-start | bytes 786432 | tf_op jit(solution)/shard_map/all_to_all | solution.py:164
  50.1 1.9 %collective-permute-start.2 = (bf16[2,2,32,512]{3,2,1,0:T(8,128)(2,1)S(1)}, bf16[2,2,32,512]{3,2,1,0:T(8,128)(2,1)S(1)}, u32[]{:S(2)}, u32[]{:S(2)}) collective-permute-start(bf16[2,2,32,512]{3,2,1,0:T(8,128)(2,1)S(1)} %get-tuple-element.16), channel_id=1, source_target_pairs={{0,1},{1,0},{2,3},{3,2},{4,5},{5,4},{6,7},{7,6},{8,9},{9,8},{10,11... | collective-permute-start | bytes 393224 | tf_op jit(solution)/shard_map/ppermute | solution.py:163
  52.0 6.9 %collective-permute-done.2.come_ref = bf16[2,2,32,512]{3,2,1,0:T(8,128)(2,1)S(1)} collective-permute-done((bf16[2,2,32,512]{3,2,1,0:T(8,128)(2,1)S(1)}, bf16[2,2,32,512]{3,2,1,0:T(8,128)(2,1)S(1)}, u32[]{:S(2)}, u32[]{:S(2)}) %collective-permute-start.2) | collective-permute-done | bytes 131104 | tf_op jit(solution)/shard_map/ppermute | solution.py:163
  58.9 4.3 %all-to-all-done.1 = bf16[64,24,128]{2,1,0:T(8,128)(2,1)S(1)} async-done(((bf16[64,24,128]{2,1,0:T(8,128)(2,1)}), bf16[64,24,128]{2,1,0:T(8,128)(2,1)S(1)}, u32[]{:S(2)}, u32[]{:S(2)}) %all-to-all-start.1) | async-done | bytes 393248 | tf_op jit(solution)/shard_map/all_to_all | solution.py:164
  63.1 5.2 %shard_map.41 = bf16[2,2,64,512]{3,2,1,0:T(8,128)(2,1)S(1)} custom-call(bf16[6,256,128]{2,1,0:T(8,128)(2,1)S(1)} %bitcast.7, bf16[2,2,32,512]{3,2,1,0:T(8,128)(2,1)S(1)} %get-tuple-element.15.kept_ref, bf16[2,2,32,512]{3,2,1,0:T(8,128)(2,1)S(1)} %collective-permute-done.2.come_ref), custom_call_target="tpu_custom_call" | custom-call | flops 4294967296 | bytes 917504 | tf_op jit(solution)/shard_map/pallas_call | solution.py:29
  68.3 18.9 %all_to_all.15 = bf16[8,32,512]{2,1,0:T(8,128)(2,1)S(1)} all-to-all(bf16[8,32,512]{2,1,0:T(8,128)(2,1)S(1)} %bitcast.8), channel_id=1, replica_groups=mesh['z'=8,'yl'=2,'x'=4,'core'=2,'yh'=4] {'yh','core'}, dimensions={0} | all-to-all | bytes 524288 | tf_op jit(solution)/shard_map/all_to_all | solution.py:168
  87.2 0.7 copy.5
  (1 shorter events, 0.0 us)
Async XLA Ops:
  0.0 1.2 %copy-start = (bf16[512,1024]{1,0:T(8,128)(2,1)S(1)}, bf16[512,1024]{1,0:T(8,128)(2,1)}, u32[]{:S(2)}) copy-start(bf16[512,1024]{1,0:T(8,128)(2,1)} %act_ref.3) | copy-start | bytes 3145732
  1.2 0.9 %copy-start.1 = (bf16[32,4096]{1,0:T(8,128)(2,1)S(1)}, bf16[32,4096]{1,0:T(8,128)(2,1)}, u32[]{:S(2)}) copy-start(bf16[32,4096]{1,0:T(8,128)(2,1)} %grad_ref.3) | copy-start | bytes 786436
  2.2 0.7 copy-start.3
  3.0 10.7 %copy-start.2 = (bf16[32,4096]{1,0:T(8,128)(2,1)S(1)}, bf16[32,4096]{1,0:T(8,128)(2,1)}, u32[]{:S(2)}) copy-start(bf16[32,4096]{1,0:T(8,128)(2,1)} %grad_ref.3) | copy-start | bytes 786436
  3.0 10.7 %collective-permute-start = (bf16[656,512]{1,0:T(8,128)(2,1)S(1)}, bf16[656,512]{1,0:T(8,128)(2,1)S(1)}, u32[]{:S(2)}, u32[]{:S(2)}) collective-permute-start(bf16[656,512]{1,0:T(8,128)(2,1)S(1)} %shard_map.37), channel_id=1, source_target_pairs={{0,4},{4,0},{1,5},{5,1},{2,6},{6,2},{3,7},{7,3},{8,12},{12,8},{9,1... | collective-permute-start | bytes 2015240 | tf_op jit(solution)/shard_map/ppermute | solution.py:147
  15.0 23.7 %all-to-all-start = ((bf16[64,24,128]{2,1,0:T(8,128)(2,1)}), bf16[64,24,128]{2,1,0:T(8,128)(2,1)S(1)}, u32[]{:S(2)}, u32[]{:S(2)}) async-start(bf16[64,24,128]{2,1,0:T(8,128)(2,1)} %bitcast.1), calls=%async_computation | async-start | bytes 786432 | tf_op jit(solution)/shard_map/all_to_all | solution.py:161
  24.1 13.5 %collective-permute-start.1 = (bf16[2,2,32,512]{3,2,1,0:T(8,128)(2,1)S(1)}, bf16[2,2,32,512]{3,2,1,0:T(8,128)(2,1)S(1)}, u32[]{:S(2)}, u32[]{:S(2)}) collective-permute-start(bf16[2,2,32,512]{3,2,1,0:T(8,128)(2,1)S(1)} %get-tuple-element.13), channel_id=1, source_target_pairs={{0,2},{1,3},{2,0},{3,1},{4,6},{5,7},{6,4},{7,5},{8,10},{9,11},{10,... | collective-permute-start | bytes 393224 | tf_op jit(solution)/shard_map/ppermute | solution.py:160
  39.5 23.7 %all-to-all-start.1 = ((bf16[64,24,128]{2,1,0:T(8,128)(2,1)}), bf16[64,24,128]{2,1,0:T(8,128)(2,1)S(1)}, u32[]{:S(2)}, u32[]{:S(2)}) async-start(bf16[64,24,128]{2,1,0:T(8,128)(2,1)} %get-tuple-element.14), calls=%async_computation.1 | async-start | bytes 786432 | tf_op jit(solution)/shard_map/all_to_all | solution.py:164
  50.1 8.8 %collective-permute-start.2 = (bf16[2,2,32,512]{3,2,1,0:T(8,128)(2,1)S(1)}, bf16[2,2,32,512]{3,2,1,0:T(8,128)(2,1)S(1)}, u32[]{:S(2)}, u32[]{:S(2)}) collective-permute-start(bf16[2,2,32,512]{3,2,1,0:T(8,128)(2,1)S(1)} %get-tuple-element.16), channel_id=1, source_target_pairs={{0,1},{1,0},{2,3},{3,2},{4,5},{5,4},{6,7},{7,6},{8,9},{9,8},{10,11... | collective-permute-start | bytes 393224 | tf_op jit(solution)/shard_map/ppermute | solution.py:163

commit v3 on v2

v3 whole, which is shorter than its diff:
```python
import jax
import jax.numpy as jnp
from jax import lax
from jax.experimental import pallas as pl
from jax.experimental.pallas import tpu as pltpu
from jax.sharding import Mesh, PartitionSpec as P

B = 512
H = 256
LANES = 128
DAMPING = 0.05
BF = jnp.bfloat16
F32 = jnp.float32
AXES = (("z", 8), ("yl", 2), ("x", 4), ("core", 2), ("yh", 4))
NAMES = tuple(name for name, _ in AXES)
PLANE = ("yl", "x")
SHARDS = 8
PACKED = 3 * 2 * H // SHARDS
ROWS = 32
TOKENS = 512
MASK_ROWS = 16
SLAB = TOKENS + 4 * ROWS + MASK_ROWS
VMEM_MIB = 16
VMEM = pl.BlockSpec(memory_space=pltpu.VMEM)
HBM = pl.BlockSpec(memory_space=pltpu.HBM)


def groups():
    at = lambda z, yl, x, core, yh: (((z * 2 + yl) * 4 + x) * 2 + core) * 4 + yh
    every = [(z, w, x) for z in range(8) for w in range(2) for x in range(4)]
    return [[at(z, w ^ (yh >> 1), x, core, yh) for yh in range(4) for core in range(2)] for z, w, x in every]


def pairs(flip):
    return [(group[2 * yh + core], group[2 * (yh ^ flip) + core]) for group in groups() for yh in range(4) for core in range(2)]


def call(kernel, outs, operands, specs=None, scratch=(), flops=0):
    shapes = [jax.ShapeDtypeStruct(*out) for out in outs]
    moved = sum(o.size * o.dtype.itemsize for o in (*operands, *shapes))
    return pl.pallas_call(
        kernel,
        out_shape=shapes,
        in_specs=specs or [VMEM] * len(operands),
        out_specs=[VMEM] * len(outs),
        scratch_shapes=scratch,
        cost_estimate=pl.CostEstimate(flops=flops, bytes_accessed=moved, transcendentals=0),
        compiler_params=pltpu.CompilerParams(vmem_limit_bytes=VMEM_MIB * 1024 * 1024),
    )(*operands)


def at(index, size=B):
    return pl.ds(pl.multiple_of(index * size, size), size)


def slab_kernel(act_ref, mask_ref, grad_ref, out_ref, mask_held, sems):
    other = 1 - lax.axis_index("core")
    copies = [pltpu.make_async_copy(act_ref.at[:, at(other)], out_ref.at[pl.ds(0, TOKENS)], sems.at[0])]
    for k in range(4):
        rows = pl.ds(TOKENS + ROWS * k, ROWS)
        copies.append(pltpu.make_async_copy(grad_ref.at[:, at(2 * k + other)], out_ref.at[rows], sems.at[k + 1]))
    copies.insert(0, pltpu.make_async_copy(mask_ref, mask_held, sems.at[5]))
    for copy in copies:
        copy.start()
    copies.pop(0).wait()
    mask = mask_held[...].astype(F32).astype(BF)
    out_ref[pl.ds(TOKENS + 4 * ROWS, MASK_ROWS), :] = jnp.broadcast_to(mask, (MASK_ROWS, TOKENS))
    for copy in copies:
        copy.wait()


def masked(columns, mask):
    column = jnp.broadcast_to(mask.astype(F32), (LANES, TOKENS)).T.astype(BF)
    return columns * jnp.concatenate([column] * (B // LANES), axis=1)


def triangle(columns):
    dot = lambda a, b: lax.dot_general(a, b, (((0,), (0,)), ((), ())), preferred_element_type=F32)
    low, high = columns[:, :H], columns[:, H:]
    return dot(low, low), dot(high, low), dot(high, high)


def own_kernel(act_ref, mask_ref, out_ref, held, mask_held, sems):
    columns = pltpu.make_async_copy(act_ref.at[:, at(lax.axis_index("core"))], held, sems.at[0])
    mask = pltpu.make_async_copy(mask_ref, mask_held, sems.at[1])
    columns.start()
    mask.start()
    columns.wait()
    mask.wait()
    for slot, block in enumerate(triangle(masked(held[...], mask_held[...]))):
        out_ref[slot] = block


def gram_kernel(slab_ref, own_ref, out_ref):
    mask = slab_ref[pl.ds(TOKENS + 4 * ROWS, MASK_ROWS), :][:1]
    for slot, block in enumerate(triangle(masked(slab_ref[pl.ds(0, TOKENS), :], mask))):
        block += own_ref[slot]
        for half in range(2):
            out_ref[2 * slot + half] = block[:, half * LANES : (half + 1) * LANES].astype(BF)


def first_kernel(slab_ref, grad_ref, send_ref, keep_ref, held, sem):
    copy = pltpu.make_async_copy(grad_ref, held, sem)
    copy.start()
    core, upper = lax.axis_index("core"), lax.axis_index("yh") // 2
    copy.wait()
    for ref, part in ((send_ref, 1 - upper), (keep_ref, upper)):
        for k in range(2):
            ref[k, core] = held[:, at(2 * (2 * part + k) + core)]
            ref[k, 1 - core] = slab_ref[pl.ds(pl.multiple_of(TOKENS + ROWS * (2 * part + k), ROWS), ROWS), :]


def spread(parts_ref, out_ref):
    total = parts_ref[0].astype(F32)
    for part in range(1, SHARDS):
        total += parts_ref[part].astype(F32)
    rounded = total.astype(BF)
    for copy in range(SHARDS):
        out_ref[copy] = rounded


def sum_kernel(parts_ref, kept_ref, come_ref, out_ref, send_ref, keep_ref):
    spread(parts_ref, out_ref)
    upper, lower = lax.axis_index("yh") // 2, lax.axis_index("yh") % 2
    for ref, part in ((send_ref, 1 - lower), (keep_ref, lower)):
        ref[upper] = kept_ref[part]
        ref[1 - upper] = come_ref[part]


def split(array):
    high = array.astype(BF)
    return high, (array - high.astype(F32)).astype(BF)


def dot3(left, right):
    one = lambda a, b: jnp.dot(a, b, preferred_element_type=F32)
    return one(left[0], right[0]) + (one(left[0], right[1]) + one(left[1], right[0]))


def root_kernel(gram_ref, out_ref):
    packed = [gram_ref[piece].astype(F32) for piece in range(6)]
    first, cross, last = [jnp.concatenate(packed[2 * k : 2 * k + 2], axis=1) for k in range(3)]
    gram = jnp.concatenate(
        [jnp.concatenate([first, cross.T], axis=1), jnp.concatenate([cross, last], axis=1)], axis=0
    )
    row = lax.broadcasted_iota(jnp.int32, (B, B), 0)
    column = lax.broadcasted_iota(jnp.int32, (B, B), 1)
    identity = jnp.where(row == column, 1.0, 0.0).astype(F32)
    damped = gram * (1.0 / 65536) + DAMPING * identity
    norm = jnp.max(jnp.sum(jnp.abs(damped), axis=1, keepdims=True), axis=0, keepdims=True)
    y = damped / norm
    ys = split(y)
    square = dot3(ys, ys)
    squares = split(square)
    z = 2.25 * identity - 2.4375 * y + 1.6875 * square + dot3(squares, split(0.0625 * square - 0.5625 * y))
    zs = split(z)
    root = 1.5 * z - 0.5 * dot3(split(dot3(zs, zs)), split(dot3(ys, zs)))
    out_ref[...] = (root / jnp.sqrt(norm)).astype(BF)


def apply_kernel(root_ref, kept_ref, come_ref, out_ref):
    turn = lax.axis_index("yh") // 2 + lax.axis_index("yh") % 2
    for ref, other in ((kept_ref, 0), (come_ref, 1)):
        product = jnp.dot(ref[...].reshape(4 * ROWS, B), root_ref[...], preferred_element_type=F32).astype(BF)
        for upper in range(2):
            out_ref[upper, (turn + upper + other) % 2] = product[2 * ROWS * upper : 2 * ROWS * (upper + 1)]


def local(activations, token_mask, gradient):
    mask = pltpu.with_memory_space_constraint(token_mask.reshape(1, TOKENS), pltpu.HBM)
    activations = pltpu.with_memory_space_constraint(activations, pltpu.HBM)
    gradient = pltpu.with_memory_space_constraint(gradient, pltpu.HBM)
    dma = pltpu.SemaphoreType.DMA
    (slab,) = call(
        slab_kernel, [((SLAB, B), BF)], (activations, mask, gradient), [HBM] * 3, [pltpu.VMEM((1, TOKENS), jnp.int32), dma((6,))]
    )
    other = lax.ppermute(slab, "core", [(0, 1), (1, 0)])
    (own,) = call(
        own_kernel,
        [((3, H, H), F32)],
        (activations, mask),
        [HBM, HBM],
        [pltpu.VMEM((TOKENS, B), BF), pltpu.VMEM((1, TOKENS), jnp.int32), dma((2,))],
        flops=6 * TOKENS * H * H,
    )
    half = ((2, 2, ROWS, B), BF)
    send, kept = call(
        first_kernel, [half, half], (other, gradient), [VMEM, HBM], [pltpu.VMEM((ROWS, 8 * B), BF), dma]
    )
    come = lax.ppermute(send, NAMES, pairs(3))
    (packed,) = call(gram_kernel, [((6, H, LANES), BF)], (other, own), flops=6 * TOKENS * H * H)
    parts = lax.all_to_all(packed.reshape(SHARDS, PACKED, LANES), PLANE, 0, 0)
    (copies,) = call(spread, [(parts.shape, BF)], (parts,))
    parts = lax.all_to_all(copies, "z", 0, 0)
    copies, send, kept = call(sum_kernel, [(parts.shape, BF), half, half], (parts, kept, come))
    come = lax.ppermute(send, NAMES, pairs(1))
    packed = lax.all_to_all(copies, PLANE, 0, 0).reshape(6, H, LANES)
    (root,) = call(root_kernel, [((B, B), BF)], (packed,), flops=2 * 15 * B * B * B)
    (product,) = call(apply_kernel, [((2, 2, 2 * ROWS, B), BF)], (root, kept, come), flops=2 * 8 * ROWS * B * B)
    product = lax.all_to_all(product.reshape(8, ROWS, B), NAMES, 0, 0, axis_index_groups=groups())
    return product.transpose(1, 0, 2).reshape(ROWS, 8 * B)


def solution(mesh):
    names, sizes = zip(*AXES)
    cut = Mesh(mesh.devices.reshape(sizes), names)
    dp = names[:4]
    placed = (P(dp, "yh"), P(dp), P(names, None))
    return jax.shard_map(local, mesh=cut, in_specs=placed, out_specs=P(names, None), check_vma=False)
```

time: 88.4 us -> 79.4 us (0.90)
  blocking collectives: 18.9 us -> 29.6 us
  waiting for transfers between devices: 20.2 us -> 9.67 us
  starting transfers between devices: 37.1 us -> 27.8 us
  Pallas kernels: 8.06 us -> 11 us
  local copies, waits for them, and re-layouts: 3.58 us -> 0.72 us
    all_to_all x1 -> x2, blocking collectives: 18.9 us -> 29.6 us  [the longest x1 19.3 us: local(): lax.all_to_all(product.reshape(8, ROWS, B), NAMES, 0, 0, axis_index_group...]
    ppermute x2, waiting for transfers between devices: 13.8 us -> 4.66 us  [the longest x1 4.66 us: local(): come = lax.ppermute(send, NAMES, pairs(3))]
    all_to_all x2, starting transfers between devices: 19.7 us -> 10.8 us  [the longest x1 6.93 us: local(): parts = lax.all_to_all(copies, 'z', 0, 0)]
    pallas_call x5 -> x8, Pallas kernels: 8.06 us -> 11 us  [call(): pl.pallas_call(kernel, out_shape=shapes, in_specs=specs or [VMEM] * len(o...]
    unnamed x8 -> x0, local copies, waits for them, and re-layouts: 2.86 us -> none
    ppermute x1, waiting for transfers between devices: 1.11 us -> 0.13 us  [local(): other = lax.ppermute(slab, 'core', [(0, 1), (1, 0)])]
  transfers between devices with their start and end apart: 5 -> 5, of which waited for: 5 -> 4; matrix products, arithmetic and copies ran while one was open for 0% -> 0% of each run, Pallas kernels for 1% -> 9%
where the time goes in v3:
time: 79.4 us; the launch traced here: 78.9 us
  blocking collectives  29.6 us (37%)
  starting transfers between devices  27.8 us (35%)
  Pallas kernels  11 us (14%)
  waiting for transfers between devices  9.67 us (12%)
    all_to_all x1, blocking collectives, local(): lax.all_to_all(product.reshape(8, ROWS, B), NAMES, 0, 0, axis_index_group...  19.3 us
    pallas_call x8, Pallas kernels, call(): pl.pallas_call(kernel, out_shape=shapes, in_specs=specs or [VMEM] * len(o...  11 us
    all_to_all x1, blocking collectives, local(): parts = lax.all_to_all(packed.reshape(SHARDS, PACKED, LANES), PLANE, 0, 0)  10.3 us
    ppermute x1, starting transfers between devices, local(): other = lax.ppermute(slab, 'core', [(0, 1), (1, 0)])  8.79 us
    all_to_all x1, starting transfers between devices, local(): parts = lax.all_to_all(copies, 'z', 0, 0)  6.93 us
    ppermute x1, waiting for transfers between devices, local(): come = lax.ppermute(send, NAMES, pairs(3))  4.66 us
    ppermute x1, starting transfers between devices, local(): come = lax.ppermute(send, NAMES, pairs(1))  4.16 us
    ppermute x1, starting transfers between devices, local(): come = lax.ppermute(send, NAMES, pairs(3))  4.09 us
  transfers between devices with their start and end apart: 5, of which 4 were waited for; matrix products, arithmetic and copies ran while one was open for 0% of the time, Pallas kernels for 9%

profile of v3, /device:TPU:1, one launch (start us, length us, event | category | flops | bytes accessed | tf_op | source)
XLA Modules:
  0.0 78.9 jit_solution(11302755030553353162)
XLA Ops:
  0.0 1.1 %shard_map.37 = bf16[656,512]{1,0:T(8,128)(2,1)S(1)} custom-call(bf16[512,1024]{1,0:T(8,128)(2,1)} %act_ref.3, s32[1,512]{1,0:T(1,128)} %bitcast.11, bf16[32,4096]{1,0:T(8,128)(2,1)} %grad_ref.3), custom_call_target="tpu_custom_call" | custom-call | bytes 1984512 | tf_op jit(solution)/shard_map/pallas_call | solution.py:41
  1.1 8.8 %collective-permute-start = (bf16[656,512]{1,0:T(8,128)(2,1)S(1)}, bf16[656,512]{1,0:T(8,128)(2,1)S(1)}, u32[]{:S(2)}, u32[]{:S(2)}) collective-permute-start(bf16[656,512]{1,0:T(8,128)(2,1)S(1)} %shard_map.37), channel_id=1, source_target_pairs={{0,4},{4,0},{1,5},{5,1},{2,6},{6,2},{3,7},{7,3},{8,12},{12,8},{9,1... | collective-permute-start | bytes 2015240 | tf_op jit(solution)/shard_map/ppermute | solution.py:177
  9.9 1.6 %shard_map.38.own_ref = f32[3,256,256]{2,1,0:T(8,128)S(1)} custom-call(bf16[512,1024]{1,0:T(8,128)(2,1)} %act_ref.3, s32[1,512]{1,0:T(1,128)} %bitcast.12), custom_call_target="tpu_custom_call" | custom-call | flops 201326592 | bytes 1837056 | tf_op jit(solution)/shard_map/pallas_call | solution.py:41
  11.5 0.1 collective-permute-done.slab_ref
  11.6 0.5 shard_map.39
  12.2 10.3 %all_to_all.20.parts_ref = bf16[8,192,128]{2,1,0:T(8,128)(2,1)S(1)} all-to-all(bf16[8,192,128]{2,1,0:T(8,128)(2,1)S(1)} %bitcast.7), channel_id=1, replica_groups=mesh['z'=8,'yl'=2,'x'=4,'core'=2,'yh'=4] {'yl','x'}, dimensions={0} | all-to-all | bytes 786432 | tf_op jit(solution)/shard_map/all_to_all | solution.py:192
  22.5 0.8 %shard_map.40 = bf16[8,192,128]{2,1,0:T(8,128)(2,1)} custom-call(bf16[8,192,128]{2,1,0:T(8,128)(2,1)S(1)} %all_to_all.20.parts_ref), custom_call_target="tpu_custom_call" | custom-call | bytes 786432 | tf_op jit(solution)/shard_map/pallas_call | solution.py:41
  23.3 6.9 %all-to-all-start.1 = ((bf16[8,192,128]{2,1,0:T(8,128)(2,1)}), bf16[8,192,128]{2,1,0:T(8,128)(2,1)S(1)}, u32[]{:S(2)}, u32[]{:S(2)}) async-start(bf16[8,192,128]{2,1,0:T(8,128)(2,1)} %shard_map.40), calls=%async_computation.1 | async-start | bytes 786432 | tf_op jit(solution)/shard_map/all_to_all | solution.py:194
  30.2 1.0 %shard_map.41 = (bf16[2,2,32,512]{3,2,1,0:T(8,128)(2,1)S(1)}, bf16[2,2,32,512]{3,2,1,0:T(8,128)(2,1)S(1)}) custom-call(bf16[656,512]{1,0:T(8,128)(2,1)S(1)} %collective-permute-done.slab_ref, bf16[32,4096]{1,0:T(8,128)(2,1)} %grad_ref.3), custom_call_target="tpu_custom_call" | custom-call | bytes 1196032 | tf_op jit(solution)/shard_map/pallas_call | solution.py:41
  31.2 4.1 %collective-permute-start.1 = (bf16[2,2,32,512]{3,2,1,0:T(8,128)(2,1)S(1)}, bf16[2,2,32,512]{3,2,1,0:T(8,128)(2,1)S(1)}, u32[]{:S(2)}, u32[]{:S(2)}) collective-permute-start(bf16[2,2,32,512]{3,2,1,0:T(8,128)(2,1)S(1)} %get-tuple-element.11), channel_id=1, source_target_pairs={{0,35},{4,39},{1,34},{5,38},{34,1},{38,5},{35,0},{39,4},{8,43},{12... | collective-permute-start | bytes 393224 | tf_op jit(solution)/shard_map/ppermute | solution.py:190
  35.3 4.7 %collective-permute-done.1.come_ref = bf16[2,2,32,512]{3,2,1,0:T(8,128)(2,1)S(1)} collective-permute-done((bf16[2,2,32,512]{3,2,1,0:T(8,128)(2,1)S(1)}, bf16[2,2,32,512]{3,2,1,0:T(8,128)(2,1)S(1)}, u32[]{:S(2)}, u32[]{:S(2)}) %collective-permute-start.1) | collective-permute-done | bytes 131104 | tf_op jit(solution)/shard_map/ppermute | solution.py:190
  40.0 2.4 %all-to-all-done.1.parts_ref = bf16[8,192,128]{2,1,0:T(8,128)(2,1)S(1)} async-done(((bf16[8,192,128]{2,1,0:T(8,128)(2,1)}), bf16[8,192,128]{2,1,0:T(8,128)(2,1)S(1)}, u32[]{:S(2)}, u32[]{:S(2)}) %all-to-all-start.1) | async-done | bytes 393248 | tf_op jit(solution)/shard_map/all_to_all | solution.py:194
  42.4 0.8 %shard_map.42 = (bf16[8,192,128]{2,1,0:T(8,128)(2,1)}, bf16[2,2,32,512]{3,2,1,0:T(8,128)(2,1)S(1)}, bf16[2,2,32,512]{3,2,1,0:T(8,128)(2,1)S(1)}) custom-call(bf16[8,192,128]{2,1,0:T(8,128)(2,1)S(1)} %all-to-all-done.1.parts_ref, bf16[2,2,32,512]{3,2,1,0:T(8,128)(2,1)S(1)} %get-tuple-element.10.kept_ref, ...), custom_call_target="tpu_custom_call" | custom-call | bytes 1310720 | tf_op jit(solution)/shard_map/pallas_call | solution.py:41
  43.2 3.9 %all-to-all-start.2 = ((bf16[8,192,128]{2,1,0:T(8,128)(2,1)}), bf16[8,192,128]{2,1,0:T(8,128)(2,1)S(1)}, u32[]{:S(2)}, u32[]{:S(2)}) async-start(bf16[8,192,128]{2,1,0:T(8,128)(2,1)} %get-tuple-element.12), calls=%async_computation.2 | async-start | bytes 786432 | tf_op jit(solution)/shard_map/all_to_all | solution.py:197
  47.1 4.2 %collective-permute-start.2 = (bf16[2,2,32,512]{3,2,1,0:T(8,128)(2,1)S(1)}, bf16[2,2,32,512]{3,2,1,0:T(8,128)(2,1)S(1)}, u32[]{:S(2)}, u32[]{:S(2)}) collective-permute-start(bf16[2,2,32,512]{3,2,1,0:T(8,128)(2,1)S(1)} %get-tuple-element.14), channel_id=1, source_target_pairs={{0,1},{4,5},{1,0},{5,4},{34,35},{38,39},{35,34},{39,38},{8,9},{12,... | collective-permute-start | bytes 393224 | tf_op jit(solution)/shard_map/ppermute | solution.py:196
  51.3 2.4 %all-to-all-done.2 = bf16[8,192,128]{2,1,0:T(8,128)(2,1)S(1)} async-done(((bf16[8,192,128]{2,1,0:T(8,128)(2,1)}), bf16[8,192,128]{2,1,0:T(8,128)(2,1)S(1)}, u32[]{:S(2)}, u32[]{:S(2)}) %all-to-all-start.2) | async-done | bytes 393248 | tf_op jit(solution)/shard_map/all_to_all | solution.py:197
  53.7 4.9 %shard_map.43.root_ref = bf16[512,512]{1,0:T(8,128)(2,1)S(1)} custom-call(bf16[6,256,128]{2,1,0:T(8,128)(2,1)S(1)} %bitcast.9), custom_call_target="tpu_custom_call" | custom-call | flops 4026531840 | bytes 917504 | tf_op jit(solution)/shard_map/pallas_call | solution.py:41
  58.6 0.0 collective-permute-done.2.come_ref
  58.6 0.3 shard_map.44
  58.9 19.3 %all_to_all.21 = bf16[8,32,512]{2,1,0:T(8,128)(2,1)S(1)} all-to-all(bf16[8,32,512]{2,1,0:T(8,128)(2,1)S(1)} %bitcast.8), channel_id=1, replica_groups={{0,4,1,5,34,38,35,39},{8,12,9,13,42,46,43,47},{16,20,17,21,50,54,51,55}..., dimensions={0} | all-to-all | bytes 524288 | tf_op jit(solution)/shard_map/all_to_all | solution.py:200
  78.2 0.7 copy.5
Async XLA Ops:
  1.1 10.5 %collective-permute-start = (bf16[656,512]{1,0:T(8,128)(2,1)S(1)}, bf16[656,512]{1,0:T(8,128)(2,1)S(1)}, u32[]{:S(2)}, u32[]{:S(2)}) collective-permute-start(bf16[656,512]{1,0:T(8,128)(2,1)S(1)} %shard_map.37), channel_id=1, source_target_pairs={{0,4},{4,0},{1,5},{5,1},{2,6},{6,2},{3,7},{7,3},{8,12},{12,8},{9,1... | collective-permute-start | bytes 2015240 | tf_op jit(solution)/shard_map/ppermute | solution.py:177
  23.3 19.1 %all-to-all-start.1 = ((bf16[8,192,128]{2,1,0:T(8,128)(2,1)}), bf16[8,192,128]{2,1,0:T(8,128)(2,1)S(1)}, u32[]{:S(2)}, u32[]{:S(2)}) async-start(bf16[8,192,128]{2,1,0:T(8,128)(2,1)} %shard_map.40), calls=%async_computation.1 | async-start | bytes 786432 | tf_op jit(solution)/shard_map/all_to_all | solution.py:194
  31.2 8.8 %collective-permute-start.1 = (bf16[2,2,32,512]{3,2,1,0:T(8,128)(2,1)S(1)}, bf16[2,2,32,512]{3,2,1,0:T(8,128)(2,1)S(1)}, u32[]{:S(2)}, u32[]{:S(2)}) collective-permute-start(bf16[2,2,32,512]{3,2,1,0:T(8,128)(2,1)S(1)} %get-tuple-element.11), channel_id=1, source_target_pairs={{0,35},{4,39},{1,34},{5,38},{34,1},{38,5},{35,0},{39,4},{8,43},{12... | collective-permute-start | bytes 393224 | tf_op jit(solution)/shard_map/ppermute | solution.py:190
  43.2 10.5 %all-to-all-start.2 = ((bf16[8,192,128]{2,1,0:T(8,128)(2,1)}), bf16[8,192,128]{2,1,0:T(8,128)(2,1)S(1)}, u32[]{:S(2)}, u32[]{:S(2)}) async-start(bf16[8,192,128]{2,1,0:T(8,128)(2,1)} %get-tuple-element.12), calls=%async_computation.2 | async-start | bytes 786432 | tf_op jit(solution)/shard_map/all_to_all | solution.py:197
  47.1 11.5 %collective-permute-start.2 = (bf16[2,2,32,512]{3,2,1,0:T(8,128)(2,1)S(1)}, bf16[2,2,32,512]{3,2,1,0:T(8,128)(2,1)S(1)}, u32[]{:S(2)}, u32[]{:S(2)}) collective-permute-start(bf16[2,2,32,512]{3,2,1,0:T(8,128)(2,1)S(1)} %get-tuple-element.14), channel_id=1, source_target_pairs={{0,1},{4,5},{1,0},{5,4},{34,35},{38,39},{35,34},{39,38},{8,9},{12,... | collective-permute-start | bytes 393224 | tf_op jit(solution)/shard_map/ppermute | solution.py:196

commit v4 on v3

--- a/solution.py
+++ b/solution.py
@@ -15,7 +15,8 @@
 NAMES = tuple(name for name, _ in AXES)
 PLANE = ("yl", "x")
 SHARDS = 8
-PACKED = 3 * 2 * H // SHARDS
+TRIANGLE = [(row, column) for column in range(4) for row in range(column, 4)]
+PACKED = len(TRIANGLE) * LANES // SHARDS
 ROWS = 32
 TOKENS = 512
 MASK_ROWS = 16
@@ -53,12 +54,14 @@
     return pl.ds(pl.multiple_of(index * size, size), size)
 
 
-def slab_kernel(act_ref, mask_ref, grad_ref, out_ref, mask_held, sems):
+def slab_kernel(act_ref, mask_ref, grad_ref, out_ref, mine_ref, mask_held, sems):
     other = 1 - lax.axis_index("core")
     copies = [pltpu.make_async_copy(act_ref.at[:, at(other)], out_ref.at[pl.ds(0, TOKENS)], sems.at[0])]
     for k in range(4):
         rows = pl.ds(TOKENS + ROWS * k, ROWS)
         copies.append(pltpu.make_async_copy(grad_ref.at[:, at(2 * k + other)], out_ref.at[rows], sems.at[k + 1]))
+        rows = pl.ds(ROWS * k, ROWS)
+        copies.append(pltpu.make_async_copy(grad_ref.at[:, at(2 * k + 1 - other)], mine_ref.at[rows], sems.at[k + 6]))
     copies.insert(0, pltpu.make_async_copy(mask_ref, mask_held, sems.at[5]))
     for copy in copies:
         copy.start()
@@ -93,20 +96,19 @@
 
 def gram_kernel(slab_ref, own_ref, out_ref):
     mask = slab_ref[pl.ds(TOKENS + 4 * ROWS, MASK_ROWS), :][:1]
-    for slot, block in enumerate(triangle(masked(slab_ref[pl.ds(0, TOKENS), :], mask))):
-        block += own_ref[slot]
-        for half in range(2):
-            out_ref[2 * slot + half] = block[:, half * LANES : (half + 1) * LANES].astype(BF)
+    blocks = triangle(masked(slab_ref[pl.ds(0, TOKENS), :], mask))
+    blocks = [block + own_ref[slot] for slot, block in enumerate(blocks)]
+    for piece, (row, column) in enumerate(TRIANGLE):
+        block = blocks[row // 2 + column // 2]
+        row, column = LANES * (row % 2), LANES * (column % 2)
+        out_ref[piece] = block[row : row + LANES, column : column + LANES].astype(BF)
 
 
-def first_kernel(slab_ref, grad_ref, send_ref, keep_ref, held, sem):
-    copy = pltpu.make_async_copy(grad_ref, held, sem)
-    copy.start()
+def first_kernel(slab_ref, mine_ref, send_ref, keep_ref):
     core, upper = lax.axis_index("core"), lax.axis_index("yh") // 2
-    copy.wait()
     for ref, part in ((send_ref, 1 - upper), (keep_ref, upper)):
         for k in range(2):
-            ref[k, core] = held[:, at(2 * (2 * part + k) + core)]
+            ref[k, core] = mine_ref[at(2 * part + k, ROWS), :]
             ref[k, 1 - core] = slab_ref[pl.ds(pl.multiple_of(TOKENS + ROWS * (2 * part + k), ROWS), ROWS), :]
 
 
@@ -127,35 +129,25 @@
         ref[1 - upper] = come_ref[part]
 
 
-def split(array):
-    high = array.astype(BF)
-    return high, (array - high.astype(F32)).astype(BF)
-
-
-def dot3(left, right):
-    one = lambda a, b: jnp.dot(a, b, preferred_element_type=F32)
-    return one(left[0], right[0]) + (one(left[0], right[1]) + one(left[1], right[0]))
-
-
 def root_kernel(gram_ref, out_ref):
-    packed = [gram_ref[piece].astype(F32) for piece in range(6)]
-    first, cross, last = [jnp.concatenate(packed[2 * k : 2 * k + 2], axis=1) for k in range(3)]
+    pieces = {place: gram_ref[piece].astype(F32) for piece, place in enumerate(TRIANGLE)}
+    entry = lambda row, column: pieces[row, column] if row >= column else pieces[column, row].T
     gram = jnp.concatenate(
-        [jnp.concatenate([first, cross.T], axis=1), jnp.concatenate([cross, last], axis=1)], axis=0
+        [jnp.concatenate([entry(row, column) for column in range(4)], axis=1) for row in range(4)], axis=0
     )
     row = lax.broadcasted_iota(jnp.int32, (B, B), 0)
     column = lax.broadcasted_iota(jnp.int32, (B, B), 1)
     identity = jnp.where(row == column, 1.0, 0.0).astype(F32)
     damped = gram * (1.0 / 65536) + DAMPING * identity
     norm = jnp.max(jnp.sum(jnp.abs(damped), axis=1, keepdims=True), axis=0, keepdims=True)
-    y = damped / norm
-    ys = split(y)
-    square = dot3(ys, ys)
-    squares = split(square)
-    z = 2.25 * identity - 2.4375 * y + 1.6875 * square + dot3(squares, split(0.0625 * square - 0.5625 * y))
-    zs = split(z)
-    root = 1.5 * z - 0.5 * dot3(split(dot3(zs, zs)), split(dot3(ys, zs)))
-    out_ref[...] = (root / jnp.sqrt(norm)).astype(BF)
+    dot = lambda left, right: jnp.dot(left, right, preferred_element_type=F32)
+    y = damped * (1.0 / norm)
+    near = y.astype(BF)
+    square = dot(near, near)
+    z = 2.25 * identity - 2.4375 * y + 1.6875 * square + dot(square.astype(BF), (0.0625 * square - 0.5625 * y).astype(BF))
+    close = z.astype(BF)
+    root = 1.5 * z - 0.5 * dot(dot(close, close).astype(BF), dot(near, close).astype(BF))
+    out_ref[...] = (root * (1.0 / jnp.sqrt(norm))).astype(BF)
 
 
 def apply_kernel(root_ref, kept_ref, come_ref, out_ref):
@@ -171,8 +163,8 @@
     activations = pltpu.with_memory_space_constraint(activations, pltpu.HBM)
     gradient = pltpu.with_memory_space_constraint(gradient, pltpu.HBM)
     dma = pltpu.SemaphoreType.DMA
-    (slab,) = call(
-        slab_kernel, [((SLAB, B), BF)], (activations, mask, gradient), [HBM] * 3, [pltpu.VMEM((1, TOKENS), jnp.int32), dma((6,))]
+    slab, mine = call(
+        slab_kernel, [((SLAB, B), BF), ((4 * ROWS, B), BF)], (activations, mask, gradient), [HBM] * 3, [pltpu.VMEM((1, TOKENS), jnp.int32), dma((10,))]
     )
     other = lax.ppermute(slab, "core", [(0, 1), (1, 0)])
     (own,) = call(
@@ -184,18 +176,16 @@
         flops=6 * TOKENS * H * H,
     )
     half = ((2, 2, ROWS, B), BF)
-    send, kept = call(
-        first_kernel, [half, half], (other, gradient), [VMEM, HBM], [pltpu.VMEM((ROWS, 8 * B), BF), dma]
-    )
+    send, kept = call(first_kernel, [half, half], (other, mine))
     come = lax.ppermute(send, NAMES, pairs(3))
-    (packed,) = call(gram_kernel, [((6, H, LANES), BF)], (other, own), flops=6 * TOKENS * H * H)
+    (packed,) = call(gram_kernel, [((len(TRIANGLE), LANES, LANES), BF)], (other, own), flops=6 * TOKENS * H * H)
     parts = lax.all_to_all(packed.reshape(SHARDS, PACKED, LANES), PLANE, 0, 0)
     (copies,) = call(spread, [(parts.shape, BF)], (parts,))
     parts = lax.all_to_all(copies, "z", 0, 0)
     copies, send, kept = call(sum_kernel, [(parts.shape, BF), half, half], (parts, kept, come))
     come = lax.ppermute(send, NAMES, pairs(1))
-    packed = lax.all_to_all(copies, PLANE, 0, 0).reshape(6, H, LANES)
-    (root,) = call(root_kernel, [((B, B), BF)], (packed,), flops=2 * 15 * B * B * B)
+    packed = lax.all_to_all(copies, PLANE, 0, 0).reshape(len(TRIANGLE), LANES, LANES)
+    (root,) = call(root_kernel, [((B, B), BF)], (packed,), flops=2 * 5 * B * B * B)
     (product,) = call(apply_kernel, [((2, 2, 2 * ROWS, B), BF)], (root, kept, come), flops=2 * 8 * ROWS * B * B)
     product = lax.all_to_all(product.reshape(8, ROWS, B), NAMES, 0, 0, axis_index_groups=groups())
     return product.transpose(1, 0, 2).reshape(ROWS, 8 * B)

time: 79.4 us -> 74.3 us (0.936)
  Pallas kernels: 11 us -> 7.22 us
    pallas_call x8, Pallas kernels: 11 us -> 7.22 us  [call(): pl.pallas_call(kernel, out_shape=shapes, in_specs=specs or [VMEM] * len(o...]
  transfers between devices with their start and end apart: 5 -> 5, of which waited for: 4 -> 4; matrix products, arithmetic and copies ran while one was open for 0% -> 0% of each run, Pallas kernels for 9% -> 5%
where the time goes in v4:
time: 74.3 us; the launch traced here: 73.8 us
  blocking collectives  29.2 us (39%)
  starting transfers between devices  27.4 us (37%)
  waiting for transfers between devices  9.18 us (12%)
  Pallas kernels  7.22 us (10%)
    all_to_all x1, blocking collectives, local(): lax.all_to_all(product.reshape(8, ROWS, B), NAMES, 0, 0, axis_index_group...  19.3 us
    all_to_all x1, blocking collectives, local(): parts = lax.all_to_all(packed.reshape(SHARDS, PACKED, LANES), PLANE, 0, 0)  9.93 us
    ppermute x1, starting transfers between devices, local(): other = lax.ppermute(slab, 'core', [(0, 1), (1, 0)])  8.79 us
    pallas_call x8, Pallas kernels, call(): pl.pallas_call(kernel, out_shape=shapes, in_specs=specs or [VMEM] * len(o...  7.22 us
    all_to_all x1, starting transfers between devices, local(): parts = lax.all_to_all(copies, 'z', 0, 0)  6.92 us
    ppermute x1, waiting for transfers between devices, local(): come = lax.ppermute(send, NAMES, pairs(3))  4.85 us
    ppermute x1, starting transfers between devices, local(): come = lax.ppermute(send, NAMES, pairs(1))  4.21 us
    ppermute x1, starting transfers between devices, local(): come = lax.ppermute(send, NAMES, pairs(3))  4.07 us
  transfers between devices with their start and end apart: 5, of which 4 were waited for; matrix products, arithmetic and copies ran while one was open for 0% of the time, Pallas kernels for 5%

profile of v4, /device:TPU:1, one launch (start us, length us, event | category | flops | bytes accessed | tf_op | source)
XLA Modules:
  0.0 73.8 jit_solution(5452780747551533814)
XLA Ops:
  0.0 1.2 %shard_map.37 = (bf16[656,512]{1,0:T(8,128)(2,1)S(1)}, bf16[128,512]{1,0:T(8,128)(2,1)S(1)}) custom-call(bf16[512,1024]{1,0:T(8,128)(2,1)} %act_ref.3, s32[1,512]{1,0:T(1,128)} %bitcast.11, bf16[32,4096]{1,0:T(8,128)(2,1)} %grad_ref.1), custom_call_target="tpu_custom_call" | custom-call | bytes 2115584 | tf_op jit(solution)/shard_map/pallas_call | solution.py:42
  1.2 8.8 %collective-permute-start = (bf16[656,512]{1,0:T(8,128)(2,1)S(1)}, bf16[656,512]{1,0:T(8,128)(2,1)S(1)}, u32[]{:S(2)}, u32[]{:S(2)}) collective-permute-start(bf16[656,512]{1,0:T(8,128)(2,1)S(1)} %get-tuple-element.12), channel_id=1, source_target_pairs={{0,4},{4,0},{1,5},{5,1},{2,6},{6,2},{3,7},{7,3},{8,12},{12,8},{9,1... | collective-permute-start | bytes 2015240 | tf_op jit(solution)/shard_map/ppermute | solution.py:169
  10.0 1.6 %shard_map.38.own_ref = f32[3,256,256]{2,1,0:T(8,128)S(1)} custom-call(bf16[512,1024]{1,0:T(8,128)(2,1)} %act_ref.3, s32[1,512]{1,0:T(1,128)} %bitcast.12), custom_call_target="tpu_custom_call" | custom-call | flops 201326592 | bytes 1837056 | tf_op jit(solution)/shard_map/pallas_call | solution.py:42
  11.6 0.1 collective-permute-done.slab_ref
  11.7 0.5 shard_map.39
  12.2 9.9 %all_to_all.20.parts_ref = bf16[8,160,128]{2,1,0:T(8,128)(2,1)S(1)} all-to-all(bf16[8,160,128]{2,1,0:T(8,128)(2,1)S(1)} %bitcast.7), channel_id=1, replica_groups=mesh['z'=8,'yl'=2,'x'=4,'core'=2,'yh'=4] {'yl','x'}, dimensions={0} | all-to-all | bytes 655360 | tf_op jit(solution)/shard_map/all_to_all | solution.py:182
  22.1 0.8 %shard_map.40 = bf16[8,160,128]{2,1,0:T(8,128)(2,1)} custom-call(bf16[8,160,128]{2,1,0:T(8,128)(2,1)S(1)} %all_to_all.20.parts_ref), custom_call_target="tpu_custom_call" | custom-call | bytes 655360 | tf_op jit(solution)/shard_map/pallas_call | solution.py:42
  22.9 6.9 %all-to-all-start.1 = ((bf16[8,160,128]{2,1,0:T(8,128)(2,1)}), bf16[8,160,128]{2,1,0:T(8,128)(2,1)S(1)}, u32[]{:S(2)}, u32[]{:S(2)}) async-start(bf16[8,160,128]{2,1,0:T(8,128)(2,1)} %shard_map.40), calls=%async_computation.1 | async-start | bytes 655360 | tf_op jit(solution)/shard_map/all_to_all | solution.py:184
  29.8 4.1 %collective-permute-start.1 = (bf16[2,2,32,512]{3,2,1,0:T(8,128)(2,1)S(1)}, bf16[2,2,32,512]{3,2,1,0:T(8,128)(2,1)S(1)}, u32[]{:S(2)}, u32[]{:S(2)}) collective-permute-start(bf16[2,2,32,512]{3,2,1,0:T(8,128)(2,1)S(1)} %get-tuple-element.15), channel_id=1, source_target_pairs={{0,35},{4,39},{1,34},{5,38},{34,1},{38,5},{35,0},{39,4},{8,43},{12... | collective-permute-start | bytes 393224 | tf_op jit(solution)/shard_map/ppermute | solution.py:180
  33.9 4.8 %collective-permute-done.1.come_ref = bf16[2,2,32,512]{3,2,1,0:T(8,128)(2,1)S(1)} collective-permute-done((bf16[2,2,32,512]{3,2,1,0:T(8,128)(2,1)S(1)}, bf16[2,2,32,512]{3,2,1,0:T(8,128)(2,1)S(1)}, u32[]{:S(2)}, u32[]{:S(2)}) %collective-permute-start.1) | collective-permute-done | bytes 131104 | tf_op jit(solution)/shard_map/ppermute | solution.py:180
  38.8 2.1 %all-to-all-done.1.parts_ref = bf16[8,160,128]{2,1,0:T(8,128)(2,1)S(1)} async-done(((bf16[8,160,128]{2,1,0:T(8,128)(2,1)}), bf16[8,160,128]{2,1,0:T(8,128)(2,1)S(1)}, u32[]{:S(2)}, u32[]{:S(2)}) %all-to-all-start.1) | async-done | bytes 327712 | tf_op jit(solution)/shard_map/all_to_all | solution.py:184
  40.9 0.8 %shard_map.42 = (bf16[8,160,128]{2,1,0:T(8,128)(2,1)}, bf16[2,2,32,512]{3,2,1,0:T(8,128)(2,1)S(1)}, bf16[2,2,32,512]{3,2,1,0:T(8,128)(2,1)S(1)}) custom-call(bf16[8,160,128]{2,1,0:T(8,128)(2,1)S(1)} %all-to-all-done.1.parts_ref, bf16[2,2,32,512]{3,2,1,0:T(8,128)(2,1)S(1)} %get-tuple-element.14.kept_ref, ...), custom_call_target="tpu_custom_call" | custom-call | bytes 1179648 | tf_op jit(solution)/shard_map/pallas_call | solution.py:42
  41.7 3.4 %all-to-all-start.2 = ((bf16[8,160,128]{2,1,0:T(8,128)(2,1)}), bf16[8,160,128]{2,1,0:T(8,128)(2,1)S(1)}, u32[]{:S(2)}, u32[]{:S(2)}) async-start(bf16[8,160,128]{2,1,0:T(8,128)(2,1)} %get-tuple-element.16), calls=%async_computation.2 | async-start | bytes 655360 | tf_op jit(solution)/shard_map/all_to_all | solution.py:187
  45.1 4.2 %collective-permute-start.2 = (bf16[2,2,32,512]{3,2,1,0:T(8,128)(2,1)S(1)}, bf16[2,2,32,512]{3,2,1,0:T(8,128)(2,1)S(1)}, u32[]{:S(2)}, u32[]{:S(2)}) collective-permute-start(bf16[2,2,32,512]{3,2,1,0:T(8,128)(2,1)S(1)} %get-tuple-element.18), channel_id=1, source_target_pairs={{0,1},{4,5},{1,0},{5,4},{34,35},{38,39},{35,34},{39,38},{8,9},{12,... | collective-permute-start | bytes 393224 | tf_op jit(solution)/shard_map/ppermute | solution.py:186
  49.4 2.0 %all-to-all-done.2 = bf16[8,160,128]{2,1,0:T(8,128)(2,1)S(1)} async-done(((bf16[8,160,128]{2,1,0:T(8,128)(2,1)}), bf16[8,160,128]{2,1,0:T(8,128)(2,1)S(1)}, u32[]{:S(2)}, u32[]{:S(2)}) %all-to-all-start.2) | async-done | bytes 327712 | tf_op jit(solution)/shard_map/all_to_all | solution.py:187
  51.4 2.1 %shard_map.43.root_ref = bf16[512,512]{1,0:T(8,128)(2,1)S(1)} custom-call(bf16[10,128,128]{2,1,0:T(8,128)(2,1)S(1)} %bitcast.9), custom_call_target="tpu_custom_call" | custom-call | flops 1342177280 | bytes 851968 | tf_op jit(solution)/shard_map/pallas_call | solution.py:42
  53.5 0.0 collective-permute-done.2.come_ref
  53.5 0.3 shard_map.44
  53.8 19.3 %all_to_all.21 = bf16[8,32,512]{2,1,0:T(8,128)(2,1)S(1)} all-to-all(bf16[8,32,512]{2,1,0:T(8,128)(2,1)S(1)} %bitcast.8), channel_id=1, replica_groups={{0,4,1,5,34,38,35,39},{8,12,9,13,42,46,43,47},{16,20,17,21,50,54,51,55}..., dimensions={0} | all-to-all | bytes 524288 | tf_op jit(solution)/shard_map/all_to_all | solution.py:190
  73.1 0.7 copy.5
  (1 shorter events, 0.0 us)
Async XLA Ops:
  1.2 10.5 %collective-permute-start = (bf16[656,512]{1,0:T(8,128)(2,1)S(1)}, bf16[656,512]{1,0:T(8,128)(2,1)S(1)}, u32[]{:S(2)}, u32[]{:S(2)}) collective-permute-start(bf16[656,512]{1,0:T(8,128)(2,1)S(1)} %get-tuple-element.12), channel_id=1, source_target_pairs={{0,4},{4,0},{1,5},{5,1},{2,6},{6,2},{3,7},{7,3},{8,12},{12,8},{9,1... | collective-permute-start | bytes 2015240 | tf_op jit(solution)/shard_map/ppermute | solution.py:169
  22.9 18.0 %all-to-all-start.1 = ((bf16[8,160,128]{2,1,0:T(8,128)(2,1)}), bf16[8,160,128]{2,1,0:T(8,128)(2,1)S(1)}, u32[]{:S(2)}, u32[]{:S(2)}) async-start(bf16[8,160,128]{2,1,0:T(8,128)(2,1)} %shard_map.40), calls=%async_computation.1 | async-start | bytes 655360 | tf_op jit(solution)/shard_map/all_to_all | solution.py:184
  29.8 8.9 %collective-permute-start.1 = (bf16[2,2,32,512]{3,2,1,0:T(8,128)(2,1)S(1)}, bf16[2,2,32,512]{3,2,1,0:T(8,128)(2,1)S(1)}, u32[]{:S(2)}, u32[]{:S(2)}) collective-permute-start(bf16[2,2,32,512]{3,2,1,0:T(8,128)(2,1)S(1)} %get-tuple-element.15), channel_id=1, source_target_pairs={{0,35},{4,39},{1,34},{5,38},{34,1},{38,5},{35,0},{39,4},{8,43},{12... | collective-permute-start | bytes 393224 | tf_op jit(solution)/shard_map/ppermute | solution.py:180
  41.7 9.7 %all-to-all-start.2 = ((bf16[8,160,128]{2,1,0:T(8,128)(2,1)}), bf16[8,160,128]{2,1,0:T(8,128)(2,1)S(1)}, u32[]{:S(2)}, u32[]{:S(2)}) async-start(bf16[8,160,128]{2,1,0:T(8,128)(2,1)} %get-tuple-element.16), calls=%async_computation.2 | async-start | bytes 655360 | tf_op jit(solution)/shard_map/all_to_all | solution.py:187
  45.1 8.4 %collective-permute-start.2 = (bf16[2,2,32,512]{3,2,1,0:T(8,128)(2,1)S(1)}, bf16[2,2,32,512]{3,2,1,0:T(8,128)(2,1)S(1)}, u32[]{:S(2)}, u32[]{:S(2)}) collective-permute-start(bf16[2,2,32,512]{3,2,1,0:T(8,128)(2,1)S(1)} %get-tuple-element.18), channel_id=1, source_target_pairs={{0,1},{4,5},{1,0},{5,4},{34,35},{38,39},{35,34},{39,38},{8,9},{12,... | collective-permute-start | bytes 393224 | tf_op jit(solution)/shard_map/ppermute | solution.py:186

commit v5 on v4

--- a/solution.py
+++ b/solution.py
@@ -1,3 +1,5 @@
+import itertools
+
 import jax
 import jax.numpy as jnp
 from jax import lax
@@ -13,27 +15,45 @@
 F32 = jnp.float32
 AXES = (("z", 8), ("yl", 2), ("x", 4), ("core", 2), ("yh", 4))
 NAMES = tuple(name for name, _ in AXES)
-PLANE = ("yl", "x")
 SHARDS = 8
 TRIANGLE = [(row, column) for column in range(4) for row in range(column, 4)]
 PACKED = len(TRIANGLE) * LANES // SHARDS
 ROWS = 32
 TOKENS = 512
 MASK_ROWS = 16
+ZFIRST = 7
+PFIRST = (1, 2)
+ORDER = (2, 3, 0, 1)
 SLAB = TOKENS + 4 * ROWS + MASK_ROWS
 VMEM_MIB = 16
 VMEM = pl.BlockSpec(memory_space=pltpu.VMEM)
 HBM = pl.BlockSpec(memory_space=pltpu.HBM)
 
 
+def place(z, yl, x, core, yh):
+    return (((z * 2 + yl) * 4 + x) * 2 + core) * 4 + yh
+
+
 def groups():
-    at = lambda z, yl, x, core, yh: (((z * 2 + yl) * 4 + x) * 2 + core) * 4 + yh
     every = [(z, w, x) for z in range(8) for w in range(2) for x in range(4)]
-    return [[at(z, w ^ (yh >> 1), x, core, yh) for yh in range(4) for core in range(2)] for z, w, x in every]
+    return [[place(z, w ^ (yh >> 1), x, core, yh) for yh in ORDER for core in range(2)] for z, w, x in every]
+
+
+def layers():
+    order = (ZFIRST, *[z for z in range(8) if z != ZFIRST])
+    rests = itertools.product(range(2), range(4), range(2), range(4))
+    return [[place(z, *rest) for z in order] for rest in rests]
+
+
+def planes():
+    spots = [(yl ^ PFIRST[0], x ^ PFIRST[1]) for yl in range(2) for x in range(4)]
+    return [[place(z, yl, x, core, yh) for yl, x in spots] for z in range(8) for core in range(2) for yh in range(4)]
 
 
 def pairs(flip):
-    return [(group[2 * yh + core], group[2 * (yh ^ flip) + core]) for group in groups() for yh in range(4) for core in range(2)]
+    spot = {yh: k for k, yh in enumerate(ORDER)}
+    ends = [(2 * spot[yh] + core, 2 * spot[yh ^ flip] + core) for yh in range(4) for core in range(2)]
+    return [(group[source], group[target]) for group in groups() for source, target in ends]
 
 
 def call(kernel, outs, operands, specs=None, scratch=(), flops=0):
@@ -104,14 +124,6 @@
         out_ref[piece] = block[row : row + LANES, column : column + LANES].astype(BF)
 
 
-def first_kernel(slab_ref, mine_ref, send_ref, keep_ref):
-    core, upper = lax.axis_index("core"), lax.axis_index("yh") // 2
-    for ref, part in ((send_ref, 1 - upper), (keep_ref, upper)):
-        for k in range(2):
-            ref[k, core] = mine_ref[at(2 * part + k, ROWS), :]
-            ref[k, 1 - core] = slab_ref[pl.ds(pl.multiple_of(TOKENS + ROWS * (2 * part + k), ROWS), ROWS), :]
-
-
 def spread(parts_ref, out_ref):
     total = parts_ref[0].astype(F32)
     for part in range(1, SHARDS):
@@ -119,6 +131,15 @@
     rounded = total.astype(BF)
     for copy in range(SHARDS):
         out_ref[copy] = rounded
+
+
+def first_sum(parts_ref, slab_ref, mine_ref, out_ref, send_ref, keep_ref):
+    spread(parts_ref, out_ref)
+    core, upper = lax.axis_index("core"), lax.axis_index("yh") // 2
+    for ref, part in ((send_ref, 1 - upper), (keep_ref, upper)):
+        for k in range(2):
+            ref[k, core] = mine_ref[at(2 * part + k, ROWS), :]
+            ref[k, 1 - core] = slab_ref[pl.ds(pl.multiple_of(TOKENS + ROWS * (2 * part + k), ROWS), ROWS), :]
 
 
 def sum_kernel(parts_ref, kept_ref, come_ref, out_ref, send_ref, keep_ref):
@@ -146,7 +167,8 @@
     square = dot(near, near)
     z = 2.25 * identity - 2.4375 * y + 1.6875 * square + dot(square.astype(BF), (0.0625 * square - 0.5625 * y).astype(BF))
     close = z.astype(BF)
-    root = 1.5 * z - 0.5 * dot(dot(close, close).astype(BF), dot(near, close).astype(BF))
+    both = dot(jnp.concatenate([close, near], axis=0), close).astype(BF)
+    root = 1.5 * z - 0.5 * dot(both[:B], both[B:])
     out_ref[...] = (root * (1.0 / jnp.sqrt(norm))).astype(BF)
 
 
@@ -155,7 +177,7 @@
     for ref, other in ((kept_ref, 0), (come_ref, 1)):
         product = jnp.dot(ref[...].reshape(4 * ROWS, B), root_ref[...], preferred_element_type=F32).astype(BF)
         for upper in range(2):
-            out_ref[upper, (turn + upper + other) % 2] = product[2 * ROWS * upper : 2 * ROWS * (upper + 1)]
+            out_ref[1 - upper, (turn + upper + other) % 2] = product[2 * ROWS * upper : 2 * ROWS * (upper + 1)]
 
 
 def local(activations, token_mask, gradient):
@@ -164,7 +186,11 @@
     gradient = pltpu.with_memory_space_constraint(gradient, pltpu.HBM)
     dma = pltpu.SemaphoreType.DMA
     slab, mine = call(
-        slab_kernel, [((SLAB, B), BF), ((4 * ROWS, B), BF)], (activations, mask, gradient), [HBM] * 3, [pltpu.VMEM((1, TOKENS), jnp.int32), dma((10,))]
+        slab_kernel,
+        [((SLAB, B), BF), ((4 * ROWS, B), BF)],
+        (activations, mask, gradient),
+        [HBM] * 3,
+        [pltpu.VMEM((1, TOKENS), jnp.int32), dma((10,))],
     )
     other = lax.ppermute(slab, "core", [(0, 1), (1, 0)])
     (own,) = call(
@@ -176,18 +202,18 @@
         flops=6 * TOKENS * H * H,
     )
     half = ((2, 2, ROWS, B), BF)
-    send, kept = call(first_kernel, [half, half], (other, mine))
+    (packed,) = call(gram_kernel, [((len(TRIANGLE), LANES, LANES), BF)], (other, own), flops=6 * TOKENS * H * H)
+    parts = lax.all_to_all(packed.reshape(SHARDS, PACKED, LANES), NAMES, 0, 0, axis_index_groups=planes())
+    copies, send, kept = call(first_sum, [(parts.shape, BF), half, half], (parts, other, mine))
     come = lax.ppermute(send, NAMES, pairs(3))
-    (packed,) = call(gram_kernel, [((len(TRIANGLE), LANES, LANES), BF)], (other, own), flops=6 * TOKENS * H * H)
-    parts = lax.all_to_all(packed.reshape(SHARDS, PACKED, LANES), PLANE, 0, 0)
-    (copies,) = call(spread, [(parts.shape, BF)], (parts,))
-    parts = lax.all_to_all(copies, "z", 0, 0)
+    parts = lax.all_to_all(copies, NAMES, 0, 0, axis_index_groups=layers())
     copies, send, kept = call(sum_kernel, [(parts.shape, BF), half, half], (parts, kept, come))
     come = lax.ppermute(send, NAMES, pairs(1))
-    packed = lax.all_to_all(copies, PLANE, 0, 0).reshape(len(TRIANGLE), LANES, LANES)
+    packed = lax.all_to_all(copies, NAMES, 0, 0, axis_index_groups=planes()).reshape(len(TRIANGLE), LANES, LANES)
     (root,) = call(root_kernel, [((B, B), BF)], (packed,), flops=2 * 5 * B * B * B)
     (product,) = call(apply_kernel, [((2, 2, 2 * ROWS, B), BF)], (root, kept, come), flops=2 * 8 * ROWS * B * B)
     product = lax.all_to_all(product.reshape(8, ROWS, B), NAMES, 0, 0, axis_index_groups=groups())
+    product = jnp.concatenate([product[4:], product[:4]], axis=0)
     return product.transpose(1, 0, 2).reshape(ROWS, 8 * B)
 
 

time: 74.3 us -> 72.4 us (0.974)
  starting transfers between devices: 27.4 us -> 32 us
  waiting for transfers between devices: 9.18 us -> 5.57 us
  blocking collectives: 29.2 us -> 25.9 us
    all_to_all x2, waiting for transfers between devices: 4.2 us -> 0.01 us  [the longest x1 0.01 us: local(): parts = lax.all_to_all(copies, NAMES, 0, 0, axis_index_groups=layers())]
    all_to_all x2, starting transfers between devices: 10.3 us -> 14.4 us  [the longest x1 8.02 us: local(): parts = lax.all_to_all(copies, NAMES, 0, 0, axis_index_groups=layers())]
    all_to_all x1, blocking collectives: 19.3 us -> 16.1 us  [local(): lax.all_to_all(product.reshape(8, ROWS, B), NAMES, 0, 0, axis_index_group...]
    ppermute x1, waiting for transfers between devices: 0.01 us -> 1.63 us  [local(): come = lax.ppermute(send, NAMES, pairs(1))]
    ppermute x1, waiting for transfers between devices: 4.85 us -> 3.8 us  [local(): come = lax.ppermute(send, NAMES, pairs(3))]
    pallas_call x8 -> x7, Pallas kernels: 7.22 us -> 7.23 us  [call(): pl.pallas_call(kernel, out_shape=shapes, in_specs=specs or [VMEM] * len(o...]
  transfers between devices with their start and end apart: 5 -> 5, of which waited for: 4 -> 3; matrix products, arithmetic and copies ran while one was open for 0% -> 0% of each run, Pallas kernels for 5% -> 5%
where the time goes in v5:
time: 72.4 us; the launch traced here: 71.5 us
  starting transfers between devices  32 us (44%)
  blocking collectives  25.9 us (36%)
  Pallas kernels  7.23 us (10%)
  waiting for transfers between devices  5.57 us (8%)
  local copies, waits for them, and re-layouts  0.74 us (1%)
    all_to_all x1, blocking collectives, local(): lax.all_to_all(product.reshape(8, ROWS, B), NAMES, 0, 0, axis_index_group...  16.1 us
    all_to_all x1, blocking collectives, local(): lax.all_to_all(packed.reshape(SHARDS, PACKED, LANES), NAMES, 0, 0, axis_i...  9.82 us
    ppermute x1, starting transfers between devices, local(): other = lax.ppermute(slab, 'core', [(0, 1), (1, 0)])  8.79 us
    all_to_all x1, starting transfers between devices, local(): parts = lax.all_to_all(copies, NAMES, 0, 0, axis_index_groups=layers())  8.02 us
    pallas_call x7, Pallas kernels, call(): pl.pallas_call(kernel, out_shape=shapes, in_specs=specs or [VMEM] * len(o...  7.23 us
    all_to_all x1, starting transfers between devices, local(): lax.all_to_all(copies, NAMES, 0, 0, axis_index_groups=planes())  6.41 us
    ppermute x1, starting transfers between devices, local(): come = lax.ppermute(send, NAMES, pairs(3))  4.5 us
    ppermute x1, starting transfers between devices, local(): come = lax.ppermute(send, NAMES, pairs(1))  4.26 us
  transfers between devices with their start and end apart: 5, of which 3 were waited for; matrix products, arithmetic and copies ran while one was open for 0% of the time, Pallas kernels for 5%

profile of v5, /device:TPU:1, one launch (start us, length us, event | category | flops | bytes accessed | tf_op | source)
XLA Modules:
  0.0 71.5 jit_solution(7243635818720920732)
XLA Ops:
  0.0 1.2 %shard_map.37 = (bf16[656,512]{1,0:T(8,128)(2,1)S(1)}, bf16[128,512]{1,0:T(8,128)(2,1)S(1)}) custom-call(bf16[512,1024]{1,0:T(8,128)(2,1)} %act_ref.3, s32[1,512]{1,0:T(1,128)} %bitcast.11, bf16[32,4096]{1,0:T(8,128)(2,1)} %grad_ref.1), custom_call_target="tpu_custom_call" | custom-call | bytes 2115584 | tf_op jit(solution)/shard_map/pallas_call | solution.py:62
  1.2 8.8 %collective-permute-start = (bf16[656,512]{1,0:T(8,128)(2,1)S(1)}, bf16[656,512]{1,0:T(8,128)(2,1)S(1)}, u32[]{:S(2)}, u32[]{:S(2)}) collective-permute-start(bf16[656,512]{1,0:T(8,128)(2,1)S(1)} %get-tuple-element.13), channel_id=1, source_target_pairs={{0,4},{4,0},{1,5},{5,1},{2,6},{6,2},{3,7},{7,3},{8,12},{12,8},{9,1... | collective-permute-start | bytes 2015240 | tf_op jit(solution)/shard_map/ppermute | solution.py:195
  10.0 1.6 %shard_map.38.own_ref = f32[3,256,256]{2,1,0:T(8,128)S(1)} custom-call(bf16[512,1024]{1,0:T(8,128)(2,1)} %act_ref.3, s32[1,512]{1,0:T(1,128)} %bitcast.12), custom_call_target="tpu_custom_call" | custom-call | flops 201326592 | bytes 1837056 | tf_op jit(solution)/shard_map/pallas_call | solution.py:62
  11.6 0.1 collective-permute-done.slab_ref
  11.7 0.5 shard_map.39
  12.2 9.8 %all_to_all.20.parts_ref = bf16[8,160,128]{2,1,0:T(8,128)(2,1)S(1)} all-to-all(bf16[8,160,128]{2,1,0:T(8,128)(2,1)S(1)} %bitcast.8), channel_id=1, replica_groups={{48,56,32,40,16,24,0,8},{49,57,33,41,17,25,1,9},{50,58,34,42,18,26,2,10..., dimensions={0} | all-to-all | bytes 655360 | tf_op jit(solution)/shard_map/all_to_all | solution.py:206
  22.0 0.8 %shard_map.40 = (bf16[8,160,128]{2,1,0:T(8,128)(2,1)}, bf16[2,2,32,512]{3,2,1,0:T(8,128)(2,1)S(1)}, bf16[2,2,32,512]{3,2,1,0:T(8,128)(2,1)S(1)}) custom-call(bf16[8,160,128]{2,1,0:T(8,128)(2,1)S(1)} %all_to_all.20.parts_ref, bf16[656,512]{1,0:T(8,128)(2,1)S(1)} %collective-permute-done.slab_ref, bf16[128,512]{1,0:T(8,128)(2,1)S(1)} %get-tuple-element.14.mine_ref), custom_call_target="tpu_custom_call" | custom-call | bytes 1720320 | tf_op jit(solution)/shard_map/pallas_call | solution.py:62
  22.8 8.0 %all-to-all-start.1 = ((bf16[8,160,128]{2,1,0:T(8,128)(2,1)}), bf16[8,160,128]{2,1,0:T(8,128)(2,1)S(1)}, u32[]{:S(2)}, u32[]{:S(2)}) async-start(bf16[8,160,128]{2,1,0:T(8,128)(2,1)} %get-tuple-element.15), calls=%async_computation.1 | async-start | bytes 655360 | tf_op jit(solution)/shard_map/all_to_all | solution.py:209
  30.8 4.5 %collective-permute-start.1 = (bf16[2,2,32,512]{3,2,1,0:T(8,128)(2,1)S(1)}, bf16[2,2,32,512]{3,2,1,0:T(8,128)(2,1)S(1)}, u32[]{:S(2)}, u32[]{:S(2)}) collective-permute-start(bf16[2,2,32,512]{3,2,1,0:T(8,128)(2,1)S(1)} %get-tuple-element.17), channel_id=1, source_target_pairs={{0,35},{4,39},{1,34},{5,38},{34,1},{38,5},{35,0},{39,4},{8,43},{12... | collective-permute-start | bytes 393224 | tf_op jit(solution)/shard_map/ppermute | solution.py:208
  35.3 3.8 %collective-permute-done.1.come_ref = bf16[2,2,32,512]{3,2,1,0:T(8,128)(2,1)S(1)} collective-permute-done((bf16[2,2,32,512]{3,2,1,0:T(8,128)(2,1)S(1)}, bf16[2,2,32,512]{3,2,1,0:T(8,128)(2,1)S(1)}, u32[]{:S(2)}, u32[]{:S(2)}) %collective-permute-start.1) | collective-permute-done | bytes 131104 | tf_op jit(solution)/shard_map/ppermute | solution.py:208
  39.1 0.0 all-to-all-done.1.parts_ref
  39.1 0.8 %shard_map.41 = (bf16[8,160,128]{2,1,0:T(8,128)(2,1)}, bf16[2,2,32,512]{3,2,1,0:T(8,128)(2,1)S(1)}, bf16[2,2,32,512]{3,2,1,0:T(8,128)(2,1)S(1)}) custom-call(bf16[8,160,128]{2,1,0:T(8,128)(2,1)S(1)} %all-to-all-done.1.parts_ref, bf16[2,2,32,512]{3,2,1,0:T(8,128)(2,1)S(1)} %get-tuple-element.16.kept_ref, ...), custom_call_target="tpu_custom_call" | custom-call | bytes 1179648 | tf_op jit(solution)/shard_map/pallas_call | solution.py:62
  39.9 6.4 %all-to-all-start.2 = ((bf16[8,160,128]{2,1,0:T(8,128)(2,1)}), bf16[8,160,128]{2,1,0:T(8,128)(2,1)S(1)}, u32[]{:S(2)}, u32[]{:S(2)}) async-start(bf16[8,160,128]{2,1,0:T(8,128)(2,1)} %get-tuple-element.18), calls=%async_computation.2 | async-start | bytes 655360 | tf_op jit(solution)/shard_map/all_to_all | solution.py:212
  46.3 4.3 %collective-permute-start.2 = (bf16[2,2,32,512]{3,2,1,0:T(8,128)(2,1)S(1)}, bf16[2,2,32,512]{3,2,1,0:T(8,128)(2,1)S(1)}, u32[]{:S(2)}, u32[]{:S(2)}) collective-permute-start(bf16[2,2,32,512]{3,2,1,0:T(8,128)(2,1)S(1)} %get-tuple-element.20), channel_id=1, source_target_pairs={{0,1},{4,5},{1,0},{5,4},{34,35},{38,39},{35,34},{39,38},{8,9},{12,... | collective-permute-start | bytes 393224 | tf_op jit(solution)/shard_map/ppermute | solution.py:211
  50.6 0.0 all-to-all-done.2
  50.6 2.1 %shard_map.42.root_ref = bf16[512,512]{1,0:T(8,128)(2,1)S(1)} custom-call(bf16[10,128,128]{2,1,0:T(8,128)(2,1)S(1)} %bitcast.10), custom_call_target="tpu_custom_call" | custom-call | flops 1342177280 | bytes 851968 | tf_op jit(solution)/shard_map/pallas_call | solution.py:62
  52.7 1.6 %collective-permute-done.2.come_ref = bf16[2,2,32,512]{3,2,1,0:T(8,128)(2,1)S(1)} collective-permute-done((bf16[2,2,32,512]{3,2,1,0:T(8,128)(2,1)S(1)}, bf16[2,2,32,512]{3,2,1,0:T(8,128)(2,1)S(1)}, u32[]{:S(2)}, u32[]{:S(2)}) %collective-permute-start.2) | collective-permute-done | bytes 131104 | tf_op jit(solution)/shard_map/ppermute | solution.py:211
  54.4 0.3 shard_map.43
  54.7 16.1 %all_to_all.21 = bf16[8,32,512]{2,1,0:T(8,128)(2,1)S(1)} all-to-all(bf16[8,32,512]{2,1,0:T(8,128)(2,1)S(1)} %bitcast.9), channel_id=1, replica_groups={{34,38,35,39,0,4,1,5},{42,46,43,47,8,12,9,13},{50,54,51,55,16,20,17,21}..., dimensions={0} | all-to-all | bytes 524288 | tf_op jit(solution)/shard_map/all_to_all | solution.py:215
  70.8 0.7 %copy.5 = bf16[8,4,8,512]{3,2,0,1:T(8,128)(2,1)} copy(bf16[8,4,8,512]{3,2,1,0:T(8,128)(2,1)S(1)} %maximum_bitcast_fusion) | data formatting | bytes 524288 | tf_op jit(solution)/shard_map/reshape | solution.py:217
  (2 shorter events, 0.0 us)
Async XLA Ops:
  1.2 10.5 %collective-permute-start = (bf16[656,512]{1,0:T(8,128)(2,1)S(1)}, bf16[656,512]{1,0:T(8,128)(2,1)S(1)}, u32[]{:S(2)}, u32[]{:S(2)}) collective-permute-start(bf16[656,512]{1,0:T(8,128)(2,1)S(1)} %get-tuple-element.13), channel_id=1, source_target_pairs={{0,4},{4,0},{1,5},{5,1},{2,6},{6,2},{3,7},{7,3},{8,12},{12,8},{9,1... | collective-permute-start | bytes 2015240 | tf_op jit(solution)/shard_map/ppermute | solution.py:195
  22.8 16.3 %all-to-all-start.1 = ((bf16[8,160,128]{2,1,0:T(8,128)(2,1)}), bf16[8,160,128]{2,1,0:T(8,128)(2,1)S(1)}, u32[]{:S(2)}, u32[]{:S(2)}) async-start(bf16[8,160,128]{2,1,0:T(8,128)(2,1)} %get-tuple-element.15), calls=%async_computation.1 | async-start | bytes 655360 | tf_op jit(solution)/shard_map/all_to_all | solution.py:209
  30.8 8.3 %collective-permute-start.1 = (bf16[2,2,32,512]{3,2,1,0:T(8,128)(2,1)S(1)}, bf16[2,2,32,512]{3,2,1,0:T(8,128)(2,1)S(1)}, u32[]{:S(2)}, u32[]{:S(2)}) collective-permute-start(bf16[2,2,32,512]{3,2,1,0:T(8,128)(2,1)S(1)} %get-tuple-element.17), channel_id=1, source_target_pairs={{0,35},{4,39},{1,34},{5,38},{34,1},{38,5},{35,0},{39,4},{8,43},{12... | collective-permute-start | bytes 393224 | tf_op jit(solution)/shard_map/ppermute | solution.py:208
  39.9 10.7 %all-to-all-start.2 = ((bf16[8,160,128]{2,1,0:T(8,128)(2,1)}), bf16[8,160,128]{2,1,0:T(8,128)(2,1)S(1)}, u32[]{:S(2)}, u32[]{:S(2)}) async-start(bf16[8,160,128]{2,1,0:T(8,128)(2,1)} %get-tuple-element.18), calls=%async_computation.2 | async-start | bytes 655360 | tf_op jit(solution)/shard_map/all_to_all | solution.py:212
  46.3 8.0 %collective-permute-start.2 = (bf16[2,2,32,512]{3,2,1,0:T(8,128)(2,1)S(1)}, bf16[2,2,32,512]{3,2,1,0:T(8,128)(2,1)S(1)}, u32[]{:S(2)}, u32[]{:S(2)}) collective-permute-start(bf16[2,2,32,512]{3,2,1,0:T(8,128)(2,1)S(1)} %get-tuple-element.20), channel_id=1, source_target_pairs={{0,1},{4,5},{1,0},{5,4},{34,35},{38,39},{35,34},{39,38},{8,9},{12,... | collective-permute-start | bytes 393224 | tf_op jit(solution)/shard_map/ppermute | solution.py:211

commit v6 on v5

--- a/solution.py
+++ b/solution.py
@@ -21,9 +21,10 @@
 ROWS = 32
 TOKENS = 512
 MASK_ROWS = 16
-ZFIRST = 7
-PFIRST = (1, 2)
-ORDER = (2, 3, 0, 1)
+ZFIRST = 6
+SCATTER = 6
+GATHER = 1
+RETURN = 2
 SLAB = TOKENS + 4 * ROWS + MASK_ROWS
 VMEM_MIB = 16
 VMEM = pl.BlockSpec(memory_space=pltpu.VMEM)
@@ -35,8 +36,9 @@
 
 
 def groups():
+    orders = [k ^ RETURN for k in range(4)]
     every = [(z, w, x) for z in range(8) for w in range(2) for x in range(4)]
-    return [[place(z, w ^ (yh >> 1), x, core, yh) for yh in ORDER for core in range(2)] for z, w, x in every]
+    return [[place(z, w ^ (yh >> 1), x, core, yh) for yh in orders for core in range(2)] for z, w, x in every]
 
 
 def layers():
@@ -45,14 +47,13 @@
     return [[place(z, *rest) for z in order] for rest in rests]
 
 
-def planes():
-    spots = [(yl ^ PFIRST[0], x ^ PFIRST[1]) for yl in range(2) for x in range(4)]
+def planes(first):
+    spots = [divmod(k ^ first, 4) for k in range(SHARDS)]
     return [[place(z, yl, x, core, yh) for yl, x in spots] for z in range(8) for core in range(2) for yh in range(4)]
 
 
 def pairs(flip):
-    spot = {yh: k for k, yh in enumerate(ORDER)}
-    ends = [(2 * spot[yh] + core, 2 * spot[yh ^ flip] + core) for yh in range(4) for core in range(2)]
+    ends = [(2 * yh + core, 2 * (yh ^ flip) + core) for yh in range(4) for core in range(2)]
     return [(group[source], group[target]) for group in groups() for source, target in ends]
 
 
@@ -151,7 +152,9 @@
 
 
 def root_kernel(gram_ref, out_ref):
-    pieces = {place: gram_ref[piece].astype(F32) for piece, place in enumerate(TRIANGLE)}
+    shards = [gram_ref[spot ^ SCATTER ^ GATHER] for spot in range(SHARDS)]
+    packed = jnp.concatenate(shards, axis=0).astype(F32)
+    pieces = {spot: packed[LANES * piece : LANES * (piece + 1)] for piece, spot in enumerate(TRIANGLE)}
     entry = lambda row, column: pieces[row, column] if row >= column else pieces[column, row].T
     gram = jnp.concatenate(
         [jnp.concatenate([entry(row, column) for column in range(4)], axis=1) for row in range(4)], axis=0
@@ -177,7 +180,7 @@
     for ref, other in ((kept_ref, 0), (come_ref, 1)):
         product = jnp.dot(ref[...].reshape(4 * ROWS, B), root_ref[...], preferred_element_type=F32).astype(BF)
         for upper in range(2):
-            out_ref[1 - upper, (turn + upper + other) % 2] = product[2 * ROWS * upper : 2 * ROWS * (upper + 1)]
+            out_ref[upper ^ (RETURN >> 1), (turn + upper + other + RETURN) % 2] = product[2 * ROWS * upper : 2 * ROWS * (upper + 1)]
 
 
 def local(activations, token_mask, gradient):
@@ -203,17 +206,17 @@
     )
     half = ((2, 2, ROWS, B), BF)
     (packed,) = call(gram_kernel, [((len(TRIANGLE), LANES, LANES), BF)], (other, own), flops=6 * TOKENS * H * H)
-    parts = lax.all_to_all(packed.reshape(SHARDS, PACKED, LANES), NAMES, 0, 0, axis_index_groups=planes())
+    parts = lax.all_to_all(packed.reshape(SHARDS, PACKED, LANES), NAMES, 0, 0, axis_index_groups=planes(SCATTER))
     copies, send, kept = call(first_sum, [(parts.shape, BF), half, half], (parts, other, mine))
     come = lax.ppermute(send, NAMES, pairs(3))
     parts = lax.all_to_all(copies, NAMES, 0, 0, axis_index_groups=layers())
     copies, send, kept = call(sum_kernel, [(parts.shape, BF), half, half], (parts, kept, come))
     come = lax.ppermute(send, NAMES, pairs(1))
-    packed = lax.all_to_all(copies, NAMES, 0, 0, axis_index_groups=planes()).reshape(len(TRIANGLE), LANES, LANES)
+    packed = lax.all_to_all(copies, NAMES, 0, 0, axis_index_groups=planes(GATHER))
     (root,) = call(root_kernel, [((B, B), BF)], (packed,), flops=2 * 5 * B * B * B)
     (product,) = call(apply_kernel, [((2, 2, 2 * ROWS, B), BF)], (root, kept, come), flops=2 * 8 * ROWS * B * B)
     product = lax.all_to_all(product.reshape(8, ROWS, B), NAMES, 0, 0, axis_index_groups=groups())
-    product = jnp.concatenate([product[4:], product[:4]], axis=0)
+    product = jnp.concatenate([product[2 * (yh ^ RETURN) :][:2] for yh in range(4)], axis=0)
     return product.transpose(1, 0, 2).reshape(ROWS, 8 * B)
 
 

time: 72.4 us -> 71.3 us (0.985)
  starting transfers between devices: 32 us -> 30 us
    all_to_all x1, starting transfers between devices: 6.41 us -> 4.22 us  [local(): lax.all_to_all(copies, NAMES, 0, 0, axis_index_groups=planes(GATHER))]
  transfers between devices with their start and end apart: 5 -> 5, of which waited for: 3 -> 4; matrix products, arithmetic and copies ran while one was open for 0% -> 0% of each run, Pallas kernels for 5% -> 5%
where the time goes in v6:
time: 71.3 us; the launch traced here: 70.7 us
  starting transfers between devices  30 us (42%)
  blocking collectives  26.5 us (37%)
  Pallas kernels  7.22 us (10%)
  waiting for transfers between devices  6.18 us (9%)
  local copies, waits for them, and re-layouts  0.74 us (1%)
    all_to_all x1, blocking collectives, local(): lax.all_to_all(product.reshape(8, ROWS, B), NAMES, 0, 0, axis_index_group...  16.7 us
    all_to_all x1, blocking collectives, local(): lax.all_to_all(packed.reshape(SHARDS, PACKED, LANES), NAMES, 0, 0, axis_i...  9.82 us
    ppermute x1, starting transfers between devices, local(): other = lax.ppermute(slab, 'core', [(0, 1), (1, 0)])  8.79 us
    all_to_all x1, starting transfers between devices, local(): parts = lax.all_to_all(copies, NAMES, 0, 0, axis_index_groups=layers())  8.01 us
    pallas_call x7, Pallas kernels, call(): pl.pallas_call(kernel, out_shape=shapes, in_specs=specs or [VMEM] * len(o...  7.22 us
    ppermute x1, starting transfers between devices, local(): come = lax.ppermute(send, NAMES, pairs(3))  4.49 us
    ppermute x1, starting transfers between devices, local(): come = lax.ppermute(send, NAMES, pairs(1))  4.46 us
    all_to_all x1, starting transfers between devices, local(): lax.all_to_all(copies, NAMES, 0, 0, axis_index_groups=planes(GATHER))  4.22 us
  transfers between devices with their start and end apart: 5, of which 4 were waited for; matrix products, arithmetic and copies ran while one was open for 0% of the time, Pallas kernels for 5%

profile of v6, /device:TPU:1, one launch (start us, length us, event | category | flops | bytes accessed | tf_op | source)
XLA Modules:
  0.0 70.7 jit_solution(2782750645183289804)
XLA Ops:
  0.0 1.2 %shard_map.37 = (bf16[656,512]{1,0:T(8,128)(2,1)S(1)}, bf16[128,512]{1,0:T(8,128)(2,1)S(1)}) custom-call(bf16[512,1024]{1,0:T(8,128)(2,1)} %act_ref.3, s32[1,512]{1,0:T(1,128)} %bitcast.9, bf16[32,4096]{1,0:T(8,128)(2,1)} %grad_ref.1), custom_call_target="tpu_custom_call" | custom-call | bytes 2115584 | tf_op jit(solution)/shard_map/pallas_call | solution.py:63
  1.2 8.8 %collective-permute-start = (bf16[656,512]{1,0:T(8,128)(2,1)S(1)}, bf16[656,512]{1,0:T(8,128)(2,1)S(1)}, u32[]{:S(2)}, u32[]{:S(2)}) collective-permute-start(bf16[656,512]{1,0:T(8,128)(2,1)S(1)} %get-tuple-element.13), channel_id=1, source_target_pairs={{0,4},{4,0},{1,5},{5,1},{2,6},{6,2},{3,7},{7,3},{8,12},{12,8},{9,1... | collective-permute-start | bytes 2015240 | tf_op jit(solution)/shard_map/ppermute | solution.py:198
  10.0 1.6 %shard_map.38.own_ref = f32[3,256,256]{2,1,0:T(8,128)S(1)} custom-call(bf16[512,1024]{1,0:T(8,128)(2,1)} %act_ref.3, s32[1,512]{1,0:T(1,128)} %bitcast.10), custom_call_target="tpu_custom_call" | custom-call | flops 201326592 | bytes 1837056 | tf_op jit(solution)/shard_map/pallas_call | solution.py:63
  11.6 0.1 collective-permute-done.slab_ref
  11.7 0.5 shard_map.39
  12.2 9.8 %all_to_all.20.parts_ref = bf16[8,160,128]{2,1,0:T(8,128)(2,1)S(1)} all-to-all(bf16[8,160,128]{2,1,0:T(8,128)(2,1)S(1)} %bitcast.7), channel_id=1, replica_groups={{48,56,32,40,16,24,0,8},{49,57,33,41,17,25,1,9},{50,58,34,42,18,26,2,10..., dimensions={0} | all-to-all | bytes 655360 | tf_op jit(solution)/shard_map/all_to_all | solution.py:209
  22.0 0.8 %shard_map.40 = (bf16[8,160,128]{2,1,0:T(8,128)(2,1)}, bf16[2,2,32,512]{3,2,1,0:T(8,128)(2,1)S(1)}, bf16[2,2,32,512]{3,2,1,0:T(8,128)(2,1)S(1)}) custom-call(bf16[8,160,128]{2,1,0:T(8,128)(2,1)S(1)} %all_to_all.20.parts_ref, bf16[656,512]{1,0:T(8,128)(2,1)S(1)} %collective-permute-done.slab_ref, bf16[128,512]{1,0:T(8,128)(2,1)S(1)} %get-tuple-element.14.mine_ref), custom_call_target="tpu_custom_call" | custom-call | bytes 1720320 | tf_op jit(solution)/shard_map/pallas_call | solution.py:63
  22.8 8.0 %all-to-all-start.1 = ((bf16[8,160,128]{2,1,0:T(8,128)(2,1)}), bf16[8,160,128]{2,1,0:T(8,128)(2,1)S(1)}, u32[]{:S(2)}, u32[]{:S(2)}) async-start(bf16[8,160,128]{2,1,0:T(8,128)(2,1)} %get-tuple-element.15), calls=%async_computation.1 | async-start | bytes 655360 | tf_op jit(solution)/shard_map/all_to_all | solution.py:212
  30.8 4.5 %collective-permute-start.1 = (bf16[2,2,32,512]{3,2,1,0:T(8,128)(2,1)S(1)}, bf16[2,2,32,512]{3,2,1,0:T(8,128)(2,1)S(1)}, u32[]{:S(2)}, u32[]{:S(2)}) collective-permute-start(bf16[2,2,32,512]{3,2,1,0:T(8,128)(2,1)S(1)} %get-tuple-element.17), channel_id=1, source_target_pairs={{34,1},{38,5},{35,0},{39,4},{0,35},{4,39},{1,34},{5,38},{42,9},{46... | collective-permute-start | bytes 393224 | tf_op jit(solution)/shard_map/ppermute | solution.py:211
  35.3 4.1 %collective-permute-done.1.come_ref = bf16[2,2,32,512]{3,2,1,0:T(8,128)(2,1)S(1)} collective-permute-done((bf16[2,2,32,512]{3,2,1,0:T(8,128)(2,1)S(1)}, bf16[2,2,32,512]{3,2,1,0:T(8,128)(2,1)S(1)}, u32[]{:S(2)}, u32[]{:S(2)}) %collective-permute-start.1) | collective-permute-done | bytes 131104 | tf_op jit(solution)/shard_map/ppermute | solution.py:211
  39.4 0.0 all-to-all-done.1.parts_ref
  39.4 0.8 %shard_map.41 = (bf16[8,160,128]{2,1,0:T(8,128)(2,1)}, bf16[2,2,32,512]{3,2,1,0:T(8,128)(2,1)S(1)}, bf16[2,2,32,512]{3,2,1,0:T(8,128)(2,1)S(1)}) custom-call(bf16[8,160,128]{2,1,0:T(8,128)(2,1)S(1)} %all-to-all-done.1.parts_ref, bf16[2,2,32,512]{3,2,1,0:T(8,128)(2,1)S(1)} %get-tuple-element.16.kept_ref, ...), custom_call_target="tpu_custom_call" | custom-call | bytes 1179648 | tf_op jit(solution)/shard_map/pallas_call | solution.py:63
  40.2 4.2 %all-to-all-start.2 = ((bf16[8,160,128]{2,1,0:T(8,128)(2,1)}), bf16[8,160,128]{2,1,0:T(8,128)(2,1)S(1)}, u32[]{:S(2)}, u32[]{:S(2)}) async-start(bf16[8,160,128]{2,1,0:T(8,128)(2,1)} %get-tuple-element.18), calls=%async_computation.2 | async-start | bytes 655360 | tf_op jit(solution)/shard_map/all_to_all | solution.py:215
  44.4 4.5 %collective-permute-start.2 = (bf16[2,2,32,512]{3,2,1,0:T(8,128)(2,1)S(1)}, bf16[2,2,32,512]{3,2,1,0:T(8,128)(2,1)S(1)}, u32[]{:S(2)}, u32[]{:S(2)}) collective-permute-start(bf16[2,2,32,512]{3,2,1,0:T(8,128)(2,1)S(1)} %get-tuple-element.20), channel_id=1, source_target_pairs={{34,35},{38,39},{35,34},{39,38},{0,1},{4,5},{1,0},{5,4},{42,43},{4... | collective-permute-start | bytes 393224 | tf_op jit(solution)/shard_map/ppermute | solution.py:214
  48.9 0.7 all-to-all-done.2.gram_ref
  49.6 2.1 %shard_map.42.root_ref = bf16[512,512]{1,0:T(8,128)(2,1)S(1)} custom-call(bf16[8,160,128]{2,1,0:T(8,128)(2,1)S(1)} %all-to-all-done.2.gram_ref), custom_call_target="tpu_custom_call" | custom-call | flops 1342177280 | bytes 851968 | tf_op jit(solution)/shard_map/pallas_call | solution.py:63
  51.7 1.2 %collective-permute-done.2.come_ref = bf16[2,2,32,512]{3,2,1,0:T(8,128)(2,1)S(1)} collective-permute-done((bf16[2,2,32,512]{3,2,1,0:T(8,128)(2,1)S(1)}, bf16[2,2,32,512]{3,2,1,0:T(8,128)(2,1)S(1)}, u32[]{:S(2)}, u32[]{:S(2)}) %collective-permute-start.2) | collective-permute-done | bytes 131104 | tf_op jit(solution)/shard_map/ppermute | solution.py:214
  53.0 0.3 shard_map.43
  53.3 16.7 %all_to_all.21 = bf16[8,32,512]{2,1,0:T(8,128)(2,1)S(1)} all-to-all(bf16[8,32,512]{2,1,0:T(8,128)(2,1)S(1)} %bitcast.8), channel_id=1, replica_groups={{34,38,35,39,0,4,1,5},{42,46,43,47,8,12,9,13},{50,54,51,55,16,20,17,21}..., dimensions={0} | all-to-all | bytes 524288 | tf_op jit(solution)/shard_map/all_to_all | solution.py:218
  70.0 0.7 %copy.5 = bf16[8,4,8,512]{3,2,0,1:T(8,128)(2,1)} copy(bf16[8,4,8,512]{3,2,1,0:T(8,128)(2,1)S(1)} %maximum_bitcast_fusion) | data formatting | bytes 524288 | tf_op jit(solution)/shard_map/reshape | solution.py:220
  (2 shorter events, 0.0 us)
Async XLA Ops:
  1.2 10.5 %collective-permute-start = (bf16[656,512]{1,0:T(8,128)(2,1)S(1)}, bf16[656,512]{1,0:T(8,128)(2,1)S(1)}, u32[]{:S(2)}, u32[]{:S(2)}) collective-permute-start(bf16[656,512]{1,0:T(8,128)(2,1)S(1)} %get-tuple-element.13), channel_id=1, source_target_pairs={{0,4},{4,0},{1,5},{5,1},{2,6},{6,2},{3,7},{7,3},{8,12},{12,8},{9,1... | collective-permute-start | bytes 2015240 | tf_op jit(solution)/shard_map/ppermute | solution.py:198
  22.8 16.6 %all-to-all-start.1 = ((bf16[8,160,128]{2,1,0:T(8,128)(2,1)}), bf16[8,160,128]{2,1,0:T(8,128)(2,1)S(1)}, u32[]{:S(2)}, u32[]{:S(2)}) async-start(bf16[8,160,128]{2,1,0:T(8,128)(2,1)} %get-tuple-element.15), calls=%async_computation.1 | async-start | bytes 655360 | tf_op jit(solution)/shard_map/all_to_all | solution.py:212
  30.8 8.6 %collective-permute-start.1 = (bf16[2,2,32,512]{3,2,1,0:T(8,128)(2,1)S(1)}, bf16[2,2,32,512]{3,2,1,0:T(8,128)(2,1)S(1)}, u32[]{:S(2)}, u32[]{:S(2)}) collective-permute-start(bf16[2,2,32,512]{3,2,1,0:T(8,128)(2,1)S(1)} %get-tuple-element.17), channel_id=1, source_target_pairs={{34,1},{38,5},{35,0},{39,4},{0,35},{4,39},{1,34},{5,38},{42,9},{46... | collective-permute-start | bytes 393224 | tf_op jit(solution)/shard_map/ppermute | solution.py:211
  40.2 9.4 %all-to-all-start.2 = ((bf16[8,160,128]{2,1,0:T(8,128)(2,1)}), bf16[8,160,128]{2,1,0:T(8,128)(2,1)S(1)}, u32[]{:S(2)}, u32[]{:S(2)}) async-start(bf16[8,160,128]{2,1,0:T(8,128)(2,1)} %get-tuple-element.18), calls=%async_computation.2 | async-start | bytes 655360 | tf_op jit(solution)/shard_map/all_to_all | solution.py:215
  44.4 8.5 %collective-permute-start.2 = (bf16[2,2,32,512]{3,2,1,0:T(8,128)(2,1)S(1)}, bf16[2,2,32,512]{3,2,1,0:T(8,128)(2,1)S(1)}, u32[]{:S(2)}, u32[]{:S(2)}) collective-permute-start(bf16[2,2,32,512]{3,2,1,0:T(8,128)(2,1)S(1)} %get-tuple-element.20), channel_id=1, source_target_pairs={{34,35},{38,39},{35,34},{39,38},{0,1},{4,5},{1,0},{5,4},{42,43},{4... | collective-permute-start | bytes 393224 | tf_op jit(solution)/shard_map/ppermute | solution.py:214

commit v7 on v6

--- a/solution.py
+++ b/solution.py
@@ -16,8 +16,10 @@
 AXES = (("z", 8), ("yl", 2), ("x", 4), ("core", 2), ("yh", 4))
 NAMES = tuple(name for name, _ in AXES)
 SHARDS = 8
-TRIANGLE = [(row, column) for column in range(4) for row in range(column, 4)]
-PACKED = len(TRIANGLE) * LANES // SHARDS
+BELOW = [(row, column) for column in range(4) for row in range(column + 1, 4)]
+PIECES = len(BELOW) + 3
+PACKED = PIECES * LANES // SHARDS
+HALF = LANES // 2
 ROWS = 32
 TOKENS = 512
 MASK_ROWS = 16
@@ -119,10 +121,19 @@
     mask = slab_ref[pl.ds(TOKENS + 4 * ROWS, MASK_ROWS), :][:1]
     blocks = triangle(masked(slab_ref[pl.ds(0, TOKENS), :], mask))
     blocks = [block + own_ref[slot] for slot, block in enumerate(blocks)]
-    for piece, (row, column) in enumerate(TRIANGLE):
+    def cut(row, column):
         block = blocks[row // 2 + column // 2]
         row, column = LANES * (row % 2), LANES * (column % 2)
-        out_ref[piece] = block[row : row + LANES, column : column + LANES].astype(BF)
+        return block[row : row + LANES, column : column + LANES]
+
+    for piece, spot in enumerate(BELOW):
+        out_ref[piece] = cut(*spot).astype(BF)
+    left = lax.broadcasted_iota(jnp.int32, (HALF, LANES), 1) < HALF
+    for pair in range(2):
+        first, second = cut(2 * pair, 2 * pair), cut(2 * pair + 1, 2 * pair + 1)
+        shared = jnp.where(left, second[:HALF], first[HALF:])
+        out_ref[len(BELOW) + pair] = jnp.concatenate([first[:HALF], shared], axis=0).astype(BF)
+        out_ref[len(BELOW) + 2, pl.ds(HALF * pair, HALF)] = second[HALF:].astype(BF)
 
 
 def spread(parts_ref, out_ref):
@@ -154,7 +165,16 @@
 def root_kernel(gram_ref, out_ref):
     shards = [gram_ref[spot ^ SCATTER ^ GATHER] for spot in range(SHARDS)]
     packed = jnp.concatenate(shards, axis=0).astype(F32)
-    pieces = {spot: packed[LANES * piece : LANES * (piece + 1)] for piece, spot in enumerate(TRIANGLE)}
+    take = lambda row, count: packed[row : row + count]
+    pieces = {spot: take(LANES * piece, LANES) for piece, spot in enumerate(BELOW)}
+    row = lax.broadcasted_iota(jnp.int32, (LANES, LANES), 0)
+    column = lax.broadcasted_iota(jnp.int32, (LANES, LANES), 1)
+    for pair in range(2):
+        base = LANES * (len(BELOW) + pair)
+        first = take(base, LANES)
+        second = jnp.concatenate([take(base + HALF, HALF), take(LANES * (len(BELOW) + 2) + HALF * pair, HALF)], axis=0)
+        pieces[2 * pair, 2 * pair] = jnp.where((row >= HALF) & (column < HALF), first.T, first)
+        pieces[2 * pair + 1, 2 * pair + 1] = jnp.where((row < HALF) & (column >= HALF), second.T, second)
     entry = lambda row, column: pieces[row, column] if row >= column else pieces[column, row].T
     gram = jnp.concatenate(
         [jnp.concatenate([entry(row, column) for column in range(4)], axis=1) for row in range(4)], axis=0
@@ -205,7 +225,7 @@
         flops=6 * TOKENS * H * H,
     )
     half = ((2, 2, ROWS, B), BF)
-    (packed,) = call(gram_kernel, [((len(TRIANGLE), LANES, LANES), BF)], (other, own), flops=6 * TOKENS * H * H)
+    (packed,) = call(gram_kernel, [((PIECES, LANES, LANES), BF)], (other, own), flops=6 * TOKENS * H * H)
     parts = lax.all_to_all(packed.reshape(SHARDS, PACKED, LANES), NAMES, 0, 0, axis_index_groups=planes(SCATTER))
     copies, send, kept = call(first_sum, [(parts.shape, BF), half, half], (parts, other, mine))
     come = lax.ppermute(send, NAMES, pairs(3))

time: 71.3 us -> 71 us (level)
  blocking collectives: 26.5 us -> 25.4 us
  starting transfers between devices: 30 us -> 30.8 us
    all_to_all x1, blocking collectives: 16.7 us -> 15.8 us  [local(): lax.all_to_all(product.reshape(8, ROWS, B), NAMES, 0, 0, axis_index_group...]
    ppermute x1, starting transfers between devices: 4.46 us -> 5.24 us  [local(): come = lax.ppermute(send, NAMES, pairs(1))]
  transfers between devices with their start and end apart: 5 -> 5, of which waited for: 4 -> 3; matrix products, arithmetic and copies ran while one was open for 0% -> 0% of each run, Pallas kernels for 5% -> 5%
where the time goes in v7:
time: 71 us; the launch traced here: 70.6 us
  starting transfers between devices  30.8 us (43%)
  blocking collectives  25.4 us (36%)
  Pallas kernels  7.21 us (10%)
  waiting for transfers between devices  6.3 us (9%)
  local copies, waits for them, and re-layouts  0.74 us (1%)
    all_to_all x1, blocking collectives, local(): lax.all_to_all(product.reshape(8, ROWS, B), NAMES, 0, 0, axis_index_group...  15.8 us
    all_to_all x1, blocking collectives, local(): lax.all_to_all(packed.reshape(SHARDS, PACKED, LANES), NAMES, 0, 0, axis_i...  9.55 us
    ppermute x1, starting transfers between devices, local(): other = lax.ppermute(slab, 'core', [(0, 1), (1, 0)])  8.79 us
    all_to_all x1, starting transfers between devices, local(): parts = lax.all_to_all(copies, NAMES, 0, 0, axis_index_groups=layers())  7.99 us
    pallas_call x7, Pallas kernels, call(): pl.pallas_call(kernel, out_shape=shapes, in_specs=specs or [VMEM] * len(o...  7.21 us
    ppermute x1, starting transfers between devices, local(): come = lax.ppermute(send, NAMES, pairs(1))  5.24 us
    ppermute x1, starting transfers between devices, local(): come = lax.ppermute(send, NAMES, pairs(3))  4.41 us
    all_to_all x1, starting transfers between devices, local(): lax.all_to_all(copies, NAMES, 0, 0, axis_index_groups=planes(GATHER))  4.38 us
  transfers between devices with their start and end apart: 5, of which 3 were waited for; matrix products, arithmetic and copies ran while one was open for 0% of the time, Pallas kernels for 5%

profile of v7, /device:TPU:1, one launch (start us, length us, event | category | flops | bytes accessed | tf_op | source)
XLA Modules:
  0.0 70.6 jit_solution(6058952769347514326)
XLA Ops:
  0.0 1.2 %shard_map.37 = (bf16[656,512]{1,0:T(8,128)(2,1)S(1)}, bf16[128,512]{1,0:T(8,128)(2,1)S(1)}) custom-call(bf16[512,1024]{1,0:T(8,128)(2,1)} %act_ref.3, s32[1,512]{1,0:T(1,128)} %bitcast.9, bf16[32,4096]{1,0:T(8,128)(2,1)} %grad_ref.1), custom_call_target="tpu_custom_call" | custom-call | bytes 2115584 | tf_op jit(solution)/shard_map/pallas_call | solution.py:65
  1.2 8.8 %collective-permute-start = (bf16[656,512]{1,0:T(8,128)(2,1)S(1)}, bf16[656,512]{1,0:T(8,128)(2,1)S(1)}, u32[]{:S(2)}, u32[]{:S(2)}) collective-permute-start(bf16[656,512]{1,0:T(8,128)(2,1)S(1)} %get-tuple-element.13), channel_id=1, source_target_pairs={{0,4},{4,0},{1,5},{5,1},{2,6},{6,2},{3,7},{7,3},{8,12},{12,8},{9,1... | collective-permute-start | bytes 2015240 | tf_op jit(solution)/shard_map/ppermute | solution.py:218
  10.0 1.6 %shard_map.38.own_ref = f32[3,256,256]{2,1,0:T(8,128)S(1)} custom-call(bf16[512,1024]{1,0:T(8,128)(2,1)} %act_ref.3, s32[1,512]{1,0:T(1,128)} %bitcast.10), custom_call_target="tpu_custom_call" | custom-call | flops 201326592 | bytes 1837056 | tf_op jit(solution)/shard_map/pallas_call | solution.py:65
  11.6 0.1 collective-permute-done.slab_ref
  11.7 0.5 shard_map.39
  12.2 9.6 %all_to_all.20.parts_ref = bf16[8,144,128]{2,1,0:T(8,128)(2,1)S(1)} all-to-all(bf16[8,144,128]{2,1,0:T(8,128)(2,1)S(1)} %bitcast.7), channel_id=1, replica_groups={{48,56,32,40,16,24,0,8},{49,57,33,41,17,25,1,9},{50,58,34,42,18,26,2,10..., dimensions={0} | all-to-all | bytes 589824 | tf_op jit(solution)/shard_map/all_to_all | solution.py:229
  21.8 0.8 %shard_map.40 = (bf16[8,144,128]{2,1,0:T(8,128)(2,1)}, bf16[2,2,32,512]{3,2,1,0:T(8,128)(2,1)S(1)}, bf16[2,2,32,512]{3,2,1,0:T(8,128)(2,1)S(1)}) custom-call(bf16[8,144,128]{2,1,0:T(8,128)(2,1)S(1)} %all_to_all.20.parts_ref, bf16[656,512]{1,0:T(8,128)(2,1)S(1)} %collective-permute-done.slab_ref, bf16[128,512]{1,0:T(8,128)(2,1)S(1)} %get-tuple-element.14.mine_ref), custom_call_target="tpu_custom_call" | custom-call | bytes 1654784 | tf_op jit(solution)/shard_map/pallas_call | solution.py:65
  22.5 8.0 %all-to-all-start.1 = ((bf16[8,144,128]{2,1,0:T(8,128)(2,1)}), bf16[8,144,128]{2,1,0:T(8,128)(2,1)S(1)}, u32[]{:S(2)}, u32[]{:S(2)}) async-start(bf16[8,144,128]{2,1,0:T(8,128)(2,1)} %get-tuple-element.15), calls=%async_computation.1 | async-start | bytes 589824 | tf_op jit(solution)/shard_map/all_to_all | solution.py:232
  30.5 4.4 %collective-permute-start.1 = (bf16[2,2,32,512]{3,2,1,0:T(8,128)(2,1)S(1)}, bf16[2,2,32,512]{3,2,1,0:T(8,128)(2,1)S(1)}, u32[]{:S(2)}, u32[]{:S(2)}) collective-permute-start(bf16[2,2,32,512]{3,2,1,0:T(8,128)(2,1)S(1)} %get-tuple-element.17), channel_id=1, source_target_pairs={{34,1},{38,5},{35,0},{39,4},{0,35},{4,39},{1,34},{5,38},{42,9},{46... | collective-permute-start | bytes 393224 | tf_op jit(solution)/shard_map/ppermute | solution.py:231
  34.9 4.3 %collective-permute-done.1.come_ref = bf16[2,2,32,512]{3,2,1,0:T(8,128)(2,1)S(1)} collective-permute-done((bf16[2,2,32,512]{3,2,1,0:T(8,128)(2,1)S(1)}, bf16[2,2,32,512]{3,2,1,0:T(8,128)(2,1)S(1)}, u32[]{:S(2)}, u32[]{:S(2)}) %collective-permute-start.1) | collective-permute-done | bytes 131104 | tf_op jit(solution)/shard_map/ppermute | solution.py:231
  39.2 0.0 all-to-all-done.1.parts_ref
  39.2 0.8 %shard_map.41 = (bf16[8,144,128]{2,1,0:T(8,128)(2,1)}, bf16[2,2,32,512]{3,2,1,0:T(8,128)(2,1)S(1)}, bf16[2,2,32,512]{3,2,1,0:T(8,128)(2,1)S(1)}) custom-call(bf16[8,144,128]{2,1,0:T(8,128)(2,1)S(1)} %all-to-all-done.1.parts_ref, bf16[2,2,32,512]{3,2,1,0:T(8,128)(2,1)S(1)} %get-tuple-element.16.kept_ref, ...), custom_call_target="tpu_custom_call" | custom-call | bytes 1114112 | tf_op jit(solution)/shard_map/pallas_call | solution.py:65
  40.0 4.4 %all-to-all-start.2 = ((bf16[8,144,128]{2,1,0:T(8,128)(2,1)}), bf16[8,144,128]{2,1,0:T(8,128)(2,1)S(1)}, u32[]{:S(2)}, u32[]{:S(2)}) async-start(bf16[8,144,128]{2,1,0:T(8,128)(2,1)} %get-tuple-element.18), calls=%async_computation.2 | async-start | bytes 589824 | tf_op jit(solution)/shard_map/all_to_all | solution.py:235
  44.3 5.2 %collective-permute-start.2 = (bf16[2,2,32,512]{3,2,1,0:T(8,128)(2,1)S(1)}, bf16[2,2,32,512]{3,2,1,0:T(8,128)(2,1)S(1)}, u32[]{:S(2)}, u32[]{:S(2)}) collective-permute-start(bf16[2,2,32,512]{3,2,1,0:T(8,128)(2,1)S(1)} %get-tuple-element.20), channel_id=1, source_target_pairs={{34,35},{38,39},{35,34},{39,38},{0,1},{4,5},{1,0},{5,4},{42,43},{4... | collective-permute-start | bytes 393224 | tf_op jit(solution)/shard_map/ppermute | solution.py:234
  49.6 0.0 all-to-all-done.2.gram_ref
  49.6 2.1 %shard_map.42.root_ref = bf16[512,512]{1,0:T(8,128)(2,1)S(1)} custom-call(bf16[8,144,128]{2,1,0:T(8,128)(2,1)S(1)} %all-to-all-done.2.gram_ref), custom_call_target="tpu_custom_call" | custom-call | flops 1342177280 | bytes 819200 | tf_op jit(solution)/shard_map/pallas_call | solution.py:65
  51.7 1.9 %collective-permute-done.2.come_ref = bf16[2,2,32,512]{3,2,1,0:T(8,128)(2,1)S(1)} collective-permute-done((bf16[2,2,32,512]{3,2,1,0:T(8,128)(2,1)S(1)}, bf16[2,2,32,512]{3,2,1,0:T(8,128)(2,1)S(1)}, u32[]{:S(2)}, u32[]{:S(2)}) %collective-permute-start.2) | collective-permute-done | bytes 131104 | tf_op jit(solution)/shard_map/ppermute | solution.py:234
  53.6 0.3 shard_map.43
  54.0 15.8 %all_to_all.21 = bf16[8,32,512]{2,1,0:T(8,128)(2,1)S(1)} all-to-all(bf16[8,32,512]{2,1,0:T(8,128)(2,1)S(1)} %bitcast.8), channel_id=1, replica_groups={{34,38,35,39,0,4,1,5},{42,46,43,47,8,12,9,13},{50,54,51,55,16,20,17,21}..., dimensions={0} | all-to-all | bytes 524288 | tf_op jit(solution)/shard_map/all_to_all | solution.py:238
  69.8 0.7 %copy.5 = bf16[8,4,8,512]{3,2,0,1:T(8,128)(2,1)} copy(bf16[8,4,8,512]{3,2,1,0:T(8,128)(2,1)S(1)} %maximum_bitcast_fusion) | data formatting | bytes 524288 | tf_op jit(solution)/shard_map/reshape | solution.py:240
  (2 shorter events, 0.0 us)
Async XLA Ops:
  1.2 10.5 %collective-permute-start = (bf16[656,512]{1,0:T(8,128)(2,1)S(1)}, bf16[656,512]{1,0:T(8,128)(2,1)S(1)}, u32[]{:S(2)}, u32[]{:S(2)}) collective-permute-start(bf16[656,512]{1,0:T(8,128)(2,1)S(1)} %get-tuple-element.13), channel_id=1, source_target_pairs={{0,4},{4,0},{1,5},{5,1},{2,6},{6,2},{3,7},{7,3},{8,12},{12,8},{9,1... | collective-permute-start | bytes 2015240 | tf_op jit(solution)/shard_map/ppermute | solution.py:218
  22.5 16.7 %all-to-all-start.1 = ((bf16[8,144,128]{2,1,0:T(8,128)(2,1)}), bf16[8,144,128]{2,1,0:T(8,128)(2,1)S(1)}, u32[]{:S(2)}, u32[]{:S(2)}) async-start(bf16[8,144,128]{2,1,0:T(8,128)(2,1)} %get-tuple-element.15), calls=%async_computation.1 | async-start | bytes 589824 | tf_op jit(solution)/shard_map/all_to_all | solution.py:232
  30.5 8.7 %collective-permute-start.1 = (bf16[2,2,32,512]{3,2,1,0:T(8,128)(2,1)S(1)}, bf16[2,2,32,512]{3,2,1,0:T(8,128)(2,1)S(1)}, u32[]{:S(2)}, u32[]{:S(2)}) collective-permute-start(bf16[2,2,32,512]{3,2,1,0:T(8,128)(2,1)S(1)} %get-tuple-element.17), channel_id=1, source_target_pairs={{34,1},{38,5},{35,0},{39,4},{0,35},{4,39},{1,34},{5,38},{42,9},{46... | collective-permute-start | bytes 393224 | tf_op jit(solution)/shard_map/ppermute | solution.py:231
  40.0 9.6 %all-to-all-start.2 = ((bf16[8,144,128]{2,1,0:T(8,128)(2,1)}), bf16[8,144,128]{2,1,0:T(8,128)(2,1)S(1)}, u32[]{:S(2)}, u32[]{:S(2)}) async-start(bf16[8,144,128]{2,1,0:T(8,128)(2,1)} %get-tuple-element.18), calls=%async_computation.2 | async-start | bytes 589824 | tf_op jit(solution)/shard_map/all_to_all | solution.py:235
  44.3 9.3 %collective-permute-start.2 = (bf16[2,2,32,512]{3,2,1,0:T(8,128)(2,1)S(1)}, bf16[2,2,32,512]{3,2,1,0:T(8,128)(2,1)S(1)}, u32[]{:S(2)}, u32[]{:S(2)}) collective-permute-start(bf16[2,2,32,512]{3,2,1,0:T(8,128)(2,1)S(1)} %get-tuple-element.20), channel_id=1, source_target_pairs={{34,35},{38,39},{35,34},{39,38},{0,1},{4,5},{1,0},{5,4},{42,43},{4... | collective-permute-start | bytes 393224 | tf_op jit(solution)/shard_map/ppermute | solution.py:234

commit v8 on v7

--- a/solution.py
+++ b/solution.py
@@ -1,5 +1,3 @@
-import itertools
-
 import jax
 import jax.numpy as jnp
 from jax import lax
@@ -23,10 +21,11 @@
 ROWS = 32
 TOKENS = 512
 MASK_ROWS = 16
-ZFIRST = 6
 SCATTER = 6
-GATHER = 1
+GATHER = 4
 RETURN = 2
+FIRST = 3
+SECOND = 1
 SLAB = TOKENS + 4 * ROWS + MASK_ROWS
 VMEM_MIB = 16
 VMEM = pl.BlockSpec(memory_space=pltpu.VMEM)
@@ -41,12 +40,6 @@
     orders = [k ^ RETURN for k in range(4)]
     every = [(z, w, x) for z in range(8) for w in range(2) for x in range(4)]
     return [[place(z, w ^ (yh >> 1), x, core, yh) for yh in orders for core in range(2)] for z, w, x in every]
-
-
-def layers():
-    order = (ZFIRST, *[z for z in range(8) if z != ZFIRST])
-    rests = itertools.product(range(2), range(4), range(2), range(4))
-    return [[place(z, *rest) for z in order] for rest in rests]
 
 
 def planes(first):
@@ -154,12 +147,21 @@
             ref[k, 1 - core] = slab_ref[pl.ds(pl.multiple_of(TOKENS + ROWS * (2 * part + k), ROWS), ROWS), :]
 
 
+def first_sum(parts_ref, slab_ref, mine_ref, out_ref, send_ref, keep_ref):
+    spread(parts_ref, out_ref)
+    core, tensor = lax.axis_index("core"), lax.axis_index("yh")
+    for ref, flip in ((send_ref, FIRST), (keep_ref, 0)):
+        for k in range(2):
+            owner = tensor ^ flip ^ (SECOND * k)
+            ref[k, core] = mine_ref[at(owner, ROWS), :]
+            ref[k, 1 - core] = slab_ref[pl.ds(pl.multiple_of(TOKENS + ROWS * owner, ROWS), ROWS), :]
+
+
 def sum_kernel(parts_ref, kept_ref, come_ref, out_ref, send_ref, keep_ref):
     spread(parts_ref, out_ref)
-    upper, lower = lax.axis_index("yh") // 2, lax.axis_index("yh") % 2
-    for ref, part in ((send_ref, 1 - lower), (keep_ref, lower)):
-        ref[upper] = kept_ref[part]
-        ref[1 - upper] = come_ref[part]
+    for k, ref in enumerate((keep_ref, send_ref)):
+        ref[0] = kept_ref[k]
+        ref[1] = come_ref[k]
 
 
 def root_kernel(gram_ref, out_ref):
@@ -196,11 +198,11 @@
 
 
 def apply_kernel(root_ref, kept_ref, come_ref, out_ref):
-    turn = lax.axis_index("yh") // 2 + lax.axis_index("yh") % 2
-    for ref, other in ((kept_ref, 0), (come_ref, 1)):
+    spot = lax.axis_index("yh") ^ RETURN
+    for ref, flip in ((kept_ref, 0), (come_ref, SECOND)):
         product = jnp.dot(ref[...].reshape(4 * ROWS, B), root_ref[...], preferred_element_type=F32).astype(BF)
-        for upper in range(2):
-            out_ref[upper ^ (RETURN >> 1), (turn + upper + other + RETURN) % 2] = product[2 * ROWS * upper : 2 * ROWS * (upper + 1)]
+        for k in range(2):
+            out_ref[spot ^ flip ^ (FIRST * k)] = product[2 * ROWS * k : 2 * ROWS * (k + 1)]
 
 
 def local(activations, token_mask, gradient):
@@ -228,13 +230,13 @@
     (packed,) = call(gram_kernel, [((PIECES, LANES, LANES), BF)], (other, own), flops=6 * TOKENS * H * H)
     parts = lax.all_to_all(packed.reshape(SHARDS, PACKED, LANES), NAMES, 0, 0, axis_index_groups=planes(SCATTER))
     copies, send, kept = call(first_sum, [(parts.shape, BF), half, half], (parts, other, mine))
-    come = lax.ppermute(send, NAMES, pairs(3))
-    parts = lax.all_to_all(copies, NAMES, 0, 0, axis_index_groups=layers())
+    come = lax.ppermute(send, NAMES, pairs(FIRST))
+    parts = lax.all_to_all(copies, "z", 0, 0)
     copies, send, kept = call(sum_kernel, [(parts.shape, BF), half, half], (parts, kept, come))
-    come = lax.ppermute(send, NAMES, pairs(1))
+    come = lax.ppermute(send, NAMES, pairs(SECOND))
     packed = lax.all_to_all(copies, NAMES, 0, 0, axis_index_groups=planes(GATHER))
     (root,) = call(root_kernel, [((B, B), BF)], (packed,), flops=2 * 5 * B * B * B)
-    (product,) = call(apply_kernel, [((2, 2, 2 * ROWS, B), BF)], (root, kept, come), flops=2 * 8 * ROWS * B * B)
+    (product,) = call(apply_kernel, [((4, 2 * ROWS, B), BF)], (root, kept, come), flops=2 * 8 * ROWS * B * B)
     product = lax.all_to_all(product.reshape(8, ROWS, B), NAMES, 0, 0, axis_index_groups=groups())
     product = jnp.concatenate([product[2 * (yh ^ RETURN) :][:2] for yh in range(4)], axis=0)
     return product.transpose(1, 0, 2).reshape(ROWS, 8 * B)

time: 71 us -> 70.6 us (level)
  starting transfers between devices: 30.8 us -> 27.3 us
  waiting for transfers between devices: 6.3 us -> 8.75 us
    all_to_all x1, waiting for transfers between devices: 0.01 us -> 2.67 us  [local(): parts = lax.all_to_all(copies, 'z', 0, 0)]
    all_to_all x1, starting transfers between devices: 7.99 us -> 5.96 us  [local(): parts = lax.all_to_all(copies, 'z', 0, 0)]
    ppermute x2, waiting for transfers between devices: 6.16 us -> 5.01 us  [the longest x1 4.25 us: local(): come = lax.ppermute(send, NAMES, pairs(FIRST))]
    ppermute x2, starting transfers between devices: 9.65 us -> 8.6 us  [the longest x1 4.42 us: local(): come = lax.ppermute(send, NAMES, pairs(FIRST))]
    all_to_all x1, waiting for transfers between devices: 0.01 us -> 0.95 us  [local(): lax.all_to_all(copies, NAMES, 0, 0, axis_index_groups=planes(GATHER))]
  transfers between devices with their start and end apart: 5 -> 5, of which waited for: 3 -> 5; matrix products, arithmetic and copies ran while one was open for 0% -> 0% of each run, Pallas kernels for 5% -> 5%
where the time goes in v8:
time: 70.6 us; the launch traced here: 69.8 us
  starting transfers between devices  27.3 us (39%)
  blocking collectives  25.6 us (36%)
  waiting for transfers between devices  8.75 us (12%)
  Pallas kernels  7.21 us (10%)
  local copies, waits for them, and re-layouts  0.74 us (1%)
    all_to_all x1, blocking collectives, local(): lax.all_to_all(product.reshape(8, ROWS, B), NAMES, 0, 0, axis_index_group...  16.1 us
    all_to_all x1, blocking collectives, local(): lax.all_to_all(packed.reshape(SHARDS, PACKED, LANES), NAMES, 0, 0, axis_i...  9.55 us
    ppermute x1, starting transfers between devices, local(): other = lax.ppermute(slab, 'core', [(0, 1), (1, 0)])  8.79 us
    pallas_call x7, Pallas kernels, call(): pl.pallas_call(kernel, out_shape=shapes, in_specs=specs or [VMEM] * len(o...  7.21 us
    all_to_all x1, starting transfers between devices, local(): parts = lax.all_to_all(copies, 'z', 0, 0)  5.96 us
    ppermute x1, starting transfers between devices, local(): come = lax.ppermute(send, NAMES, pairs(FIRST))  4.42 us
    ppermute x1, waiting for transfers between devices, local(): come = lax.ppermute(send, NAMES, pairs(FIRST))  4.25 us
    ppermute x1, starting transfers between devices, local(): come = lax.ppermute(send, NAMES, pairs(SECOND))  4.18 us
  transfers between devices with their start and end apart: 5, of which 5 were waited for; matrix products, arithmetic and copies ran while one was open for 0% of the time, Pallas kernels for 5%

profile of v8, /device:TPU:1, one launch (start us, length us, event | category | flops | bytes accessed | tf_op | source)
XLA Modules:
  0.0 69.8 jit_solution(16926221549926360627)
XLA Ops:
  0.0 1.2 %shard_map.37 = (bf16[656,512]{1,0:T(8,128)(2,1)S(1)}, bf16[128,512]{1,0:T(8,128)(2,1)S(1)}) custom-call(bf16[512,1024]{1,0:T(8,128)(2,1)} %act_ref.3, s32[1,512]{1,0:T(1,128)} %bitcast.9, bf16[32,4096]{1,0:T(8,128)(2,1)} %grad_ref.1), custom_call_target="tpu_custom_call" | custom-call | bytes 2115584 | tf_op jit(solution)/shard_map/pallas_call | solution.py:58
  1.2 8.8 %collective-permute-start = (bf16[656,512]{1,0:T(8,128)(2,1)S(1)}, bf16[656,512]{1,0:T(8,128)(2,1)S(1)}, u32[]{:S(2)}, u32[]{:S(2)}) collective-permute-start(bf16[656,512]{1,0:T(8,128)(2,1)S(1)} %get-tuple-element.13), channel_id=1, source_target_pairs={{0,4},{4,0},{1,5},{5,1},{2,6},{6,2},{3,7},{7,3},{8,12},{12,8},{9,1... | collective-permute-start | bytes 2015240 | tf_op jit(solution)/shard_map/ppermute | solution.py:220
  10.0 1.6 %shard_map.38.own_ref = f32[3,256,256]{2,1,0:T(8,128)S(1)} custom-call(bf16[512,1024]{1,0:T(8,128)(2,1)} %act_ref.3, s32[1,512]{1,0:T(1,128)} %bitcast.10), custom_call_target="tpu_custom_call" | custom-call | flops 201326592 | bytes 1837056 | tf_op jit(solution)/shard_map/pallas_call | solution.py:58
  11.6 0.1 collective-permute-done.slab_ref
  11.7 0.5 shard_map.39
  12.2 9.6 %all_to_all.20.parts_ref = bf16[8,144,128]{2,1,0:T(8,128)(2,1)S(1)} all-to-all(bf16[8,144,128]{2,1,0:T(8,128)(2,1)S(1)} %bitcast.7), channel_id=1, replica_groups={{48,56,32,40,16,24,0,8},{49,57,33,41,17,25,1,9},{50,58,34,42,18,26,2,10..., dimensions={0} | all-to-all | bytes 589824 | tf_op jit(solution)/shard_map/all_to_all | solution.py:231
  21.8 0.8 %shard_map.40 = (bf16[8,144,128]{2,1,0:T(8,128)(2,1)}, bf16[2,2,32,512]{3,2,1,0:T(8,128)(2,1)S(1)}, bf16[2,2,32,512]{3,2,1,0:T(8,128)(2,1)S(1)}) custom-call(bf16[8,144,128]{2,1,0:T(8,128)(2,1)S(1)} %all_to_all.20.parts_ref, bf16[656,512]{1,0:T(8,128)(2,1)S(1)} %collective-permute-done.slab_ref, bf16[128,512]{1,0:T(8,128)(2,1)S(1)} %get-tuple-element.14.mine_ref), custom_call_target="tpu_custom_call" | custom-call | bytes 1654784 | tf_op jit(solution)/shard_map/pallas_call | solution.py:58
  22.5 6.0 %all-to-all-start.1 = ((bf16[8,144,128]{2,1,0:T(8,128)(2,1)}), bf16[8,144,128]{2,1,0:T(8,128)(2,1)S(1)}, u32[]{:S(2)}, u32[]{:S(2)}) async-start(bf16[8,144,128]{2,1,0:T(8,128)(2,1)} %get-tuple-element.15), calls=%async_computation.1 | async-start | bytes 589824 | tf_op jit(solution)/shard_map/all_to_all | solution.py:234
  28.5 4.4 %collective-permute-start.1 = (bf16[2,2,32,512]{3,2,1,0:T(8,128)(2,1)S(1)}, bf16[2,2,32,512]{3,2,1,0:T(8,128)(2,1)S(1)}, u32[]{:S(2)}, u32[]{:S(2)}) collective-permute-start(bf16[2,2,32,512]{3,2,1,0:T(8,128)(2,1)S(1)} %get-tuple-element.17), channel_id=1, source_target_pairs={{34,1},{38,5},{35,0},{39,4},{0,35},{4,39},{1,34},{5,38},{42,9},{46... | collective-permute-start | bytes 393224 | tf_op jit(solution)/shard_map/ppermute | solution.py:233
  32.9 4.3 %collective-permute-done.1.come_ref = bf16[2,2,32,512]{3,2,1,0:T(8,128)(2,1)S(1)} collective-permute-done((bf16[2,2,32,512]{3,2,1,0:T(8,128)(2,1)S(1)}, bf16[2,2,32,512]{3,2,1,0:T(8,128)(2,1)S(1)}, u32[]{:S(2)}, u32[]{:S(2)}) %collective-permute-start.1) | collective-permute-done | bytes 131104 | tf_op jit(solution)/shard_map/ppermute | solution.py:233
  37.2 2.7 %all-to-all-done.1.parts_ref = bf16[8,144,128]{2,1,0:T(8,128)(2,1)S(1)} async-done(((bf16[8,144,128]{2,1,0:T(8,128)(2,1)}), bf16[8,144,128]{2,1,0:T(8,128)(2,1)S(1)}, u32[]{:S(2)}, u32[]{:S(2)}) %all-to-all-start.1) | async-done | bytes 294944 | tf_op jit(solution)/shard_map/all_to_all | solution.py:234
  39.8 0.8 %shard_map.41 = (bf16[8,144,128]{2,1,0:T(8,128)(2,1)}, bf16[2,2,32,512]{3,2,1,0:T(8,128)(2,1)S(1)}, bf16[2,2,32,512]{3,2,1,0:T(8,128)(2,1)S(1)}) custom-call(bf16[8,144,128]{2,1,0:T(8,128)(2,1)S(1)} %all-to-all-done.1.parts_ref, bf16[2,2,32,512]{3,2,1,0:T(8,128)(2,1)S(1)} %get-tuple-element.16.kept_ref, ...), custom_call_target="tpu_custom_call" | custom-call | bytes 1114112 | tf_op jit(solution)/shard_map/pallas_call | solution.py:58
  40.6 4.0 %all-to-all-start.2 = ((bf16[8,144,128]{2,1,0:T(8,128)(2,1)}), bf16[8,144,128]{2,1,0:T(8,128)(2,1)S(1)}, u32[]{:S(2)}, u32[]{:S(2)}) async-start(bf16[8,144,128]{2,1,0:T(8,128)(2,1)} %get-tuple-element.18), calls=%async_computation.2 | async-start | bytes 589824 | tf_op jit(solution)/shard_map/all_to_all | solution.py:237
  44.6 4.2 %collective-permute-start.2 = (bf16[2,2,32,512]{3,2,1,0:T(8,128)(2,1)S(1)}, bf16[2,2,32,512]{3,2,1,0:T(8,128)(2,1)S(1)}, u32[]{:S(2)}, u32[]{:S(2)}) collective-permute-start(bf16[2,2,32,512]{3,2,1,0:T(8,128)(2,1)S(1)} %get-tuple-element.20), channel_id=1, source_target_pairs={{34,35},{38,39},{35,34},{39,38},{0,1},{4,5},{1,0},{5,4},{42,43},{4... | collective-permute-start | bytes 393224 | tf_op jit(solution)/shard_map/ppermute | solution.py:236
  48.8 0.9 %all-to-all-done.2.gram_ref = bf16[8,144,128]{2,1,0:T(8,128)(2,1)S(1)} async-done(((bf16[8,144,128]{2,1,0:T(8,128)(2,1)}), bf16[8,144,128]{2,1,0:T(8,128)(2,1)S(1)}, u32[]{:S(2)}, u32[]{:S(2)}) %all-to-all-start.2) | async-done | bytes 294944 | tf_op jit(solution)/shard_map/all_to_all | solution.py:237
  49.7 2.1 %shard_map.42.root_ref = bf16[512,512]{1,0:T(8,128)(2,1)S(1)} custom-call(bf16[8,144,128]{2,1,0:T(8,128)(2,1)S(1)} %all-to-all-done.2.gram_ref), custom_call_target="tpu_custom_call" | custom-call | flops 1342177280 | bytes 819200 | tf_op jit(solution)/shard_map/pallas_call | solution.py:58
  51.9 0.8 %collective-permute-done.2.come_ref = bf16[2,2,32,512]{3,2,1,0:T(8,128)(2,1)S(1)} collective-permute-done((bf16[2,2,32,512]{3,2,1,0:T(8,128)(2,1)S(1)}, bf16[2,2,32,512]{3,2,1,0:T(8,128)(2,1)S(1)}, u32[]{:S(2)}, u32[]{:S(2)}) %collective-permute-start.2) | collective-permute-done | bytes 131104 | tf_op jit(solution)/shard_map/ppermute | solution.py:236
  52.6 0.3 shard_map.43
  52.9 16.1 %all_to_all.21 = bf16[8,32,512]{2,1,0:T(8,128)(2,1)S(1)} all-to-all(bf16[8,32,512]{2,1,0:T(8,128)(2,1)S(1)} %bitcast.8), channel_id=1, replica_groups={{34,38,35,39,0,4,1,5},{42,46,43,47,8,12,9,13},{50,54,51,55,16,20,17,21}..., dimensions={0} | all-to-all | bytes 524288 | tf_op jit(solution)/shard_map/all_to_all | solution.py:240
  69.1 0.7 %copy.5 = bf16[8,4,8,512]{3,2,0,1:T(8,128)(2,1)} copy(bf16[8,4,8,512]{3,2,1,0:T(8,128)(2,1)S(1)} %maximum_bitcast_fusion) | data formatting | bytes 524288 | tf_op jit(solution)/shard_map/reshape | solution.py:242
  (2 shorter events, 0.0 us)
Async XLA Ops:
  1.2 10.5 %collective-permute-start = (bf16[656,512]{1,0:T(8,128)(2,1)S(1)}, bf16[656,512]{1,0:T(8,128)(2,1)S(1)}, u32[]{:S(2)}, u32[]{:S(2)}) collective-permute-start(bf16[656,512]{1,0:T(8,128)(2,1)S(1)} %get-tuple-element.13), channel_id=1, source_target_pairs={{0,4},{4,0},{1,5},{5,1},{2,6},{6,2},{3,7},{7,3},{8,12},{12,8},{9,1... | collective-permute-start | bytes 2015240 | tf_op jit(solution)/shard_map/ppermute | solution.py:220
  22.5 17.3 %all-to-all-start.1 = ((bf16[8,144,128]{2,1,0:T(8,128)(2,1)}), bf16[8,144,128]{2,1,0:T(8,128)(2,1)S(1)}, u32[]{:S(2)}, u32[]{:S(2)}) async-start(bf16[8,144,128]{2,1,0:T(8,128)(2,1)} %get-tuple-element.15), calls=%async_computation.1 | async-start | bytes 589824 | tf_op jit(solution)/shard_map/all_to_all | solution.py:234
  28.5 8.7 %collective-permute-start.1 = (bf16[2,2,32,512]{3,2,1,0:T(8,128)(2,1)S(1)}, bf16[2,2,32,512]{3,2,1,0:T(8,128)(2,1)S(1)}, u32[]{:S(2)}, u32[]{:S(2)}) collective-permute-start(bf16[2,2,32,512]{3,2,1,0:T(8,128)(2,1)S(1)} %get-tuple-element.17), channel_id=1, source_target_pairs={{34,1},{38,5},{35,0},{39,4},{0,35},{4,39},{1,34},{5,38},{42,9},{46... | collective-permute-start | bytes 393224 | tf_op jit(solution)/shard_map/ppermute | solution.py:233
  40.6 9.1 %all-to-all-start.2 = ((bf16[8,144,128]{2,1,0:T(8,128)(2,1)}), bf16[8,144,128]{2,1,0:T(8,128)(2,1)S(1)}, u32[]{:S(2)}, u32[]{:S(2)}) async-start(bf16[8,144,128]{2,1,0:T(8,128)(2,1)} %get-tuple-element.18), calls=%async_computation.2 | async-start | bytes 589824 | tf_op jit(solution)/shard_map/all_to_all | solution.py:237
  44.6 8.0 %collective-permute-start.2 = (bf16[2,2,32,512]{3,2,1,0:T(8,128)(2,1)S(1)}, bf16[2,2,32,512]{3,2,1,0:T(8,128)(2,1)S(1)}, u32[]{:S(2)}, u32[]{:S(2)}) collective-permute-start(bf16[2,2,32,512]{3,2,1,0:T(8,128)(2,1)S(1)} %get-tuple-element.20), channel_id=1, source_target_pairs={{34,35},{38,39},{35,34},{39,38},{0,1},{4,5},{1,0},{5,4},{42,43},{4... | collective-permute-start | bytes 393224 | tf_op jit(solution)/shard_map/ppermute | solution.py:236

commit v9 on v8

--- a/solution.py
+++ b/solution.py
@@ -140,15 +140,6 @@
 
 def first_sum(parts_ref, slab_ref, mine_ref, out_ref, send_ref, keep_ref):
     spread(parts_ref, out_ref)
-    core, upper = lax.axis_index("core"), lax.axis_index("yh") // 2
-    for ref, part in ((send_ref, 1 - upper), (keep_ref, upper)):
-        for k in range(2):
-            ref[k, core] = mine_ref[at(2 * part + k, ROWS), :]
-            ref[k, 1 - core] = slab_ref[pl.ds(pl.multiple_of(TOKENS + ROWS * (2 * part + k), ROWS), ROWS), :]
-
-
-def first_sum(parts_ref, slab_ref, mine_ref, out_ref, send_ref, keep_ref):
-    spread(parts_ref, out_ref)
     core, tensor = lax.axis_index("core"), lax.axis_index("yh")
     for ref, flip in ((send_ref, FIRST), (keep_ref, 0)):
         for k in range(2):
@@ -164,7 +155,7 @@
         ref[1] = come_ref[k]
 
 
-def root_kernel(gram_ref, out_ref):
+def root_kernel(gram_ref, kept_ref, out_ref, product_ref):
     shards = [gram_ref[spot ^ SCATTER ^ GATHER] for spot in range(SHARDS)]
     packed = jnp.concatenate(shards, axis=0).astype(F32)
     take = lambda row, count: packed[row : row + count]
@@ -194,13 +185,15 @@
     close = z.astype(BF)
     both = dot(jnp.concatenate([close, near], axis=0), close).astype(BF)
     root = 1.5 * z - 0.5 * dot(both[:B], both[B:])
-    out_ref[...] = (root * (1.0 / jnp.sqrt(norm))).astype(BF)
-
-
-def apply_kernel(root_ref, kept_ref, come_ref, out_ref):
+    root = (root * (1.0 / jnp.sqrt(norm))).astype(BF)
+    out_ref[...] = root
+    product_ref[...] = dot(kept_ref[...].reshape(4 * ROWS, B), root).astype(BF)
+
+
+def apply_kernel(root_ref, product_ref, come_ref, out_ref):
     spot = lax.axis_index("yh") ^ RETURN
-    for ref, flip in ((kept_ref, 0), (come_ref, SECOND)):
-        product = jnp.dot(ref[...].reshape(4 * ROWS, B), root_ref[...], preferred_element_type=F32).astype(BF)
+    late = jnp.dot(come_ref[...].reshape(4 * ROWS, B), root_ref[...], preferred_element_type=F32).astype(BF)
+    for product, flip in ((product_ref[...], 0), (late, SECOND)):
         for k in range(2):
             out_ref[spot ^ flip ^ (FIRST * k)] = product[2 * ROWS * k : 2 * ROWS * (k + 1)]
 
@@ -235,8 +228,12 @@
     copies, send, kept = call(sum_kernel, [(parts.shape, BF), half, half], (parts, kept, come))
     come = lax.ppermute(send, NAMES, pairs(SECOND))
     packed = lax.all_to_all(copies, NAMES, 0, 0, axis_index_groups=planes(GATHER))
-    (root,) = call(root_kernel, [((B, B), BF)], (packed,), flops=2 * 5 * B * B * B)
-    (product,) = call(apply_kernel, [((4, 2 * ROWS, B), BF)], (root, kept, come), flops=2 * 8 * ROWS * B * B)
+    root, product = call(
+        root_kernel, [((B, B), BF), ((4 * ROWS, B), BF)], (packed, kept), flops=2 * 5 * B * B * B
+    )
+    (product,) = call(
+        apply_kernel, [((4, 2 * ROWS, B), BF)], (root, product, come), flops=2 * 4 * ROWS * B * B
+    )
     product = lax.all_to_all(product.reshape(8, ROWS, B), NAMES, 0, 0, axis_index_groups=groups())
     product = jnp.concatenate([product[2 * (yh ^ RETURN) :][:2] for yh in range(4)], axis=0)
     return product.transpose(1, 0, 2).reshape(ROWS, 8 * B)

time: 70.6 us -> 70.5 us (level)
  transfers between devices with their start and end apart: 5 -> 5, of which waited for: 5 -> 5; matrix products, arithmetic and copies ran while one was open for 0% -> 0% of each run, Pallas kernels for 5% -> 6%
where the time goes in v9:
time: 70.5 us; the launch traced here: 69.9 us
  starting transfers between devices  27.3 us (39%)
  blocking collectives  25.8 us (37%)
  waiting for transfers between devices  8.56 us (12%)
  Pallas kernels  7.31 us (10%)
  local copies, waits for them, and re-layouts  0.74 us (1%)
    all_to_all x1, blocking collectives, local(): lax.all_to_all(product.reshape(8, ROWS, B), NAMES, 0, 0, axis_index_group...  16.3 us
    all_to_all x1, blocking collectives, local(): lax.all_to_all(packed.reshape(SHARDS, PACKED, LANES), NAMES, 0, 0, axis_i...  9.55 us
    ppermute x1, starting transfers between devices, local(): other = lax.ppermute(slab, 'core', [(0, 1), (1, 0)])  8.79 us
    pallas_call x7, Pallas kernels, call(): pl.pallas_call(kernel, out_shape=shapes, in_specs=specs or [VMEM] * len(o...  7.31 us
    all_to_all x1, starting transfers between devices, local(): parts = lax.all_to_all(copies, 'z', 0, 0)  5.96 us
    ppermute x1, starting transfers between devices, local(): come = lax.ppermute(send, NAMES, pairs(FIRST))  4.42 us
    ppermute x1, waiting for transfers between devices, local(): come = lax.ppermute(send, NAMES, pairs(FIRST))  4.25 us
    ppermute x1, starting transfers between devices, local(): come = lax.ppermute(send, NAMES, pairs(SECOND))  4.18 us
  transfers between devices with their start and end apart: 5, of which 5 were waited for; matrix products, arithmetic and copies ran while one was open for 0% of the time, Pallas kernels for 6%

profile of v9, /device:TPU:1, one launch (start us, length us, event | category | flops | bytes accessed | tf_op | source)
XLA Modules:
  0.0 69.9 jit_solution(2190545476376169436)
XLA Ops:
  0.0 1.2 %shard_map.37 = (bf16[656,512]{1,0:T(8,128)(2,1)S(1)}, bf16[128,512]{1,0:T(8,128)(2,1)S(1)}) custom-call(bf16[512,1024]{1,0:T(8,128)(2,1)} %act_ref.3, s32[1,512]{1,0:T(1,128)} %bitcast.9, bf16[32,4096]{1,0:T(8,128)(2,1)} %grad_ref.1), custom_call_target="tpu_custom_call" | custom-call | bytes 2115584 | tf_op jit(solution)/shard_map/pallas_call | solution.py:58
  1.2 8.8 %collective-permute-start = (bf16[656,512]{1,0:T(8,128)(2,1)S(1)}, bf16[656,512]{1,0:T(8,128)(2,1)S(1)}, u32[]{:S(2)}, u32[]{:S(2)}) collective-permute-start(bf16[656,512]{1,0:T(8,128)(2,1)S(1)} %get-tuple-element.15), channel_id=1, source_target_pairs={{0,4},{4,0},{1,5},{5,1},{2,6},{6,2},{3,7},{7,3},{8,12},{12,8},{9,1... | collective-permute-start | bytes 2015240 | tf_op jit(solution)/shard_map/ppermute | solution.py:213
  10.0 1.6 %shard_map.38.own_ref = f32[3,256,256]{2,1,0:T(8,128)S(1)} custom-call(bf16[512,1024]{1,0:T(8,128)(2,1)} %act_ref.3, s32[1,512]{1,0:T(1,128)} %bitcast.10), custom_call_target="tpu_custom_call" | custom-call | flops 201326592 | bytes 1837056 | tf_op jit(solution)/shard_map/pallas_call | solution.py:58
  11.6 0.1 collective-permute-done.slab_ref
  11.7 0.5 shard_map.39
  12.2 9.6 %all_to_all.20.parts_ref = bf16[8,144,128]{2,1,0:T(8,128)(2,1)S(1)} all-to-all(bf16[8,144,128]{2,1,0:T(8,128)(2,1)S(1)} %bitcast.7), channel_id=1, replica_groups={{48,56,32,40,16,24,0,8},{49,57,33,41,17,25,1,9},{50,58,34,42,18,26,2,10..., dimensions={0} | all-to-all | bytes 589824 | tf_op jit(solution)/shard_map/all_to_all | solution.py:224
  21.8 0.8 %shard_map.40 = (bf16[8,144,128]{2,1,0:T(8,128)(2,1)}, bf16[2,2,32,512]{3,2,1,0:T(8,128)(2,1)S(1)}, bf16[2,2,32,512]{3,2,1,0:T(8,128)(2,1)S(1)}) custom-call(bf16[8,144,128]{2,1,0:T(8,128)(2,1)S(1)} %all_to_all.20.parts_ref, bf16[656,512]{1,0:T(8,128)(2,1)S(1)} %collective-permute-done.slab_ref, bf16[128,512]{1,0:T(8,128)(2,1)S(1)} %get-tuple-element.16.mine_ref), custom_call_target="tpu_custom_call" | custom-call | bytes 1654784 | tf_op jit(solution)/shard_map/pallas_call | solution.py:58
  22.5 6.0 %all-to-all-start.1 = ((bf16[8,144,128]{2,1,0:T(8,128)(2,1)}), bf16[8,144,128]{2,1,0:T(8,128)(2,1)S(1)}, u32[]{:S(2)}, u32[]{:S(2)}) async-start(bf16[8,144,128]{2,1,0:T(8,128)(2,1)} %get-tuple-element.17), calls=%async_computation.1 | async-start | bytes 589824 | tf_op jit(solution)/shard_map/all_to_all | solution.py:227
  28.5 4.4 %collective-permute-start.1 = (bf16[2,2,32,512]{3,2,1,0:T(8,128)(2,1)S(1)}, bf16[2,2,32,512]{3,2,1,0:T(8,128)(2,1)S(1)}, u32[]{:S(2)}, u32[]{:S(2)}) collective-permute-start(bf16[2,2,32,512]{3,2,1,0:T(8,128)(2,1)S(1)} %get-tuple-element.19), channel_id=1, source_target_pairs={{34,1},{38,5},{35,0},{39,4},{0,35},{4,39},{1,34},{5,38},{42,9},{46... | collective-permute-start | bytes 393224 | tf_op jit(solution)/shard_map/ppermute | solution.py:226
  32.9 4.3 %collective-permute-done.1.come_ref = bf16[2,2,32,512]{3,2,1,0:T(8,128)(2,1)S(1)} collective-permute-done((bf16[2,2,32,512]{3,2,1,0:T(8,128)(2,1)S(1)}, bf16[2,2,32,512]{3,2,1,0:T(8,128)(2,1)S(1)}, u32[]{:S(2)}, u32[]{:S(2)}) %collective-permute-start.1) | collective-permute-done | bytes 131104 | tf_op jit(solution)/shard_map/ppermute | solution.py:226
  37.2 2.7 %all-to-all-done.1.parts_ref = bf16[8,144,128]{2,1,0:T(8,128)(2,1)S(1)} async-done(((bf16[8,144,128]{2,1,0:T(8,128)(2,1)}), bf16[8,144,128]{2,1,0:T(8,128)(2,1)S(1)}, u32[]{:S(2)}, u32[]{:S(2)}) %all-to-all-start.1) | async-done | bytes 294944 | tf_op jit(solution)/shard_map/all_to_all | solution.py:227
  39.8 0.8 %shard_map.41 = (bf16[8,144,128]{2,1,0:T(8,128)(2,1)}, bf16[2,2,32,512]{3,2,1,0:T(8,128)(2,1)S(1)}, bf16[2,2,32,512]{3,2,1,0:T(8,128)(2,1)S(1)}) custom-call(bf16[8,144,128]{2,1,0:T(8,128)(2,1)S(1)} %all-to-all-done.1.parts_ref, bf16[2,2,32,512]{3,2,1,0:T(8,128)(2,1)S(1)} %get-tuple-element.18.kept_ref, ...), custom_call_target="tpu_custom_call" | custom-call | bytes 1114112 | tf_op jit(solution)/shard_map/pallas_call | solution.py:58
  40.6 4.0 %all-to-all-start.2 = ((bf16[8,144,128]{2,1,0:T(8,128)(2,1)}), bf16[8,144,128]{2,1,0:T(8,128)(2,1)S(1)}, u32[]{:S(2)}, u32[]{:S(2)}) async-start(bf16[8,144,128]{2,1,0:T(8,128)(2,1)} %get-tuple-element.20), calls=%async_computation.2 | async-start | bytes 589824 | tf_op jit(solution)/shard_map/all_to_all | solution.py:230
  44.6 4.2 %collective-permute-start.2 = (bf16[2,2,32,512]{3,2,1,0:T(8,128)(2,1)S(1)}, bf16[2,2,32,512]{3,2,1,0:T(8,128)(2,1)S(1)}, u32[]{:S(2)}, u32[]{:S(2)}) collective-permute-start(bf16[2,2,32,512]{3,2,1,0:T(8,128)(2,1)S(1)} %get-tuple-element.24), channel_id=1, source_target_pairs={{34,35},{38,39},{35,34},{39,38},{0,1},{4,5},{1,0},{5,4},{42,43},{4... | collective-permute-start | bytes 393224 | tf_op jit(solution)/shard_map/ppermute | solution.py:229
  48.8 0.9 %all-to-all-done.2.gram_ref = bf16[8,144,128]{2,1,0:T(8,128)(2,1)S(1)} async-done(((bf16[8,144,128]{2,1,0:T(8,128)(2,1)}), bf16[8,144,128]{2,1,0:T(8,128)(2,1)S(1)}, u32[]{:S(2)}, u32[]{:S(2)}) %all-to-all-start.2) | async-done | bytes 294944 | tf_op jit(solution)/shard_map/all_to_all | solution.py:230
  49.7 2.3 %shard_map.42 = (bf16[512,512]{1,0:T(8,128)(2,1)S(1)}, bf16[128,512]{1,0:T(8,128)(2,1)S(1)}) custom-call(bf16[8,144,128]{2,1,0:T(8,128)(2,1)S(1)} %all-to-all-done.2.gram_ref, bf16[2,2,32,512]{3,2,1,0:T(8,128)(2,1)S(1)} %get-tuple-element.21.kept_ref), custom_call_target="tpu_custom_call" | custom-call | flops 1342177280 | bytes 1081344 | tf_op jit(solution)/shard_map/pallas_call | solution.py:58
  52.0 0.6 collective-permute-done.2.come_ref
  52.6 0.2 shard_map.43
  52.8 16.3 %all_to_all.21 = bf16[8,32,512]{2,1,0:T(8,128)(2,1)S(1)} all-to-all(bf16[8,32,512]{2,1,0:T(8,128)(2,1)S(1)} %bitcast.8), channel_id=1, replica_groups={{34,38,35,39,0,4,1,5},{42,46,43,47,8,12,9,13},{50,54,51,55,16,20,17,21}..., dimensions={0} | all-to-all | bytes 524288 | tf_op jit(solution)/shard_map/all_to_all | solution.py:237
  69.2 0.7 %copy.5 = bf16[8,4,8,512]{3,2,0,1:T(8,128)(2,1)} copy(bf16[8,4,8,512]{3,2,1,0:T(8,128)(2,1)S(1)} %maximum_bitcast_fusion) | data formatting | bytes 524288 | tf_op jit(solution)/shard_map/reshape | solution.py:239
  (2 shorter events, 0.0 us)
Async XLA Ops:
  1.2 10.5 %collective-permute-start = (bf16[656,512]{1,0:T(8,128)(2,1)S(1)}, bf16[656,512]{1,0:T(8,128)(2,1)S(1)}, u32[]{:S(2)}, u32[]{:S(2)}) collective-permute-start(bf16[656,512]{1,0:T(8,128)(2,1)S(1)} %get-tuple-element.15), channel_id=1, source_target_pairs={{0,4},{4,0},{1,5},{5,1},{2,6},{6,2},{3,7},{7,3},{8,12},{12,8},{9,1... | collective-permute-start | bytes 2015240 | tf_op jit(solution)/shard_map/ppermute | solution.py:213
  22.5 17.3 %all-to-all-start.1 = ((bf16[8,144,128]{2,1,0:T(8,128)(2,1)}), bf16[8,144,128]{2,1,0:T(8,128)(2,1)S(1)}, u32[]{:S(2)}, u32[]{:S(2)}) async-start(bf16[8,144,128]{2,1,0:T(8,128)(2,1)} %get-tuple-element.17), calls=%async_computation.1 | async-start | bytes 589824 | tf_op jit(solution)/shard_map/all_to_all | solution.py:227
  28.5 8.7 %collective-permute-start.1 = (bf16[2,2,32,512]{3,2,1,0:T(8,128)(2,1)S(1)}, bf16[2,2,32,512]{3,2,1,0:T(8,128)(2,1)S(1)}, u32[]{:S(2)}, u32[]{:S(2)}) collective-permute-start(bf16[2,2,32,512]{3,2,1,0:T(8,128)(2,1)S(1)} %get-tuple-element.19), channel_id=1, source_target_pairs={{34,1},{38,5},{35,0},{39,4},{0,35},{4,39},{1,34},{5,38},{42,9},{46... | collective-permute-start | bytes 393224 | tf_op jit(solution)/shard_map/ppermute | solution.py:226
  40.6 9.1 %all-to-all-start.2 = ((bf16[8,144,128]{2,1,0:T(8,128)(2,1)}), bf16[8,144,128]{2,1,0:T(8,128)(2,1)S(1)}, u32[]{:S(2)}, u32[]{:S(2)}) async-start(bf16[8,144,128]{2,1,0:T(8,128)(2,1)} %get-tuple-element.20), calls=%async_computation.2 | async-start | bytes 589824 | tf_op jit(solution)/shard_map/all_to_all | solution.py:230
  44.6 8.0 %collective-permute-start.2 = (bf16[2,2,32,512]{3,2,1,0:T(8,128)(2,1)S(1)}, bf16[2,2,32,512]{3,2,1,0:T(8,128)(2,1)S(1)}, u32[]{:S(2)}, u32[]{:S(2)}) collective-permute-start(bf16[2,2,32,512]{3,2,1,0:T(8,128)(2,1)S(1)} %get-tuple-element.24), channel_id=1, source_target_pairs={{34,35},{38,39},{35,34},{39,38},{0,1},{4,5},{1,0},{5,4},{42,43},{4... | collective-permute-start | bytes 393224 | tf_op jit(solution)/shard_map/ppermute | solution.py:229

commit v10 on v9

--- a/solution.py
+++ b/solution.py
@@ -70,14 +70,12 @@
     return pl.ds(pl.multiple_of(index * size, size), size)
 
 
-def slab_kernel(act_ref, mask_ref, grad_ref, out_ref, mine_ref, mask_held, sems):
+def slab_kernel(act_ref, mask_ref, grad_ref, out_ref, mask_held, sems):
     other = 1 - lax.axis_index("core")
     copies = [pltpu.make_async_copy(act_ref.at[:, at(other)], out_ref.at[pl.ds(0, TOKENS)], sems.at[0])]
     for k in range(4):
         rows = pl.ds(TOKENS + ROWS * k, ROWS)
         copies.append(pltpu.make_async_copy(grad_ref.at[:, at(2 * k + other)], out_ref.at[rows], sems.at[k + 1]))
-        rows = pl.ds(ROWS * k, ROWS)
-        copies.append(pltpu.make_async_copy(grad_ref.at[:, at(2 * k + 1 - other)], mine_ref.at[rows], sems.at[k + 6]))
     copies.insert(0, pltpu.make_async_copy(mask_ref, mask_held, sems.at[5]))
     for copy in copies:
         copy.start()
@@ -99,13 +97,17 @@
     return dot(low, low), dot(high, low), dot(high, high)
 
 
-def own_kernel(act_ref, mask_ref, out_ref, held, mask_held, sems):
-    columns = pltpu.make_async_copy(act_ref.at[:, at(lax.axis_index("core"))], held, sems.at[0])
-    mask = pltpu.make_async_copy(mask_ref, mask_held, sems.at[1])
-    columns.start()
-    mask.start()
-    columns.wait()
-    mask.wait()
+def own_kernel(act_ref, mask_ref, grad_ref, out_ref, mine_ref, held, mask_held, sems):
+    core = lax.axis_index("core")
+    copies = [pltpu.make_async_copy(act_ref.at[:, at(core)], held, sems.at[0])]
+    copies.append(pltpu.make_async_copy(mask_ref, mask_held, sems.at[1]))
+    for k in range(4):
+        rows = pl.ds(ROWS * k, ROWS)
+        copies.append(pltpu.make_async_copy(grad_ref.at[:, at(2 * k + core)], mine_ref.at[rows], sems.at[k + 2]))
+    for copy in copies:
+        copy.start()
+    for copy in copies:
+        copy.wait()
     for slot, block in enumerate(triangle(masked(held[...], mask_held[...]))):
         out_ref[slot] = block
 
@@ -203,20 +205,20 @@
     activations = pltpu.with_memory_space_constraint(activations, pltpu.HBM)
     gradient = pltpu.with_memory_space_constraint(gradient, pltpu.HBM)
     dma = pltpu.SemaphoreType.DMA
-    slab, mine = call(
+    (slab,) = call(
         slab_kernel,
-        [((SLAB, B), BF), ((4 * ROWS, B), BF)],
+        [((SLAB, B), BF)],
         (activations, mask, gradient),
         [HBM] * 3,
-        [pltpu.VMEM((1, TOKENS), jnp.int32), dma((10,))],
+        [pltpu.VMEM((1, TOKENS), jnp.int32), dma((6,))],
     )
     other = lax.ppermute(slab, "core", [(0, 1), (1, 0)])
-    (own,) = call(
+    own, mine = call(
         own_kernel,
-        [((3, H, H), F32)],
-        (activations, mask),
-        [HBM, HBM],
-        [pltpu.VMEM((TOKENS, B), BF), pltpu.VMEM((1, TOKENS), jnp.int32), dma((2,))],
+        [((3, H, H), F32), ((4 * ROWS, B), BF)],
+        (activations, mask, gradient),
+        [HBM] * 3,
+        [pltpu.VMEM((TOKENS, B), BF), pltpu.VMEM((1, TOKENS), jnp.int32), dma((6,))],
         flops=6 * TOKENS * H * H,
     )
     half = ((2, 2, ROWS, B), BF)

time: 70.5 us -> 70.5 us (level)
  no operation moved by 1% of the time
where the time goes in v10:
time: 70.5 us; the launch traced here: 69.9 us
  starting transfers between devices  27.3 us (39%)
  blocking collectives  25.8 us (37%)
  waiting for transfers between devices  8.52 us (12%)
  Pallas kernels  7.32 us (10%)
  local copies, waits for them, and re-layouts  0.74 us (1%)
    all_to_all x1, blocking collectives, local(): lax.all_to_all(product.reshape(8, ROWS, B), NAMES, 0, 0, axis_index_group...  16.3 us
    all_to_all x1, blocking collectives, local(): lax.all_to_all(packed.reshape(SHARDS, PACKED, LANES), NAMES, 0, 0, axis_i...  9.55 us
    ppermute x1, starting transfers between devices, local(): other = lax.ppermute(slab, 'core', [(0, 1), (1, 0)])  8.79 us
    pallas_call x7, Pallas kernels, call(): pl.pallas_call(kernel, out_shape=shapes, in_specs=specs or [VMEM] * len(o...  7.32 us
    all_to_all x1, starting transfers between devices, local(): parts = lax.all_to_all(copies, 'z', 0, 0)  5.96 us
    ppermute x1, starting transfers between devices, local(): come = lax.ppermute(send, NAMES, pairs(FIRST))  4.42 us
    ppermute x1, waiting for transfers between devices, local(): come = lax.ppermute(send, NAMES, pairs(FIRST))  4.25 us
    ppermute x1, starting transfers between devices, local(): come = lax.ppermute(send, NAMES, pairs(SECOND))  4.18 us
  transfers between devices with their start and end apart: 5, of which 5 were waited for; matrix products, arithmetic and copies ran while one was open for 0% of the time, Pallas kernels for 6%

profile of v10, /device:TPU:1, one launch (start us, length us, event | category | flops | bytes accessed | tf_op | source)
XLA Modules:
  0.0 69.9 jit_solution(1778099504970519798)
XLA Ops:
  0.0 1.1 %shard_map.37 = bf16[656,512]{1,0:T(8,128)(2,1)S(1)} custom-call(bf16[512,1024]{1,0:T(8,128)(2,1)} %act_ref.3, s32[1,512]{1,0:T(1,128)} %bitcast.9, bf16[32,4096]{1,0:T(8,128)(2,1)} %grad_ref.3), custom_call_target="tpu_custom_call" | custom-call | bytes 1984512 | tf_op jit(solution)/shard_map/pallas_call | solution.py:58
  1.1 8.8 %collective-permute-start = (bf16[656,512]{1,0:T(8,128)(2,1)S(1)}, bf16[656,512]{1,0:T(8,128)(2,1)S(1)}, u32[]{:S(2)}, u32[]{:S(2)}) collective-permute-start(bf16[656,512]{1,0:T(8,128)(2,1)S(1)} %shard_map.37), channel_id=1, source_target_pairs={{0,4},{4,0},{1,5},{5,1},{2,6},{6,2},{3,7},{7,3},{8,12},{12,8},{9,1... | collective-permute-start | bytes 2015240 | tf_op jit(solution)/shard_map/ppermute | solution.py:215
  9.9 1.6 %shard_map.38 = (f32[3,256,256]{2,1,0:T(8,128)S(1)}, bf16[128,512]{1,0:T(8,128)(2,1)S(1)}) custom-call(bf16[512,1024]{1,0:T(8,128)(2,1)} %act_ref.3, s32[1,512]{1,0:T(1,128)} %bitcast.10, bf16[32,4096]{1,0:T(8,128)(2,1)} %grad_ref.3), custom_call_target="tpu_custom_call" | custom-call | flops 201326592 | bytes 2230272 | tf_op jit(solution)/shard_map/pallas_call | solution.py:58
  11.6 0.1 collective-permute-done.slab_ref
  11.6 0.5 shard_map.39
  12.2 9.6 %all_to_all.20.parts_ref = bf16[8,144,128]{2,1,0:T(8,128)(2,1)S(1)} all-to-all(bf16[8,144,128]{2,1,0:T(8,128)(2,1)S(1)} %bitcast.7), channel_id=1, replica_groups={{48,56,32,40,16,24,0,8},{49,57,33,41,17,25,1,9},{50,58,34,42,18,26,2,10..., dimensions={0} | all-to-all | bytes 589824 | tf_op jit(solution)/shard_map/all_to_all | solution.py:226
  21.7 0.8 %shard_map.40 = (bf16[8,144,128]{2,1,0:T(8,128)(2,1)}, bf16[2,2,32,512]{3,2,1,0:T(8,128)(2,1)S(1)}, bf16[2,2,32,512]{3,2,1,0:T(8,128)(2,1)S(1)}) custom-call(bf16[8,144,128]{2,1,0:T(8,128)(2,1)S(1)} %all_to_all.20.parts_ref, bf16[656,512]{1,0:T(8,128)(2,1)S(1)} %collective-permute-done.slab_ref, bf16[128,512]{1,0:T(8,128)(2,1)S(1)} %get-tuple-element.16.mine_ref), custom_call_target="tpu_custom_call" | custom-call | bytes 1654784 | tf_op jit(solution)/shard_map/pallas_call | solution.py:58
  22.5 6.0 %all-to-all-start.1 = ((bf16[8,144,128]{2,1,0:T(8,128)(2,1)}), bf16[8,144,128]{2,1,0:T(8,128)(2,1)S(1)}, u32[]{:S(2)}, u32[]{:S(2)}) async-start(bf16[8,144,128]{2,1,0:T(8,128)(2,1)} %get-tuple-element.17), calls=%async_computation.1 | async-start | bytes 589824 | tf_op jit(solution)/shard_map/all_to_all | solution.py:229
  28.4 4.4 %collective-permute-start.1 = (bf16[2,2,32,512]{3,2,1,0:T(8,128)(2,1)S(1)}, bf16[2,2,32,512]{3,2,1,0:T(8,128)(2,1)S(1)}, u32[]{:S(2)}, u32[]{:S(2)}) collective-permute-start(bf16[2,2,32,512]{3,2,1,0:T(8,128)(2,1)S(1)} %get-tuple-element.19), channel_id=1, source_target_pairs={{34,1},{38,5},{35,0},{39,4},{0,35},{4,39},{1,34},{5,38},{42,9},{46... | collective-permute-start | bytes 393224 | tf_op jit(solution)/shard_map/ppermute | solution.py:228
  32.9 4.3 %collective-permute-done.1.come_ref = bf16[2,2,32,512]{3,2,1,0:T(8,128)(2,1)S(1)} collective-permute-done((bf16[2,2,32,512]{3,2,1,0:T(8,128)(2,1)S(1)}, bf16[2,2,32,512]{3,2,1,0:T(8,128)(2,1)S(1)}, u32[]{:S(2)}, u32[]{:S(2)}) %collective-permute-start.1) | collective-permute-done | bytes 131104 | tf_op jit(solution)/shard_map/ppermute | solution.py:228
  37.1 2.7 %all-to-all-done.1.parts_ref = bf16[8,144,128]{2,1,0:T(8,128)(2,1)S(1)} async-done(((bf16[8,144,128]{2,1,0:T(8,128)(2,1)}), bf16[8,144,128]{2,1,0:T(8,128)(2,1)S(1)}, u32[]{:S(2)}, u32[]{:S(2)}) %all-to-all-start.1) | async-done | bytes 294944 | tf_op jit(solution)/shard_map/all_to_all | solution.py:229
  39.8 0.8 %shard_map.41 = (bf16[8,144,128]{2,1,0:T(8,128)(2,1)}, bf16[2,2,32,512]{3,2,1,0:T(8,128)(2,1)S(1)}, bf16[2,2,32,512]{3,2,1,0:T(8,128)(2,1)S(1)}) custom-call(bf16[8,144,128]{2,1,0:T(8,128)(2,1)S(1)} %all-to-all-done.1.parts_ref, bf16[2,2,32,512]{3,2,1,0:T(8,128)(2,1)S(1)} %get-tuple-element.18.kept_ref, ...), custom_call_target="tpu_custom_call" | custom-call | bytes 1114112 | tf_op jit(solution)/shard_map/pallas_call | solution.py:58
  40.5 4.0 %all-to-all-start.2 = ((bf16[8,144,128]{2,1,0:T(8,128)(2,1)}), bf16[8,144,128]{2,1,0:T(8,128)(2,1)S(1)}, u32[]{:S(2)}, u32[]{:S(2)}) async-start(bf16[8,144,128]{2,1,0:T(8,128)(2,1)} %get-tuple-element.20), calls=%async_computation.2 | async-start | bytes 589824 | tf_op jit(solution)/shard_map/all_to_all | solution.py:232
  44.5 4.2 %collective-permute-start.2 = (bf16[2,2,32,512]{3,2,1,0:T(8,128)(2,1)S(1)}, bf16[2,2,32,512]{3,2,1,0:T(8,128)(2,1)S(1)}, u32[]{:S(2)}, u32[]{:S(2)}) collective-permute-start(bf16[2,2,32,512]{3,2,1,0:T(8,128)(2,1)S(1)} %get-tuple-element.24), channel_id=1, source_target_pairs={{34,35},{38,39},{35,34},{39,38},{0,1},{4,5},{1,0},{5,4},{42,43},{4... | collective-permute-start | bytes 393224 | tf_op jit(solution)/shard_map/ppermute | solution.py:231
  48.7 0.9 %all-to-all-done.2.gram_ref = bf16[8,144,128]{2,1,0:T(8,128)(2,1)S(1)} async-done(((bf16[8,144,128]{2,1,0:T(8,128)(2,1)}), bf16[8,144,128]{2,1,0:T(8,128)(2,1)S(1)}, u32[]{:S(2)}, u32[]{:S(2)}) %all-to-all-start.2) | async-done | bytes 294944 | tf_op jit(solution)/shard_map/all_to_all | solution.py:232
  49.7 2.3 %shard_map.42 = (bf16[512,512]{1,0:T(8,128)(2,1)S(1)}, bf16[128,512]{1,0:T(8,128)(2,1)S(1)}) custom-call(bf16[8,144,128]{2,1,0:T(8,128)(2,1)S(1)} %all-to-all-done.2.gram_ref, bf16[2,2,32,512]{3,2,1,0:T(8,128)(2,1)S(1)} %get-tuple-element.21.kept_ref), custom_call_target="tpu_custom_call" | custom-call | flops 1342177280 | bytes 1081344 | tf_op jit(solution)/shard_map/pallas_call | solution.py:58
  52.0 0.6 collective-permute-done.2.come_ref
  52.6 0.2 shard_map.43
  52.8 16.3 %all_to_all.21 = bf16[8,32,512]{2,1,0:T(8,128)(2,1)S(1)} all-to-all(bf16[8,32,512]{2,1,0:T(8,128)(2,1)S(1)} %bitcast.8), channel_id=1, replica_groups={{34,38,35,39,0,4,1,5},{42,46,43,47,8,12,9,13},{50,54,51,55,16,20,17,21}..., dimensions={0} | all-to-all | bytes 524288 | tf_op jit(solution)/shard_map/all_to_all | solution.py:239
  69.1 0.7 %copy.5 = bf16[8,4,8,512]{3,2,0,1:T(8,128)(2,1)} copy(bf16[8,4,8,512]{3,2,1,0:T(8,128)(2,1)S(1)} %maximum_bitcast_fusion) | data formatting | bytes 524288 | tf_op jit(solution)/shard_map/reshape | solution.py:241
  (2 shorter events, 0.0 us)
Async XLA Ops:
  1.1 10.5 %collective-permute-start = (bf16[656,512]{1,0:T(8,128)(2,1)S(1)}, bf16[656,512]{1,0:T(8,128)(2,1)S(1)}, u32[]{:S(2)}, u32[]{:S(2)}) collective-permute-start(bf16[656,512]{1,0:T(8,128)(2,1)S(1)} %shard_map.37), channel_id=1, source_target_pairs={{0,4},{4,0},{1,5},{5,1},{2,6},{6,2},{3,7},{7,3},{8,12},{12,8},{9,1... | collective-permute-start | bytes 2015240 | tf_op jit(solution)/shard_map/ppermute | solution.py:215
  22.5 17.3 %all-to-all-start.1 = ((bf16[8,144,128]{2,1,0:T(8,128)(2,1)}), bf16[8,144,128]{2,1,0:T(8,128)(2,1)S(1)}, u32[]{:S(2)}, u32[]{:S(2)}) async-start(bf16[8,144,128]{2,1,0:T(8,128)(2,1)} %get-tuple-element.17), calls=%async_computation.1 | async-start | bytes 589824 | tf_op jit(solution)/shard_map/all_to_all | solution.py:229
  28.4 8.7 %collective-permute-start.1 = (bf16[2,2,32,512]{3,2,1,0:T(8,128)(2,1)S(1)}, bf16[2,2,32,512]{3,2,1,0:T(8,128)(2,1)S(1)}, u32[]{:S(2)}, u32[]{:S(2)}) collective-permute-start(bf16[2,2,32,512]{3,2,1,0:T(8,128)(2,1)S(1)} %get-tuple-element.19), channel_id=1, source_target_pairs={{34,1},{38,5},{35,0},{39,4},{0,35},{4,39},{1,34},{5,38},{42,9},{46... | collective-permute-start | bytes 393224 | tf_op jit(solution)/shard_map/ppermute | solution.py:228
  40.5 9.1 %all-to-all-start.2 = ((bf16[8,144,128]{2,1,0:T(8,128)(2,1)}), bf16[8,144,128]{2,1,0:T(8,128)(2,1)S(1)}, u32[]{:S(2)}, u32[]{:S(2)}) async-start(bf16[8,144,128]{2,1,0:T(8,128)(2,1)} %get-tuple-element.20), calls=%async_computation.2 | async-start | bytes 589824 | tf_op jit(solution)/shard_map/all_to_all | solution.py:232
  44.5 8.0 %collective-permute-start.2 = (bf16[2,2,32,512]{3,2,1,0:T(8,128)(2,1)S(1)}, bf16[2,2,32,512]{3,2,1,0:T(8,128)(2,1)S(1)}, u32[]{:S(2)}, u32[]{:S(2)}) collective-permute-start(bf16[2,2,32,512]{3,2,1,0:T(8,128)(2,1)S(1)} %get-tuple-element.24), channel_id=1, source_target_pairs={{34,35},{38,39},{35,34},{39,38},{0,1},{4,5},{1,0},{5,4},{42,43},{4... | collective-permute-start | bytes 393224 | tf_op jit(solution)/shard_map/ppermute | solution.py:231

commit v11 on v10

--- a/solution.py
+++ b/solution.py
@@ -76,10 +76,10 @@
     for k in range(4):
         rows = pl.ds(TOKENS + ROWS * k, ROWS)
         copies.append(pltpu.make_async_copy(grad_ref.at[:, at(2 * k + other)], out_ref.at[rows], sems.at[k + 1]))
-    copies.insert(0, pltpu.make_async_copy(mask_ref, mask_held, sems.at[5]))
+    copies.insert(1, pltpu.make_async_copy(mask_ref, mask_held, sems.at[5]))
     for copy in copies:
         copy.start()
-    copies.pop(0).wait()
+    copies.pop(1).wait()
     mask = mask_held[...].astype(F32).astype(BF)
     out_ref[pl.ds(TOKENS + 4 * ROWS, MASK_ROWS), :] = jnp.broadcast_to(mask, (MASK_ROWS, TOKENS))
     for copy in copies:

time: 70.5 us -> 70.4 us (level)
  no operation moved by 1% of the time
where the time goes in v11:
time: 70.4 us; the launch traced here: 69.8 us
  starting transfers between devices  27.3 us (39%)
  blocking collectives  25.8 us (37%)
  waiting for transfers between devices  8.52 us (12%)
  Pallas kernels  7.29 us (10%)
  local copies, waits for them, and re-layouts  0.74 us (1%)
    all_to_all x1, blocking collectives, local(): lax.all_to_all(product.reshape(8, ROWS, B), NAMES, 0, 0, axis_index_group...  16.3 us
    all_to_all x1, blocking collectives, local(): lax.all_to_all(packed.reshape(SHARDS, PACKED, LANES), NAMES, 0, 0, axis_i...  9.55 us
    ppermute x1, starting transfers between devices, local(): other = lax.ppermute(slab, 'core', [(0, 1), (1, 0)])  8.79 us
    pallas_call x7, Pallas kernels, call(): pl.pallas_call(kernel, out_shape=shapes, in_specs=specs or [VMEM] * len(o...  7.29 us
    all_to_all x1, starting transfers between devices, local(): parts = lax.all_to_all(copies, 'z', 0, 0)  5.96 us
    ppermute x1, starting transfers between devices, local(): come = lax.ppermute(send, NAMES, pairs(FIRST))  4.42 us
    ppermute x1, waiting for transfers between devices, local(): come = lax.ppermute(send, NAMES, pairs(FIRST))  4.25 us
    ppermute x1, starting transfers between devices, local(): come = lax.ppermute(send, NAMES, pairs(SECOND))  4.18 us
  transfers between devices with their start and end apart: 5, of which 5 were waited for; matrix products, arithmetic and copies ran while one was open for 0% of the time, Pallas kernels for 6%

profile of v11, /device:TPU:1, one launch (start us, length us, event | category | flops | bytes accessed | tf_op | source)
XLA Modules:
  0.0 69.8 jit_solution(2995681555106780075)
XLA Ops:
  0.0 1.1 %shard_map.37 = bf16[656,512]{1,0:T(8,128)(2,1)S(1)} custom-call(bf16[512,1024]{1,0:T(8,128)(2,1)} %act_ref.3, s32[1,512]{1,0:T(1,128)} %bitcast.9, bf16[32,4096]{1,0:T(8,128)(2,1)} %grad_ref.3), custom_call_target="tpu_custom_call" | custom-call | bytes 1984512 | tf_op jit(solution)/shard_map/pallas_call | solution.py:58
  1.1 8.8 %collective-permute-start = (bf16[656,512]{1,0:T(8,128)(2,1)S(1)}, bf16[656,512]{1,0:T(8,128)(2,1)S(1)}, u32[]{:S(2)}, u32[]{:S(2)}) collective-permute-start(bf16[656,512]{1,0:T(8,128)(2,1)S(1)} %shard_map.37), channel_id=1, source_target_pairs={{0,4},{4,0},{1,5},{5,1},{2,6},{6,2},{3,7},{7,3},{8,12},{12,8},{9,1... | collective-permute-start | bytes 2015240 | tf_op jit(solution)/shard_map/ppermute | solution.py:215
  9.9 1.6 %shard_map.38 = (f32[3,256,256]{2,1,0:T(8,128)S(1)}, bf16[128,512]{1,0:T(8,128)(2,1)S(1)}) custom-call(bf16[512,1024]{1,0:T(8,128)(2,1)} %act_ref.3, s32[1,512]{1,0:T(1,128)} %bitcast.10, bf16[32,4096]{1,0:T(8,128)(2,1)} %grad_ref.3), custom_call_target="tpu_custom_call" | custom-call | flops 201326592 | bytes 2230272 | tf_op jit(solution)/shard_map/pallas_call | solution.py:58
  11.5 0.1 collective-permute-done.slab_ref
  11.6 0.5 shard_map.39
  12.1 9.6 %all_to_all.20.parts_ref = bf16[8,144,128]{2,1,0:T(8,128)(2,1)S(1)} all-to-all(bf16[8,144,128]{2,1,0:T(8,128)(2,1)S(1)} %bitcast.7), channel_id=1, replica_groups={{48,56,32,40,16,24,0,8},{49,57,33,41,17,25,1,9},{50,58,34,42,18,26,2,10..., dimensions={0} | all-to-all | bytes 589824 | tf_op jit(solution)/shard_map/all_to_all | solution.py:226
  21.7 0.8 %shard_map.40 = (bf16[8,144,128]{2,1,0:T(8,128)(2,1)}, bf16[2,2,32,512]{3,2,1,0:T(8,128)(2,1)S(1)}, bf16[2,2,32,512]{3,2,1,0:T(8,128)(2,1)S(1)}) custom-call(bf16[8,144,128]{2,1,0:T(8,128)(2,1)S(1)} %all_to_all.20.parts_ref, bf16[656,512]{1,0:T(8,128)(2,1)S(1)} %collective-permute-done.slab_ref, bf16[128,512]{1,0:T(8,128)(2,1)S(1)} %get-tuple-element.16.mine_ref), custom_call_target="tpu_custom_call" | custom-call | bytes 1654784 | tf_op jit(solution)/shard_map/pallas_call | solution.py:58
  22.5 6.0 %all-to-all-start.1 = ((bf16[8,144,128]{2,1,0:T(8,128)(2,1)}), bf16[8,144,128]{2,1,0:T(8,128)(2,1)S(1)}, u32[]{:S(2)}, u32[]{:S(2)}) async-start(bf16[8,144,128]{2,1,0:T(8,128)(2,1)} %get-tuple-element.17), calls=%async_computation.1 | async-start | bytes 589824 | tf_op jit(solution)/shard_map/all_to_all | solution.py:229
  28.4 4.4 %collective-permute-start.1 = (bf16[2,2,32,512]{3,2,1,0:T(8,128)(2,1)S(1)}, bf16[2,2,32,512]{3,2,1,0:T(8,128)(2,1)S(1)}, u32[]{:S(2)}, u32[]{:S(2)}) collective-permute-start(bf16[2,2,32,512]{3,2,1,0:T(8,128)(2,1)S(1)} %get-tuple-element.19), channel_id=1, source_target_pairs={{34,1},{38,5},{35,0},{39,4},{0,35},{4,39},{1,34},{5,38},{42,9},{46... | collective-permute-start | bytes 393224 | tf_op jit(solution)/shard_map/ppermute | solution.py:228
  32.9 4.3 %collective-permute-done.1.come_ref = bf16[2,2,32,512]{3,2,1,0:T(8,128)(2,1)S(1)} collective-permute-done((bf16[2,2,32,512]{3,2,1,0:T(8,128)(2,1)S(1)}, bf16[2,2,32,512]{3,2,1,0:T(8,128)(2,1)S(1)}, u32[]{:S(2)}, u32[]{:S(2)}) %collective-permute-start.1) | collective-permute-done | bytes 131104 | tf_op jit(solution)/shard_map/ppermute | solution.py:228
  37.1 2.7 %all-to-all-done.1.parts_ref = bf16[8,144,128]{2,1,0:T(8,128)(2,1)S(1)} async-done(((bf16[8,144,128]{2,1,0:T(8,128)(2,1)}), bf16[8,144,128]{2,1,0:T(8,128)(2,1)S(1)}, u32[]{:S(2)}, u32[]{:S(2)}) %all-to-all-start.1) | async-done | bytes 294944 | tf_op jit(solution)/shard_map/all_to_all | solution.py:229
  39.8 0.8 %shard_map.41 = (bf16[8,144,128]{2,1,0:T(8,128)(2,1)}, bf16[2,2,32,512]{3,2,1,0:T(8,128)(2,1)S(1)}, bf16[2,2,32,512]{3,2,1,0:T(8,128)(2,1)S(1)}) custom-call(bf16[8,144,128]{2,1,0:T(8,128)(2,1)S(1)} %all-to-all-done.1.parts_ref, bf16[2,2,32,512]{3,2,1,0:T(8,128)(2,1)S(1)} %get-tuple-element.18.kept_ref, ...), custom_call_target="tpu_custom_call" | custom-call | bytes 1114112 | tf_op jit(solution)/shard_map/pallas_call | solution.py:58
  40.5 4.0 %all-to-all-start.2 = ((bf16[8,144,128]{2,1,0:T(8,128)(2,1)}), bf16[8,144,128]{2,1,0:T(8,128)(2,1)S(1)}, u32[]{:S(2)}, u32[]{:S(2)}) async-start(bf16[8,144,128]{2,1,0:T(8,128)(2,1)} %get-tuple-element.20), calls=%async_computation.2 | async-start | bytes 589824 | tf_op jit(solution)/shard_map/all_to_all | solution.py:232
  44.5 4.2 %collective-permute-start.2 = (bf16[2,2,32,512]{3,2,1,0:T(8,128)(2,1)S(1)}, bf16[2,2,32,512]{3,2,1,0:T(8,128)(2,1)S(1)}, u32[]{:S(2)}, u32[]{:S(2)}) collective-permute-start(bf16[2,2,32,512]{3,2,1,0:T(8,128)(2,1)S(1)} %get-tuple-element.24), channel_id=1, source_target_pairs={{34,35},{38,39},{35,34},{39,38},{0,1},{4,5},{1,0},{5,4},{42,43},{4... | collective-permute-start | bytes 393224 | tf_op jit(solution)/shard_map/ppermute | solution.py:231
  48.7 0.9 %all-to-all-done.2.gram_ref = bf16[8,144,128]{2,1,0:T(8,128)(2,1)S(1)} async-done(((bf16[8,144,128]{2,1,0:T(8,128)(2,1)}), bf16[8,144,128]{2,1,0:T(8,128)(2,1)S(1)}, u32[]{:S(2)}, u32[]{:S(2)}) %all-to-all-start.2) | async-done | bytes 294944 | tf_op jit(solution)/shard_map/all_to_all | solution.py:232
  49.7 2.3 %shard_map.42 = (bf16[512,512]{1,0:T(8,128)(2,1)S(1)}, bf16[128,512]{1,0:T(8,128)(2,1)S(1)}) custom-call(bf16[8,144,128]{2,1,0:T(8,128)(2,1)S(1)} %all-to-all-done.2.gram_ref, bf16[2,2,32,512]{3,2,1,0:T(8,128)(2,1)S(1)} %get-tuple-element.21.kept_ref), custom_call_target="tpu_custom_call" | custom-call | flops 1342177280 | bytes 1081344 | tf_op jit(solution)/shard_map/pallas_call | solution.py:58
  52.0 0.6 collective-permute-done.2.come_ref
  52.5 0.2 shard_map.43
  52.8 16.3 %all_to_all.21 = bf16[8,32,512]{2,1,0:T(8,128)(2,1)S(1)} all-to-all(bf16[8,32,512]{2,1,0:T(8,128)(2,1)S(1)} %bitcast.8), channel_id=1, replica_groups={{34,38,35,39,0,4,1,5},{42,46,43,47,8,12,9,13},{50,54,51,55,16,20,17,21}..., dimensions={0} | all-to-all | bytes 524288 | tf_op jit(solution)/shard_map/all_to_all | solution.py:239
  69.1 0.7 %copy.5 = bf16[8,4,8,512]{3,2,0,1:T(8,128)(2,1)} copy(bf16[8,4,8,512]{3,2,1,0:T(8,128)(2,1)S(1)} %maximum_bitcast_fusion) | data formatting | bytes 524288 | tf_op jit(solution)/shard_map/reshape | solution.py:241
  (2 shorter events, 0.0 us)
Async XLA Ops:
  1.1 10.5 %collective-permute-start = (bf16[656,512]{1,0:T(8,128)(2,1)S(1)}, bf16[656,512]{1,0:T(8,128)(2,1)S(1)}, u32[]{:S(2)}, u32[]{:S(2)}) collective-permute-start(bf16[656,512]{1,0:T(8,128)(2,1)S(1)} %shard_map.37), channel_id=1, source_target_pairs={{0,4},{4,0},{1,5},{5,1},{2,6},{6,2},{3,7},{7,3},{8,12},{12,8},{9,1... | collective-permute-start | bytes 2015240 | tf_op jit(solution)/shard_map/ppermute | solution.py:215
  22.5 17.3 %all-to-all-start.1 = ((bf16[8,144,128]{2,1,0:T(8,128)(2,1)}), bf16[8,144,128]{2,1,0:T(8,128)(2,1)S(1)}, u32[]{:S(2)}, u32[]{:S(2)}) async-start(bf16[8,144,128]{2,1,0:T(8,128)(2,1)} %get-tuple-element.17), calls=%async_computation.1 | async-start | bytes 589824 | tf_op jit(solution)/shard_map/all_to_all | solution.py:229
  28.4 8.7 %collective-permute-start.1 = (bf16[2,2,32,512]{3,2,1,0:T(8,128)(2,1)S(1)}, bf16[2,2,32,512]{3,2,1,0:T(8,128)(2,1)S(1)}, u32[]{:S(2)}, u32[]{:S(2)}) collective-permute-start(bf16[2,2,32,512]{3,2,1,0:T(8,128)(2,1)S(1)} %get-tuple-element.19), channel_id=1, source_target_pairs={{34,1},{38,5},{35,0},{39,4},{0,35},{4,39},{1,34},{5,38},{42,9},{46... | collective-permute-start | bytes 393224 | tf_op jit(solution)/shard_map/ppermute | solution.py:228
  40.5 9.1 %all-to-all-start.2 = ((bf16[8,144,128]{2,1,0:T(8,128)(2,1)}), bf16[8,144,128]{2,1,0:T(8,128)(2,1)S(1)}, u32[]{:S(2)}, u32[]{:S(2)}) async-start(bf16[8,144,128]{2,1,0:T(8,128)(2,1)} %get-tuple-element.20), calls=%async_computation.2 | async-start | bytes 589824 | tf_op jit(solution)/shard_map/all_to_all | solution.py:232
  44.5 8.0 %collective-permute-start.2 = (bf16[2,2,32,512]{3,2,1,0:T(8,128)(2,1)S(1)}, bf16[2,2,32,512]{3,2,1,0:T(8,128)(2,1)S(1)}, u32[]{:S(2)}, u32[]{:S(2)}) collective-permute-start(bf16[2,2,32,512]{3,2,1,0:T(8,128)(2,1)S(1)} %get-tuple-element.24), channel_id=1, source_target_pairs={{34,35},{38,39},{35,34},{39,38},{0,1},{4,5},{1,0},{5,4},{42,43},{4... | collective-permute-start | bytes 393224 | tf_op jit(solution)/shard_map/ppermute | solution.py:231
